TPU v7x, 32 devices: a whole 2x2x4 slice. The times are simulated.
32 devices in a mesh: cluster: 4 (over z), seq: 8 (over y, x, core).
Axes of the slice: x: 2, y: 2, z: 4, core: 2. Of those that a mesh axis runs over, the one named last changes fastest.
Arguments:
- nodes: bfloat16 [16384, 1024], P(('cluster', 'seq')), may hold values from -48 to 48
- w_qkv: bfloat16 [1024, 3072], replicated, may hold values from -0.1875 to 0.1875
- w_out: bfloat16 [1024, 1024], replicated, may hold values from -1.5 to 1.5
- kv_ids: int32 [128, 16], P('cluster'), may hold values from 0 to 127, as said below
- counts: int32 [128], P('cluster'), may hold values from 13 to 16, as said below
Outputs:
- attended_out: bfloat16 [16384, 1024], P(('cluster', 'seq'))
Inputs may be any that keep to these rules, and one draw needn't show every extreme that they name: `kv_ids`: entries name blocks; the cluster of block b is b // 32. For query block q, entry 0 is q itself, entries 0 to 11 are distinct blocks of q's cluster, and the last 4 entries are distinct blocks of other clusters. Over all entries of the query blocks of one cluster, at most 8 distinct blocks of any one other cluster are named, and exactly 8 for some pair of clusters. The first counts[q] entries of query block q's list are valid, the others are padding.
All inputs are finite; a program needn't handle non-finite values.
Results may differ from a plain program's by a relative error of at most 0.012.
Values may be sent and summed in bfloat16 or wider, within the bound.
No kernel may reach another device: no remote copies, remote signals or barrier semaphores. Data moves between devices by JAX's collectives and lax.ppermute only.
A program may use at most 128 MiB of HBM per device.

v0:
```python
import jax
import jax.numpy as jnp
from jax import lax
from jax.sharding import PartitionSpec as P

D = 1024
HEADS = 16
HD = 64
BLK = 128
KVB = 16
REMOTE = 4


def on_device(nodes, w_qkv, w_out, kv_ids, counts):
    seq_size = lax.axis_size("seq")
    cluster_size = lax.axis_size("cluster")
    node_rows = nodes.shape[0]
    heads_dev = HEADS // seq_size
    w_grouped = w_qkv.reshape(D, seq_size, heads_dev, 3, HD)
    w_query = w_grouped[:, :, :, 0].reshape(D, seq_size, heads_dev * HD)
    w_keyval = w_grouped[:, :, :, 1:].reshape(D, seq_size, heads_dev * 2 * HD)
    query_proj = jnp.einsum(
        "rd,dsf->srf", nodes, w_query, preferred_element_type=jnp.float32
    ).astype(jnp.bfloat16)
    keyval_proj = jnp.einsum(
        "rd,dsf->srf", nodes, w_keyval, preferred_element_type=jnp.float32
    ).astype(jnp.bfloat16)
    query_recv, keyval_recv = (
        lax.all_to_all(query_proj, "seq", split_axis=0, concat_axis=0, tiled=True),
        lax.all_to_all(keyval_proj, "seq", split_axis=0, concat_axis=0, tiled=True),
    )
    cluster_rows = seq_size * node_rows
    block_count = cluster_rows // BLK
    queries = query_recv.reshape(block_count, BLK, heads_dev, HD)
    keyval_blocks = keyval_recv.reshape(block_count, BLK, heads_dev, 2, HD)
    key_table = jnp.transpose(keyval_blocks[:, :, :, 0], (0, 2, 3, 1))
    value_table = jnp.transpose(keyval_blocks[:, :, :, 1], (0, 2, 1, 3))
    cluster = lax.axis_index("cluster")
    local_ids = kv_ids[:, : KVB - REMOTE] - cluster * block_count
    remote_ids = kv_ids[:, KVB - REMOTE :]
    slot_ids = jnp.arange(KVB, dtype=jnp.int32)
    is_valid = slot_ids[None, :] < counts[:, None]
    block_total = cluster_size * block_count
    capacity = block_count // 4
    flat_ids = remote_ids.reshape(-1)
    flat_valid = is_valid[:, KVB - REMOTE :].reshape(-1)
    every_id = jnp.arange(block_total, dtype=jnp.int32)
    present = jnp.any((flat_ids[:, None] == every_id[None, :]) & flat_valid[:, None], axis=0)
    present = present.astype(jnp.int32).reshape(cluster_size, block_count)
    block_rank = jnp.cumsum(present, axis=1) - 1
    chosen = (block_rank[:, None, :] == jnp.arange(capacity, dtype=jnp.int32)[None, :, None]) & (
        present[:, None, :] > 0
    )
    wanted = jnp.sum(
        jnp.where(chosen, jnp.arange(block_count, dtype=jnp.int32)[None, None, :], 0), axis=2
    )
    asked_ids = lax.all_to_all(wanted, "cluster", split_axis=0, concat_axis=0, tiled=True).reshape(
        -1
    )
    out_keys = key_table[asked_ids].reshape((cluster_size, capacity) + key_table.shape[1:])
    out_values = value_table[asked_ids].reshape((cluster_size, capacity) + value_table.shape[1:])
    back_keys, back_values = (
        lax.all_to_all(out_keys, "cluster", split_axis=0, concat_axis=0, tiled=True),
        lax.all_to_all(out_values, "cluster", split_axis=0, concat_axis=0, tiled=True),
    )
    far_keys = back_keys.reshape((cluster_size * capacity,) + key_table.shape[1:])
    far_values = back_values.reshape((cluster_size * capacity,) + value_table.shape[1:])
    rank_flat = block_rank.reshape(-1)
    looked = jnp.sum(
        jnp.where(remote_ids[:, :, None] == every_id[None, None, :], rank_flat[None, None, :], 0),
        axis=2,
    )
    peer_id = remote_ids // block_count
    remote_pos = peer_id * capacity + jnp.maximum(looked, 0)
    groups = block_count // 4
    scale = HD ** (-0.5)

    def attend(packed):
        query_blk, near_ids, far_ids, valid_blk = packed
        near_k = key_table[near_ids]
        far_k = far_keys[far_ids]
        near_v = value_table[near_ids]
        far_v = far_values[far_ids]
        near_scores = (
            jnp.einsum("qahe,qjhek->qhajk", query_blk, near_k, preferred_element_type=jnp.float32)
            * scale
        )
        far_scores = (
            jnp.einsum("qahe,qjhek->qhajk", query_blk, far_k, preferred_element_type=jnp.float32)
            * scale
        )
        near_scores = jnp.where(valid_blk[:, None, None, : KVB - REMOTE, None], near_scores, -1e30)
        far_scores = jnp.where(valid_blk[:, None, None, KVB - REMOTE :, None], far_scores, -1e30)
        row_top = jnp.maximum(
            jnp.max(near_scores, axis=(3, 4), keepdims=True),
            jnp.max(far_scores, axis=(3, 4), keepdims=True),
        )
        near_exp = jnp.exp(near_scores - row_top)
        far_exp = jnp.exp(far_scores - row_top)
        row_total = jnp.sum(near_exp, axis=(3, 4), keepdims=True) + jnp.sum(
            far_exp, axis=(3, 4), keepdims=True
        )
        near_weight = (near_exp / row_total).astype(jnp.bfloat16)
        far_weight = (far_exp / row_total).astype(jnp.bfloat16)
        summed = jnp.einsum(
            "qhajk,qjhke->qahe", near_weight, near_v, preferred_element_type=jnp.float32
        )
        summed = summed + jnp.einsum(
            "qhajk,qjhke->qahe", far_weight, far_v, preferred_element_type=jnp.float32
        )
        return summed.astype(jnp.bfloat16)

    attended = lax.map(
        attend,
        (
            queries.reshape(groups, 4, BLK, heads_dev, HD),
            local_ids.reshape(groups, 4, KVB - REMOTE),
            remote_pos.reshape(groups, 4, REMOTE),
            is_valid.reshape(groups, 4, KVB),
        ),
    )
    attended = attended.reshape(seq_size, node_rows, heads_dev * HD)
    returned = lax.all_to_all(attended, "seq", split_axis=0, concat_axis=0, tiled=True)
    w_split = w_out.reshape(seq_size, heads_dev * HD, D)
    return jnp.einsum("srf,sfd->rd", returned, w_split, preferred_element_type=jnp.float32).astype(
        jnp.bfloat16
    )


def solution(mesh):
    placed = (P(("cluster", "seq"), None), P(), P(), P("cluster", None), P("cluster"))
    return jax.shard_map(
        on_device,
        mesh=mesh,
        in_specs=placed,
        out_specs=P(("cluster", "seq"), None),
        check_vma=False,
    )
```

profile of v0, /device:TPU:0, one launch (start us, length us, event | category | flops | bytes accessed | tf_op | source)
XLA Modules:
  0.0 462.0 jit_solution(15432283709272678105)
XLA Ops:
  3.1 6.3 %all-to-all-start.2 = ((s32[4,1,8]{2,1,0:T(1,128)}), s32[4,1,8]{2,1,0:T(1,128)S(1)}, u32[]{:S(2)}, u32[]{:S(2)}) async-start(s32[4,1,8]{2,1,0:T(1,128)} %bitcast.31), calls=%async_computation.2 | async-start | bytes 4096 | tf_op jit(solution)/shard_map/all_to_all | solution.py:57
  9.4 8.7 %copy.87 = bf16[1024,3072]{0,1:T(8,128)(2,1)} copy(bf16[1024,3072]{1,0:T(8,128)(2,1)} %param.8) | data formatting | bytes 12582912 | tf_op args[1]
  20.8 3.8 convert_bitcast_fusion
  24.6 4.4 all-to-all-start
  33.2 22.5 %all-to-all-done = bf16[8,512,256]{1,2,0:T(8,128)(2,1)} async-done(((bf16[8,512,256]{1,2,0:T(8,128)(2,1)}), bf16[8,512,256]{1,2,0:T(8,128)(2,1)}, u32[]{:S(2)}, u32[]{:S(2)}) %all-to-all-start) | async-done | bytes 2097184 | tf_op jit(solution)/shard_map/all_to_all | solution.py:30
  55.6 4.2 all-to-all-start.1
  61.2 4.1 copy.88
  65.3 4.4 reshape.175
  69.6 3.4 fusion.43
  75.3 5.1 %all-to-all-start.4 = ((bf16[4,8,2,128,64]{3,4,2,1,0:T(8,128)(2,1)}), bf16[4,8,2,128,64]{3,4,2,1,0:T(8,128)(2,1)}, u32[]{:S(2)}, u32[]{:S(2)}) async-start(bf16[4,8,2,128,64]{3,4,2,1,0:T(8,128)(2,1)} %bitcast.36), calls=%async_computation.4 | async-start | bytes 2097152 | tf_op jit(solution)/shard_map/all_to_all | solution.py:64
  83.7 22.8 %all-to-all-done.4 = bf16[4,8,2,128,64]{3,4,2,1,0:T(8,128)(2,1)} async-done(((bf16[4,8,2,128,64]{3,4,2,1,0:T(8,128)(2,1)}), bf16[4,8,2,128,64]{3,4,2,1,0:T(8,128)(2,1)}, u32[]{:S(2)}, u32[]{:S(2)}) %all-to-all-start.4) | async-done | bytes 1048608 | tf_op jit(solution)/shard_map/all_to_all | solution.py:64
  106.5 4.4 all-to-all-start.3
  119.5 16.6 %all-to-all-done.3 = bf16[4,8,2,64,128]{4,3,2,1,0:T(8,128)(2,1)} async-done(((bf16[4,8,2,64,128]{4,3,2,1,0:T(8,128)(2,1)}), bf16[4,8,2,64,128]{4,3,2,1,0:T(8,128)(2,1)}, u32[]{:S(2)}, u32[]{:S(2)}) %all-to-all-start.3) | async-done | bytes 1048608 | tf_op jit(solution)/shard_map/all_to_all | solution.py:63
  136.1 294.7 %while.10 = (s32[]{:T(128)}, bf16[8,4,128,2,64]{2,4,3,1,0:T(8,128)(2,1)}, s32[8,4,12]{2,1,0:T(4,128)S(1)}, bf16[32,2,128,64]{3,2,1,0:T(8,128)(2,1)}, pred[8,4,16...) while((s32[]{:T(128)}, ...), condition=%wide.region_9.10_spmd, body=%wide.region_4.9_spmd.sunk | while | flops 562168000 | bytes 48966392 | solution.py:113
  139.1 5.8 %fusion.58 = (f32[4,2,128]{2,1,0:T(2,128)S(1)}, f32[4,2,128,12,128]{2,4,3,1,0:T(8,128)}) fusion(pred[4,12]{1,0:T(4,128)(4,1)S(1)} %bitcast.132, bf16[4,12,2,64,128]{4,3,2,1,0:T(8,128)(2,1)} %bitcast.119, bf16[1,4,128,2,64]{2,1,4,3,0:T(4,128)(2,1)S(1)} %constant_dynamic-slice_fusion.2), kind=kOutput, calls=%fused_computation.9.clone.1 | convolution fusion | flops 206044160 | bytes 7999536 | tf_op jit(solution)/shard_map/while/body/eval_jaxpr/qahe,qjhek->qhajk/dot_general | solution.py:85
  151.2 4.2 fusion.59
  155.5 3.3 gather_fusion
  158.8 3.4 convolution_bitcast_fusion.2
  162.2 4.3 gather_fusion.3
  166.6 6.4 %fusion.61 = bf16[8,4,128,2,64]{2,4,3,1,0:T(8,128)(2,1)} fusion(bf16[8,4,128,2,64]{2,4,3,1,0:T(8,128)(2,1)} %get-tuple-element.216, s32[]{:T(128)} %get-tuple-element.215, f32[4,2,64,128]{3,2,1,0:T(8,128)} %convolution_bitcast_fusion.2, f32[4,2,128,12,128]{2,4,3,1,0:T(8,128)} %get-tuple-element.201, f32[4,2,128]{2,1,0:T(2,128)S(1)} %add.92, ...), kind=kOutput, calls=%fused_computation.26.clone.1 | convolution fusion | flops 209321984 | bytes 9839152 | tf_op jit(solution)/shard_map/while/body/eval_jaxpr/qhajk,qjhke->qahe/dot_general | solution.py:105
  175.9 5.8 %fusion.58 = (f32[4,2,128]{2,1,0:T(2,128)S(1)}, f32[4,2,128,12,128]{2,4,3,1,0:T(8,128)}) fusion(pred[4,12]{1,0:T(4,128)(4,1)S(1)} %bitcast.132, bf16[4,12,2,64,128]{4,3,2,1,0:T(8,128)(2,1)} %bitcast.119, bf16[1,4,128,2,64]{2,1,4,3,0:T(4,128)(2,1)S(1)} %constant_dynamic-slice_fusion.2), kind=kOutput, calls=%fused_computation.9.clone.1 | convolution fusion | flops 206044160 | bytes 7999536 | tf_op jit(solution)/shard_map/while/body/eval_jaxpr/qahe,qjhek->qhajk/dot_general | solution.py:85
  188.1 4.2 fusion.59
  192.3 3.3 gather_fusion
  195.7 3.4 convolution_bitcast_fusion.2
  199.1 4.3 gather_fusion.3
  203.4 6.4 %fusion.61 = bf16[8,4,128,2,64]{2,4,3,1,0:T(8,128)(2,1)} fusion(bf16[8,4,128,2,64]{2,4,3,1,0:T(8,128)(2,1)} %get-tuple-element.216, s32[]{:T(128)} %get-tuple-element.215, f32[4,2,64,128]{3,2,1,0:T(8,128)} %convolution_bitcast_fusion.2, f32[4,2,128,12,128]{2,4,3,1,0:T(8,128)} %get-tuple-element.201, f32[4,2,128]{2,1,0:T(2,128)S(1)} %add.92, ...), kind=kOutput, calls=%fused_computation.26.clone.1 | convolution fusion | flops 209321984 | bytes 9839152 | tf_op jit(solution)/shard_map/while/body/eval_jaxpr/qhajk,qjhke->qahe/dot_general | solution.py:105
  212.8 5.8 %fusion.58 = (f32[4,2,128]{2,1,0:T(2,128)S(1)}, f32[4,2,128,12,128]{2,4,3,1,0:T(8,128)}) fusion(pred[4,12]{1,0:T(4,128)(4,1)S(1)} %bitcast.132, bf16[4,12,2,64,128]{4,3,2,1,0:T(8,128)(2,1)} %bitcast.119, bf16[1,4,128,2,64]{2,1,4,3,0:T(4,128)(2,1)S(1)} %constant_dynamic-slice_fusion.2), kind=kOutput, calls=%fused_computation.9.clone.1 | convolution fusion | flops 206044160 | bytes 7999536 | tf_op jit(solution)/shard_map/while/body/eval_jaxpr/qahe,qjhek->qhajk/dot_general | solution.py:85
  224.9 4.2 fusion.59
  229.2 3.3 gather_fusion
  232.5 3.4 convolution_bitcast_fusion.2
  235.9 4.3 gather_fusion.3
  240.2 6.4 %fusion.61 = bf16[8,4,128,2,64]{2,4,3,1,0:T(8,128)(2,1)} fusion(bf16[8,4,128,2,64]{2,4,3,1,0:T(8,128)(2,1)} %get-tuple-element.216, s32[]{:T(128)} %get-tuple-element.215, f32[4,2,64,128]{3,2,1,0:T(8,128)} %convolution_bitcast_fusion.2, f32[4,2,128,12,128]{2,4,3,1,0:T(8,128)} %get-tuple-element.201, f32[4,2,128]{2,1,0:T(2,128)S(1)} %add.92, ...), kind=kOutput, calls=%fused_computation.26.clone.1 | convolution fusion | flops 209321984 | bytes 9839152 | tf_op jit(solution)/shard_map/while/body/eval_jaxpr/qhajk,qjhke->qahe/dot_general | solution.py:105
  249.6 5.8 %fusion.58 = (f32[4,2,128]{2,1,0:T(2,128)S(1)}, f32[4,2,128,12,128]{2,4,3,1,0:T(8,128)}) fusion(pred[4,12]{1,0:T(4,128)(4,1)S(1)} %bitcast.132, bf16[4,12,2,64,128]{4,3,2,1,0:T(8,128)(2,1)} %bitcast.119, bf16[1,4,128,2,64]{2,1,4,3,0:T(4,128)(2,1)S(1)} %constant_dynamic-slice_fusion.2), kind=kOutput, calls=%fused_computation.9.clone.1 | convolution fusion | flops 206044160 | bytes 7999536 | tf_op jit(solution)/shard_map/while/body/eval_jaxpr/qahe,qjhek->qhajk/dot_general | solution.py:85
  261.8 4.2 fusion.59
  266.0 3.3 gather_fusion
  269.3 3.4 convolution_bitcast_fusion.2
  272.7 4.3 gather_fusion.3
  277.1 6.4 %fusion.61 = bf16[8,4,128,2,64]{2,4,3,1,0:T(8,128)(2,1)} fusion(bf16[8,4,128,2,64]{2,4,3,1,0:T(8,128)(2,1)} %get-tuple-element.216, s32[]{:T(128)} %get-tuple-element.215, f32[4,2,64,128]{3,2,1,0:T(8,128)} %convolution_bitcast_fusion.2, f32[4,2,128,12,128]{2,4,3,1,0:T(8,128)} %get-tuple-element.201, f32[4,2,128]{2,1,0:T(2,128)S(1)} %add.92, ...), kind=kOutput, calls=%fused_computation.26.clone.1 | convolution fusion | flops 209321984 | bytes 9839152 | tf_op jit(solution)/shard_map/while/body/eval_jaxpr/qhajk,qjhke->qahe/dot_general | solution.py:105
  286.5 5.8 %fusion.58 = (f32[4,2,128]{2,1,0:T(2,128)S(1)}, f32[4,2,128,12,128]{2,4,3,1,0:T(8,128)}) fusion(pred[4,12]{1,0:T(4,128)(4,1)S(1)} %bitcast.132, bf16[4,12,2,64,128]{4,3,2,1,0:T(8,128)(2,1)} %bitcast.119, bf16[1,4,128,2,64]{2,1,4,3,0:T(4,128)(2,1)S(1)} %constant_dynamic-slice_fusion.2), kind=kOutput, calls=%fused_computation.9.clone.1 | convolution fusion | flops 206044160 | bytes 7999536 | tf_op jit(solution)/shard_map/while/body/eval_jaxpr/qahe,qjhek->qhajk/dot_general | solution.py:85
  298.6 4.2 fusion.59
  302.8 3.3 gather_fusion
  306.2 3.4 convolution_bitcast_fusion.2
  309.6 4.3 gather_fusion.3
  313.9 6.4 %fusion.61 = bf16[8,4,128,2,64]{2,4,3,1,0:T(8,128)(2,1)} fusion(bf16[8,4,128,2,64]{2,4,3,1,0:T(8,128)(2,1)} %get-tuple-element.216, s32[]{:T(128)} %get-tuple-element.215, f32[4,2,64,128]{3,2,1,0:T(8,128)} %convolution_bitcast_fusion.2, f32[4,2,128,12,128]{2,4,3,1,0:T(8,128)} %get-tuple-element.201, f32[4,2,128]{2,1,0:T(2,128)S(1)} %add.92, ...), kind=kOutput, calls=%fused_computation.26.clone.1 | convolution fusion | flops 209321984 | bytes 9839152 | tf_op jit(solution)/shard_map/while/body/eval_jaxpr/qhajk,qjhke->qahe/dot_general | solution.py:105
  323.3 5.8 %fusion.58 = (f32[4,2,128]{2,1,0:T(2,128)S(1)}, f32[4,2,128,12,128]{2,4,3,1,0:T(8,128)}) fusion(pred[4,12]{1,0:T(4,128)(4,1)S(1)} %bitcast.132, bf16[4,12,2,64,128]{4,3,2,1,0:T(8,128)(2,1)} %bitcast.119, bf16[1,4,128,2,64]{2,1,4,3,0:T(4,128)(2,1)S(1)} %constant_dynamic-slice_fusion.2), kind=kOutput, calls=%fused_computation.9.clone.1 | convolution fusion | flops 206044160 | bytes 7999536 | tf_op jit(solution)/shard_map/while/body/eval_jaxpr/qahe,qjhek->qhajk/dot_general | solution.py:85
  335.5 4.2 fusion.59
  339.7 3.3 gather_fusion
  343.0 3.4 convolution_bitcast_fusion.2
  346.4 4.3 gather_fusion.3
  350.8 6.4 %fusion.61 = bf16[8,4,128,2,64]{2,4,3,1,0:T(8,128)(2,1)} fusion(bf16[8,4,128,2,64]{2,4,3,1,0:T(8,128)(2,1)} %get-tuple-element.216, s32[]{:T(128)} %get-tuple-element.215, f32[4,2,64,128]{3,2,1,0:T(8,128)} %convolution_bitcast_fusion.2, f32[4,2,128,12,128]{2,4,3,1,0:T(8,128)} %get-tuple-element.201, f32[4,2,128]{2,1,0:T(2,128)S(1)} %add.92, ...), kind=kOutput, calls=%fused_computation.26.clone.1 | convolution fusion | flops 209321984 | bytes 9839152 | tf_op jit(solution)/shard_map/while/body/eval_jaxpr/qhajk,qjhke->qahe/dot_general | solution.py:105
  360.2 5.8 %fusion.58 = (f32[4,2,128]{2,1,0:T(2,128)S(1)}, f32[4,2,128,12,128]{2,4,3,1,0:T(8,128)}) fusion(pred[4,12]{1,0:T(4,128)(4,1)S(1)} %bitcast.132, bf16[4,12,2,64,128]{4,3,2,1,0:T(8,128)(2,1)} %bitcast.119, bf16[1,4,128,2,64]{2,1,4,3,0:T(4,128)(2,1)S(1)} %constant_dynamic-slice_fusion.2), kind=kOutput, calls=%fused_computation.9.clone.1 | convolution fusion | flops 206044160 | bytes 7999536 | tf_op jit(solution)/shard_map/while/body/eval_jaxpr/qahe,qjhek->qhajk/dot_general | solution.py:85
  372.3 4.2 fusion.59
  376.5 3.3 gather_fusion
  379.9 3.4 convolution_bitcast_fusion.2
  383.3 4.3 gather_fusion.3
  387.6 6.4 %fusion.61 = bf16[8,4,128,2,64]{2,4,3,1,0:T(8,128)(2,1)} fusion(bf16[8,4,128,2,64]{2,4,3,1,0:T(8,128)(2,1)} %get-tuple-element.216, s32[]{:T(128)} %get-tuple-element.215, f32[4,2,64,128]{3,2,1,0:T(8,128)} %convolution_bitcast_fusion.2, f32[4,2,128,12,128]{2,4,3,1,0:T(8,128)} %get-tuple-element.201, f32[4,2,128]{2,1,0:T(2,128)S(1)} %add.92, ...), kind=kOutput, calls=%fused_computation.26.clone.1 | convolution fusion | flops 209321984 | bytes 9839152 | tf_op jit(solution)/shard_map/while/body/eval_jaxpr/qhajk,qjhke->qahe/dot_general | solution.py:105
  397.0 5.8 %fusion.58 = (f32[4,2,128]{2,1,0:T(2,128)S(1)}, f32[4,2,128,12,128]{2,4,3,1,0:T(8,128)}) fusion(pred[4,12]{1,0:T(4,128)(4,1)S(1)} %bitcast.132, bf16[4,12,2,64,128]{4,3,2,1,0:T(8,128)(2,1)} %bitcast.119, bf16[1,4,128,2,64]{2,1,4,3,0:T(4,128)(2,1)S(1)} %constant_dynamic-slice_fusion.2), kind=kOutput, calls=%fused_computation.9.clone.1 | convolution fusion | flops 206044160 | bytes 7999536 | tf_op jit(solution)/shard_map/while/body/eval_jaxpr/qahe,qjhek->qhajk/dot_general | solution.py:85
  409.1 4.2 fusion.59
  416.7 3.4 convolution_bitcast_fusion.2
  420.1 4.3 gather_fusion.3
  424.5 6.4 %fusion.61 = bf16[8,4,128,2,64]{2,4,3,1,0:T(8,128)(2,1)} fusion(bf16[8,4,128,2,64]{2,4,3,1,0:T(8,128)(2,1)} %get-tuple-element.216, s32[]{:T(128)} %get-tuple-element.215, f32[4,2,64,128]{3,2,1,0:T(8,128)} %convolution_bitcast_fusion.2, f32[4,2,128,12,128]{2,4,3,1,0:T(8,128)} %get-tuple-element.201, f32[4,2,128]{2,1,0:T(2,128)S(1)} %add.92, ...), kind=kOutput, calls=%fused_computation.26.clone.1 | convolution fusion | flops 209321984 | bytes 9839152 | tf_op jit(solution)/shard_map/while/body/eval_jaxpr/qhajk,qjhke->qahe/dot_general | solution.py:105
  430.8 6.0 %copy.109 = bf16[8,4,128,2,64]{4,3,2,1,0:T(2,128)(2,1)} copy(bf16[8,4,128,2,64]{2,4,3,1,0:T(8,128)(2,1)} %get-tuple-element.57) | data formatting | bytes 2097152 | tf_op jit(solution)/shard_map/reshape | solution.py:122
  436.8 3.9 reshape.242
  440.7 19.0 %all_to_all.34 = bf16[8,512,128]{2,1,0:T(8,128)(2,1)S(1)} all-to-all(bf16[8,512,128]{2,1,0:T(8,128)(2,1)S(1)} %reshape.242), channel_id=1, replica_groups=mesh['cluster'=4,'seq'=8] {'seq'}, dimensions={0} | all-to-all | bytes 2097152 | tf_op jit(solution)/shard_map/all_to_all | solution.py:123
  (186 shorter events, 105.9 us)
Async XLA Ops:
  0.0 459.7 %copy-start = (bf16[1024,1024]{1,0:T(8,128)(2,1)S(1)}, bf16[1024,1024]{1,0:T(8,128)(2,1)}, u32[]{:S(2)}) copy-start(bf16[1024,1024]{1,0:T(8,128)(2,1)} %param.9) | copy-start | bytes 6291460
  3.1 21.6 %all-to-all-start.2 = ((s32[4,1,8]{2,1,0:T(1,128)}), s32[4,1,8]{2,1,0:T(1,128)S(1)}, u32[]{:S(2)}, u32[]{:S(2)}) async-start(s32[4,1,8]{2,1,0:T(1,128)} %bitcast.31), calls=%async_computation.2 | async-start | bytes 4096 | tf_op jit(solution)/shard_map/all_to_all | solution.py:57
  18.1 2.7 copy-start.4
  24.6 31.0 %all-to-all-start = ((bf16[8,512,256]{1,2,0:T(8,128)(2,1)}), bf16[8,512,256]{1,2,0:T(8,128)(2,1)}, u32[]{:S(2)}, u32[]{:S(2)}) async-start(bf16[8,512,256]{1,2,0:T(8,128)(2,1)} %convert_bitcast_fusion), calls=%async_computation | async-start | bytes 4194304 | tf_op jit(solution)/shard_map/all_to_all | solution.py:30
  29.0 1.9 copy-start.5
  55.6 19.7 %all-to-all-start.1 = ((bf16[8,512,128]{1,2,0:T(8,128)(2,1)}), bf16[8,512,128]{1,2,0:T(8,128)(2,1)}, u32[]{:S(2)}, u32[]{:S(2)}) async-start(bf16[8,512,128]{1,2,0:T(8,128)(2,1)} %fusion.32), calls=%async_computation.1 | async-start | bytes 2097152 | tf_op jit(solution)/shard_map/all_to_all | solution.py:29
  75.3 31.2 %all-to-all-start.4 = ((bf16[4,8,2,128,64]{3,4,2,1,0:T(8,128)(2,1)}), bf16[4,8,2,128,64]{3,4,2,1,0:T(8,128)(2,1)}, u32[]{:S(2)}, u32[]{:S(2)}) async-start(bf16[4,8,2,128,64]{3,4,2,1,0:T(8,128)(2,1)} %bitcast.36), calls=%async_computation.4 | async-start | bytes 2097152 | tf_op jit(solution)/shard_map/all_to_all | solution.py:64
  82.0 29.0 %copy-start.3 = (s32[32]{0:T(128)S(1)}, s32[32]{0:T(128)}, u32[]{:S(2)}) copy-start(s32[32]{0:T(128)} %param.11) | copy-start | bytes 388
  82.0 29.3 %copy-start.2 = (s32[32,16]{0,1:T(8,128)S(1)}, s32[32,16]{0,1:T(8,128)}, u32[]{:S(2)}) copy-start(s32[32,16]{0,1:T(8,128)} %param.10) | copy-start | bytes 6148
  106.5 29.6 %all-to-all-start.3 = ((bf16[4,8,2,64,128]{4,3,2,1,0:T(8,128)(2,1)}), bf16[4,8,2,64,128]{4,3,2,1,0:T(8,128)(2,1)}, u32[]{:S(2)}, u32[]{:S(2)}) async-start(bf16[4,8,2,64,128]{4,3,2,1,0:T(8,128)(2,1)} %bitcast.129), calls=%async_computation.3 | async-start | bytes 2097152 | tf_op jit(solution)/shard_map/all_to_all | solution.py:63
  149.4 1.3 copy-start.1
  186.2 1.3 copy-start.1
  223.1 1.3 copy-start.1
  259.9 1.3 copy-start.1
  296.8 1.3 copy-start.1
  333.6 1.3 copy-start.1
  370.5 1.3 copy-start.1
  407.3 1.3 copy-start.1
where the time goes:
time: 465 us; the launch traced here: 462 us
  local copies, waits for them, and re-layouts  169 us (36%)
  matrix products  147 us (32%)
  waiting for transfers between devices  62.1 us (13%)
  other arithmetic  40.7 us (9%)
  starting transfers between devices  24.4 us (5%)
  blocking collectives  19 us (4%)
    dot_general x8, matrix products, attend(): jnp.einsum('qhajk,qjhke->qahe', near_weight, near_v, preferred_element_ty...  51.1 us
    dot_general x8, matrix products, attend(): jnp.einsum('qahe,qjhek->qhajk', query_blk, near_k, preferred_element_type...  46 us
    gather x8, local copies, waits for them, and re-layouts, attend(): near_v = value_table[near_ids]  34.7 us
    reduce_sum x8, other arithmetic, attend(): jnp.sum(near_exp, axis=(3, 4), keepdims=True)  33.7 us
    dot_general x8, matrix products, attend(): jnp.einsum('qhajk,qjhke->qahe', far_weight, far_v, preferred_element_type...  27.2 us
    gather x8, local copies, waits for them, and re-layouts, attend(): far_v = far_values[far_ids]  26.7 us
    all_to_all x1, waiting for transfers between devices, on_device(): lax.all_to_all(out_values, 'cluster', split_axis=0, concat_axis=0, tiled=...  22.8 us
    all_to_all x1, waiting for transfers between devices, on_device(): lax.all_to_all(keyval_proj, 'seq', split_axis=0, concat_axis=0, tiled=True)  22.5 us
  transfers between devices with their start and end apart: 5, of which 4 were waited for; matrix products, arithmetic and copies ran while one was open for 10% of the time, Pallas kernels for 0%

commit v1 on v0

v1 whole, which is shorter than its diff:
```python
import functools

import jax
import jax.numpy as jnp
from jax import lax
from jax.experimental import pallas as pl
from jax.experimental.pallas import tpu as pltpu
from jax.sharding import PartitionSpec as P

D = 1024
HEADS = 16
HD = 64
BLK = 128
KVB = 16
REMOTE = 4
NEAR = KVB - REMOTE
LOG2E = 1.4426950408889634
F32 = jnp.float32
BF16 = jnp.bfloat16

ANY = pl.BlockSpec(memory_space=pl.ANY)
SMEM = pl.BlockSpec(memory_space=pltpu.SMEM)
VMEM = pl.BlockSpec(memory_space=pltpu.VMEM)


def params():
    return pltpu.CompilerParams(vmem_limit_bytes=44 * 1024 * 1024)


def cost(flops, byts, trans=0):
    return pl.CostEstimate(flops=flops, bytes_accessed=byts, transcendentals=trans)


def nt_dot(a, b):
    return lax.dot_general(a, b, (((1,), (1,)), ((), ())), preferred_element_type=F32)


def project(parts, heads_dev, npair, meta, own, other, w_qkv):
    rows = own.shape[0]
    group = 3 * HD * heads_dev
    shared = group % 128 != 0
    slab = 2 * group if shared else group
    top = slab if shared else max(s + n for part in parts for s, n in part)
    width = -(-top // 128) * 128
    heights = [sum(n for _, n in part) for part in parts]
    total = sum(heights)

    def body(meta_ref, own_ref, other_ref, w_ref, *refs):
        outs = refs[: len(parts) * npair]
        x, w, wt, turned, sems = refs[len(parts) * npair :]
        pair = meta_ref[0]
        core = meta_ref[1]
        loads = []
        for j in range(npair):
            dest = pair ^ j
            start = dest * slab if shared else (2 * dest + core) * slab
            loads.append(
                pltpu.make_async_copy(
                    w_ref.at[:, pl.ds(pl.multiple_of(start, 128), width)], w.at[j], sems.at[j]
                )
            )
        here = pl.multiple_of(core * rows, 128)
        there = pl.multiple_of((1 - core) * rows, 128)
        loads.append(pltpu.make_async_copy(own_ref, x.at[pl.ds(here, rows)], sems.at[npair]))
        loads.append(pltpu.make_async_copy(other_ref, x.at[pl.ds(there, rows)], sems.at[npair + 1]))
        for load in loads:
            load.start()
        for j in range(npair):
            loads[j].wait()
            if shared:
                turned[...] = w[j].T
            else:
                full = w[j].T
            at = j * total
            for part in parts:
                for s, n in part:
                    if shared:
                        off = pl.multiple_of(core * group + s, HD)
                        wt[at : at + n, :] = turned[pl.ds(off, n), :]
                    else:
                        wt[at : at + n, :] = full[s : s + n, :]
                    at += n
        loads[npair].wait()
        loads[npair + 1].wait()
        step = 256
        for r in range(0, 2 * rows, step):
            res = nt_dot(wt[...], x[r : r + step, :]).astype(BF16)
            for j in range(npair):
                at = j * total
                for k in range(len(parts)):
                    outs[k * npair + j][:, r : r + step] = res[at : at + heights[k], :]
                    at += heights[k]

    shapes = [jax.ShapeDtypeStruct((heights[k], 2 * rows), BF16) for k in range(len(parts)) for _ in range(npair)]
    outs = pl.pallas_call(
        body,
        out_shape=shapes,
        in_specs=[SMEM, ANY, ANY, ANY],
        out_specs=[VMEM] * len(shapes),
        scratch_shapes=[
            pltpu.VMEM((2 * rows, D), BF16),
            pltpu.VMEM((npair, D, width), BF16),
            pltpu.VMEM((npair * total, D), BF16),
            pltpu.VMEM((width, D) if shared else (16, 128), BF16),
            pltpu.SemaphoreType.DMA((npair + 2,)),
        ],
        compiler_params=params(),
        cost_estimate=cost(2 * 2 * rows * D * total * npair, 4 * rows * D + 2 * D * width * npair),
        name="project",
    )(meta, own, other, w_qkv)
    return [list(outs[k * npair : (k + 1) * npair]) for k in range(len(parts))]


def select(npair, ncl, cap, meta, asked, tables):
    wide = tables[0].shape[1]
    per = wide // BLK

    def body(meta_ref, asked_ref, *refs):
        tabs = refs[:npair]
        outs = refs[npair : npair + ncl - 1]
        held, in_sems, out_sems = refs[npair + ncl - 1 :]
        pair = meta_ref[0]
        cluster = meta_ref[2]
        loads = [
            pltpu.make_async_copy(tabs[j], held.at[pair ^ j], in_sems.at[j]) for j in range(npair)
        ]
        for load in loads:
            load.start()
        for load in loads:
            load.wait()
        sends = []
        for s in range(1, ncl):
            dest = lax.rem(cluster + s, ncl)
            for i in range(cap):
                block = asked_ref[dest * cap + i]
                lane = pl.multiple_of(lax.rem(block, per) * BLK, BLK)
                sends.append(
                    pltpu.make_async_copy(
                        held.at[block // per, :, pl.ds(lane, BLK)],
                        outs[s - 1].at[i],
                        out_sems.at[(s - 1) * cap + i],
                    )
                )
        for send in sends:
            send.start()
        for send in sends:
            send.wait()

    shape = jax.ShapeDtypeStruct((cap, 2 * HD, BLK), BF16)
    return pl.pallas_call(
        body,
        out_shape=[shape] * (ncl - 1),
        in_specs=[SMEM, SMEM] + [ANY] * npair,
        out_specs=[ANY] * (ncl - 1),
        scratch_shapes=[
            pltpu.VMEM((npair, 2 * HD, wide), BF16),
            pltpu.SemaphoreType.DMA((npair,)),
            pltpu.SemaphoreType.DMA(((ncl - 1) * cap,)),
        ],
        compiler_params=params(),
        cost_estimate=cost(0, 4 * npair * 2 * HD * wide),
        name="select",
    )(meta, asked, *tables)


def near_attention(heads_dev, npair, meta, ids, tables, queries):
    wide = queries[0].shape[1]
    per = wide // BLK
    nblk = npair * per
    feats = heads_dev * HD
    cols = heads_dev * BLK
    keys = NEAR * BLK

    def body(meta_ref, ids_ref, *refs):
        tabs = refs[: npair * heads_dev]
        qs = refs[npair * heads_dev : npair * (heads_dev + 1)]
        out_ref, stat_ref, kv, q, ktab, vtab, s_a, s_b, sems = refs[npair * (heads_dev + 1) :]
        pair = meta_ref[0]
        loads = []
        for h in range(heads_dev):
            for j in range(npair):
                k = h * npair + j
                loads.append(pltpu.make_async_copy(tabs[k], kv.at[h, pair ^ j], sems.at[k]))
        for j in range(npair):
            loads.append(
                pltpu.make_async_copy(qs[j], q.at[pair ^ j], sems.at[heads_dev * npair + j])
            )
        for load in loads:
            load.start()
        for load in loads:
            load.wait()

        def build(p, carry):
            for i in range(per):
                at = slice(i * BLK, (i + 1) * BLK)
                pieces = [kv[h, p, :, at] for h in range(heads_dev)]
                if heads_dev == 1:
                    ktab[p * per + i] = pieces[0].T
                else:
                    ktab[p * per + i] = jnp.concatenate([x[:HD] for x in pieces], axis=0).T
                vtab[p * per + i] = jnp.concatenate([x[HD:] for x in pieces], axis=0)
            return carry

        lax.fori_loop(0, npair, build, 0)

        def first(b, held):
            lane = pl.multiple_of(lax.rem(b, per) * BLK, BLK)
            qt = q[b // per, :, pl.ds(lane, BLK)] * jnp.asarray(HD**-0.5, BF16)
            zero = jnp.zeros((HD, BLK), BF16)
            if heads_dev == 1:
                qm = jnp.concatenate([qt, zero], axis=0)
            else:
                qm = jnp.concatenate(
                    [
                        jnp.concatenate([qt[:HD], zero], axis=1),
                        jnp.concatenate([zero, qt[HD:]], axis=1),
                    ],
                    axis=0,
                )
            top = None
            for j in range(NEAR):
                s = jnp.dot(ktab[ids_ref[b * NEAR + j]], qm, preferred_element_type=F32)
                held[j * BLK : (j + 1) * BLK, :] = s
                part = jnp.max(s.reshape(BLK // 8, 8, cols), axis=0)
                top = part if top is None else jnp.maximum(top, part)
            return jnp.max(top, axis=0, keepdims=True)

        def second(b, held, top):
            acc = None
            total = None
            for c in range(0, NEAR, 4):
                p = jnp.exp2((held[c * BLK : (c + 4) * BLK, :] - top) * LOG2E)
                part = jnp.sum(p.reshape(4 * BLK // 8, 8, cols), axis=0)
                total = part if total is None else total + part
                v = jnp.concatenate([vtab[ids_ref[b * NEAR + c + i]] for i in range(4)], axis=1)
                o = jnp.dot(v, p.astype(BF16), preferred_element_type=F32)
                acc = o if acc is None else acc + o
            out_ref[b] = jnp.concatenate(
                [
                    acc[h * HD : (h + 1) * HD, h * BLK : (h + 1) * BLK]
                    for h in range(heads_dev)
                ],
                axis=0,
            )
            stat_ref[b, 0:1, :] = top
            stat_ref[b, 1:2, :] = jnp.sum(total, axis=0, keepdims=True)

        def step(i, top):
            b = 2 * i
            top_b = first(b + 1, s_b)
            second(b, s_a, top)
            top_a = first(jnp.minimum(b + 2, nblk - 1), s_a)
            second(b + 1, s_b, top_b)
            return top_a

        lax.fori_loop(0, nblk // 2, step, first(0, s_a))

    flops = nblk * keys * BLK * feats * 4 * heads_dev
    return pl.pallas_call(
        body,
        out_shape=[
            jax.ShapeDtypeStruct((nblk, feats, BLK), F32),
            jax.ShapeDtypeStruct((nblk, 8, cols), F32),
        ],
        in_specs=[SMEM, SMEM] + [ANY] * (npair * (heads_dev + 1)),
        out_specs=[VMEM, VMEM],
        scratch_shapes=[
            pltpu.VMEM((heads_dev, npair, 2 * HD, wide), BF16),
            pltpu.VMEM((npair, feats, wide), BF16),
            pltpu.VMEM((nblk, BLK, 2 * HD), BF16),
            pltpu.VMEM((nblk, feats, BLK), BF16),
            pltpu.VMEM((keys, cols), F32),
            pltpu.VMEM((keys, cols), F32),
            pltpu.SemaphoreType.DMA((npair * (heads_dev + 1),)),
        ],
        compiler_params=params(),
        cost_estimate=cost(2 * flops, 8 * nblk * BLK * feats, nblk * keys * cols),
        name="near_attention",
    )(meta, ids, *tables, *queries)


def far_attention(head, heads_dev, npair, seq_size, ncl, cap, meta, pos, counts, tables, queries, near, stats):
    wide = queries[0].shape[1]
    per = wide // BLK
    nblk = npair * per
    dev_blocks = nblk // seq_size
    feats = heads_dev * HD
    low = head * HD

    def body(meta_ref, pos_ref, counts_ref, *refs):
        tabs = refs[: ncl - 1]
        qs = refs[ncl - 1 : ncl - 1 + npair]
        near_ref, stat_ref = refs[ncl - 1 + npair : ncl + 1 + npair]
        outs = refs[ncl + 1 + npair : ncl + 1 + npair + seq_size]
        kv, q, ktab, o, sems = refs[ncl + 1 + npair + seq_size :]
        pair = meta_ref[0]
        cluster = meta_ref[2]
        seq = meta_ref[3]
        loads = []
        for s in range(1, ncl):
            origin = lax.rem(cluster + ncl - s, ncl)
            loads.append(
                pltpu.make_async_copy(
                    tabs[s - 1], kv.at[pl.ds(origin * cap, cap)], sems.at[s - 1]
                )
            )
        for j in range(npair):
            loads.append(
                pltpu.make_async_copy(
                    qs[j].at[pl.ds(low, HD)], q.at[pair ^ j], sems.at[ncl - 1 + j]
                )
            )
        loads.append(
            pltpu.make_async_copy(near_ref.at[:, pl.ds(low, HD), :], o, sems.at[ncl - 1 + npair])
        )
        for load in loads:
            load.start()
        for load in loads:
            load.wait()

        def build(s, carry):
            origin = lax.rem(cluster + ncl - s, ncl) * cap
            for i in range(cap):
                ktab[origin + i] = kv[origin + i].T
            return carry

        lax.fori_loop(1, ncl, build, 0)

        def block(b):
            lane = pl.multiple_of(lax.rem(b, per) * BLK, BLK)
            qt = q[b // per, :, pl.ds(lane, BLK)] * jnp.asarray(HD**-0.5, BF16)
            qm = jnp.concatenate([qt, jnp.zeros((HD, BLK), BF16)], axis=0)
            valid = counts_ref[b] - NEAR
            scores = []
            top = stat_ref[b, 0:1, low * 2 : low * 2 + BLK]
            was = top
            for j in range(REMOTE):
                s = jnp.dot(ktab[pos_ref[b * REMOTE + j]], qm, preferred_element_type=F32)
                s = jnp.where(j < valid, s, -1e30)
                scores.append(s)
                top = jnp.maximum(top, jnp.max(s, axis=0, keepdims=True))
            p = jnp.exp2((jnp.concatenate(scores, axis=0) - top) * LOG2E)
            fade = jnp.exp2((was - top) * LOG2E)
            total = stat_ref[b, 1:2, low * 2 : low * 2 + BLK] * fade + jnp.sum(p, axis=0, keepdims=True)
            v = jnp.concatenate([kv[pos_ref[b * REMOTE + j], HD:, :] for j in range(REMOTE)], axis=1)
            acc = jnp.dot(v, p.astype(BF16), preferred_element_type=F32)
            return ((acc + o[b] * fade) / total).astype(BF16)

        for k in range(seq_size):
            first = (seq ^ k) * dev_blocks
            for i in range(dev_blocks):
                outs[k][:, i * BLK : (i + 1) * BLK] = block(first + i)

    keys = REMOTE * BLK
    flops = nblk * keys * BLK * HD * 4
    return pl.pallas_call(
        body,
        out_shape=[jax.ShapeDtypeStruct((HD, dev_blocks * BLK), BF16)] * seq_size,
        in_specs=[SMEM, SMEM, SMEM] + [ANY] * (ncl - 1 + npair) + [ANY, VMEM],
        out_specs=[VMEM] * seq_size,
        scratch_shapes=[
            pltpu.VMEM((ncl * cap, 2 * HD, BLK), BF16),
            pltpu.VMEM((npair, HD, wide), BF16),
            pltpu.VMEM((ncl * cap, BLK, 2 * HD), BF16),
            pltpu.VMEM((nblk, HD, BLK), F32),
            pltpu.SemaphoreType.DMA((ncl + npair,)),
        ],
        compiler_params=params(),
        cost_estimate=cost(2 * flops, 6 * nblk * BLK * HD, nblk * keys * BLK),
        name="far_attention",
    )(meta, pos, counts, *tables, *queries, near, stats)


def project_out(heads_dev, seq_size, meta, pieces, w_out):
    rows = pieces[0][0].shape[1]

    def body(meta_ref, *refs):
        parts = refs[: heads_dev * seq_size]
        w_ref, out_ref, at, sems = refs[heads_dev * seq_size :]
        seq = meta_ref[3]
        loads = []
        for h in range(heads_dev):
            for k in range(seq_size):
                row = pl.multiple_of(((seq ^ k) * heads_dev + h) * HD, HD)
                n = h * seq_size + k
                loads.append(pltpu.make_async_copy(parts[n], at.at[pl.ds(row, HD)], sems.at[n]))
        for load in loads:
            load.start()
        for load in loads:
            load.wait()
        for r in range(0, rows, 128):
            out_ref[r : r + 128, :] = jnp.dot(
                at[:, r : r + 128].T, w_ref[...], preferred_element_type=F32
            ).astype(BF16)

    return pl.pallas_call(
        body,
        out_shape=jax.ShapeDtypeStruct((rows, D), BF16),
        in_specs=[SMEM] + [ANY] * (heads_dev * seq_size) + [VMEM],
        out_specs=VMEM,
        scratch_shapes=[
            pltpu.VMEM((HEADS * HD, rows), BF16),
            pltpu.SemaphoreType.DMA((heads_dev * seq_size,)),
        ],
        compiler_params=params(),
        cost_estimate=cost(2 * rows * D * D, 2 * D * D + 4 * rows * D),
        name="project_out",
    )(meta, *[x for head in pieces for x in head], w_out)


def shifted(x, axis, size, shift):
    return lax.ppermute(x, axis, [(i, (i + shift) % size) for i in range(size)])


def crossed(x, size, k):
    return lax.ppermute(x, "seq", [(i, i ^ k) for i in range(size)])


def on_device(nodes, w_qkv, w_out, kv_ids, counts):
    seq_size = lax.axis_size("seq")
    ncl = lax.axis_size("cluster")
    heads_dev = HEADS // seq_size
    npair = seq_size // 2
    nblk = seq_size * nodes.shape[0] // BLK
    cap = nblk // 4
    seq = lax.axis_index("seq")
    cluster = lax.axis_index("cluster")
    meta = jnp.stack([seq // 2, seq % 2, cluster, seq]).astype(jnp.int32)

    other = crossed(nodes, seq_size, 1)

    near_ids = (kv_ids[:, :NEAR] - cluster * nblk).reshape(-1)
    remote_ids = kv_ids[:, NEAR:]
    valid = jnp.arange(NEAR, KVB, dtype=jnp.int32)[None, :] < counts[:, None]
    every = jnp.arange(ncl * nblk, dtype=jnp.int32)
    present = jnp.any(
        (remote_ids.reshape(-1)[:, None] == every[None, :]) & valid.reshape(-1)[:, None], axis=0
    )
    present = present.astype(jnp.int32).reshape(ncl, nblk)
    rank = jnp.cumsum(present, axis=1) - 1
    chosen = (rank[:, None, :] == jnp.arange(cap, dtype=jnp.int32)[None, :, None]) & (
        present[:, None, :] > 0
    )
    wanted = jnp.sum(jnp.where(chosen, jnp.arange(nblk, dtype=jnp.int32)[None, None, :], 0), axis=2)
    asked = lax.all_to_all(wanted, "cluster", split_axis=0, concat_axis=0, tiled=True).reshape(-1)
    place = (remote_ids // nblk) * cap + jnp.sum(
        jnp.where(remote_ids[:, :, None] == every[None, None, :], rank.reshape(-1)[None, None, :], 0),
        axis=2,
    )
    pos = jnp.where(valid, place, place[:, :1]).reshape(-1)

    spans = [[((3 * h + 1) * HD, 2 * HD)] for h in range(heads_dev)]
    q_span = [(3 * h * HD, HD) for h in range(heads_dev)]
    (kv_first,) = project(spans[:1], heads_dev, npair, meta, nodes, other, w_qkv)
    rest = project(spans[1:] + [q_span], heads_dev, npair, meta, nodes, other, w_qkv)
    kinds = [kv_first] + rest
    arrived = [
        [x if j == 0 else crossed(x, seq_size, 2 * j) for j, x in enumerate(kind)] for kind in kinds
    ]
    kvs, queries = arrived[:heads_dev], arrived[heads_dev]
    far = []
    for h in range(heads_dev):
        picked = select(npair, ncl, cap, meta, asked, kvs[h])
        far.append([shifted(x, "cluster", ncl, s + 1) for s, x in enumerate(picked)])
    near, stats = near_attention(
        heads_dev, npair, meta, near_ids, [x for kv in kvs for x in kv], queries
    )
    pieces = []
    for h in range(heads_dev):
        outs = far_attention(
            h, heads_dev, npair, seq_size, ncl, cap, meta, pos, counts, far[h], queries, near, stats
        )
        pieces.append([x if k == 0 else crossed(x, seq_size, k) for k, x in enumerate(outs)])
    return project_out(heads_dev, seq_size, meta, pieces, w_out)


def solution(mesh):
    placed = (P(("cluster", "seq"), None), P(), P(), P("cluster", None), P("cluster"))
    return jax.shard_map(
        on_device,
        mesh=mesh,
        in_specs=placed,
        out_specs=P(("cluster", "seq"), None),
        check_vma=False,
    )
```

time: 465 us -> 129 us (0.28)
  local copies, waits for them, and re-layouts: 169 us -> 9.38 us
  matrix products: 147 us -> 0 us
  Pallas kernels: 0 us -> 56.4 us
  waiting for transfers between devices: 62.1 us -> 17.8 us
  other arithmetic: 40.7 us -> 2.82 us
  blocking collectives: 19 us -> 0 us
  starting transfers between devices: 24.4 us -> 41.5 us
    dot_general x35 -> x0, matrix products: 147 us -> none  [the longest x8 51.1 us: attend(): jnp.einsum('qhajk,qjhke->qahe', near_weight, near_v, preferred_element_ty...]
    gather x34 -> x0, local copies, waits for them, and re-layouts: 101 us -> none  [the longest x8 34.7 us: attend(): near_v = value_table[near_ids]]
    all_to_all x4 -> x0, waiting for transfers between devices: 62.1 us -> none  [the longest x1 22.8 us: on_device(): lax.all_to_all(out_values, 'cluster', split_axis=0, concat_axis=0, tiled=...]
    pallas_call x0 -> x8, Pallas kernels: none -> 56.4 us  [the longest x1 19.7 us: near_attention(): pl.pallas_call(body, out_shape=[jax.ShapeDtypeStruct((nblk, feats, BLK),...]
    reduce_sum x18 -> x2, other arithmetic: 38.6 us -> 0.94 us  [the longest x1 0.72 us: on_device(): jnp.sum(jnp.where(chosen, jnp.arange(nblk, dtype=jnp.int32)[None, None, :...]
    ppermute x0 -> x30, starting transfers between devices: none -> 35.7 us  [the longest x24 25.4 us: crossed(): return lax.ppermute(x, 'seq', [(i, i ^ k) for i in range(size)])]
    all_to_all x1 -> x0, blocking collectives: 19 us -> none  [on_device(): lax.all_to_all(attended, 'seq', split_axis=0, concat_axis=0, tiled=True)]
    all_to_all x4 -> x0, starting transfers between devices: 18.1 us -> none  [the longest x1 5.09 us: on_device(): lax.all_to_all(out_values, 'cluster', split_axis=0, concat_axis=0, tiled=...]
  transfers between devices with their start and end apart: 5 -> 31, of which waited for: 4 -> 7; matrix products, arithmetic and copies ran while one was open for 10% -> 4% of each run, Pallas kernels for 0% -> 40%
where the time goes in v1:
time: 129 us; the launch traced here: 128 us
  Pallas kernels  56.4 us (44%)
  starting transfers between devices  41.5 us (32%)
  waiting for transfers between devices  17.8 us (14%)
  local copies, waits for them, and re-layouts  9.38 us (7%)
  other arithmetic  2.82 us (2%)
    ppermute x24, starting transfers between devices, crossed(): return lax.ppermute(x, 'seq', [(i, i ^ k) for i in range(size)])  25.4 us
    pallas_call x1, Pallas kernels, near_attention(): pl.pallas_call(body, out_shape=[jax.ShapeDtypeStruct((nblk, feats, BLK),...  19.7 us
    pallas_call x2, Pallas kernels, far_attention(): pl.pallas_call(body, out_shape=[jax.ShapeDtypeStruct((HD, dev_blocks * BL...  19.4 us
    ppermute x24, waiting for transfers between devices, crossed(): return lax.ppermute(x, 'seq', [(i, i ^ k) for i in range(size)])  17.8 us
    ppermute x6, starting transfers between devices, shifted(): return lax.ppermute(x, axis, [(i, (i + shift) % size) for i in range(size)])  10.2 us
    pallas_call x2, Pallas kernels, project(): pl.pallas_call(body, out_shape=shapes, in_specs=[SMEM, ANY, ANY, ANY], ou...  9.71 us
    unnamed x20, local copies, waits for them, and re-layouts  7.08 us
    all_to_all x1, starting transfers between devices, on_device(): lax.all_to_all(wanted, 'cluster', split_axis=0, concat_axis=0, tiled=True)  5.87 us
  transfers between devices with their start and end apart: 31, of which 7 were waited for; matrix products, arithmetic and copies ran while one was open for 4% of the time, Pallas kernels for 40%

profile of v1, /device:TPU:0, one launch (start us, length us, event | category | flops | bytes accessed | tf_op | source)
XLA Modules:
  0.0 128.4 jit_solution(14560581089693151102)
XLA Ops:
  0.0 0.5 collective-permute-start
  0.5 0.7 slice.9
  1.2 0.1 eq.46
  1.3 0.7 broadcast_compare_fusion.1
  2.1 0.1 copy.22
  2.2 0.1 lt.30
  2.3 0.1 fusion.1
  2.5 0.2 reduce_window_sum.11
  2.7 0.7 select_reduce_fusion.1
  3.5 5.9 %all-to-all-start = ((s32[4,1,8]{2,1,0:T(1,128)}), s32[4,1,8]{2,1,0:T(1,128)S(1)}, u32[]{:S(2)}, u32[]{:S(2)}) async-start(s32[4,1,8]{2,1,0:T(1,128)} %bitcast.6), calls=%async_computation | async-start | bytes 4096 | tf_op jit(solution)/shard_map/all_to_all | solution.py:445
  9.5 0.2 select_reduce_fusion
  9.7 2.8 %copy-done = bf16[1024,3072]{1,0:T(8,128)(2,1)S(1)} copy-done((bf16[1024,3072]{1,0:T(8,128)(2,1)S(1)}, bf16[1024,3072]{1,0:T(8,128)(2,1)}, u32[]{:S(2)}) %copy-start) | copy-done | bytes 6291480
  12.5 1.2 copy-done.1
  13.7 3.8 %project.2 = (bf16[128,1024]{1,0:T(8,128)(2,1)S(1)}, bf16[128,1024]{1,0:T(8,128)(2,1)}, bf16[128,1024]{1,0:T(8,128)(2,1)}, bf16[128,1024]{1,0:T(8,128)(2,1)S(1)}) custom-call(s32[4]{0:T(128)S(1)} %pad_add_fusion.meta_ref, bf16[512,1024]{1,0:T(8,128)(2,1)S(1)} %copy-done.1, bf16[512,1024]{1,0:T(8,128)(2,1)S(1)} %collective-permute-done.other_ref, ...), custom_call_target="tpu_custom_call" | custom-call | flops 1073741824 | bytes 4194304 | tf_op jit(solution)/shard_map/project/pallas_call | solution.py:95
  17.5 1.6 %collective-permute-start.1 = (bf16[128,1024]{1,0:T(8,128)(2,1)}, bf16[128,1024]{1,0:T(8,128)(2,1)S(1)}, u32[]{:S(2)}, u32[]{:S(2)}) collective-permute-start(bf16[128,1024]{1,0:T(8,128)(2,1)} %get-tuple-element.42), channel_id=1, source_target_pairs={{0,2},{1,3},{2,0},{3,1},{4,6},{5,7},{6,4},{7,5},{8,10},{9,11},{10,... | collective-permute-start | bytes 786440 | tf_op jit(solution)/shard_map/ppermute | solution.py:416
  19.1 1.5 %collective-permute-start.2 = (bf16[128,1024]{1,0:T(8,128)(2,1)}, bf16[128,1024]{1,0:T(8,128)(2,1)S(1)}, u32[]{:S(2)}, u32[]{:S(2)}) collective-permute-start(bf16[128,1024]{1,0:T(8,128)(2,1)} %get-tuple-element.43), channel_id=1, source_target_pairs={{0,4},{1,5},{2,6},{3,7},{4,0},{5,1},{6,2},{7,3},{8,12},{9,13},{10,... | collective-permute-start | bytes 786440 | tf_op jit(solution)/shard_map/ppermute | solution.py:416
  20.6 0.5 collective-permute-start.3
  21.1 6.0 %project.3 = (bf16[128,1024]{1,0:T(8,128)(2,1)S(1)}, bf16[128,1024]{1,0:T(8,128)(2,1)S(1)}, bf16[128,1024]{1,0:T(8,128)(2,1)}, bf16[128,1024]{1,0:T(8,128)(2,1)S...) custom-call(s32[4]{0:T(128)S(1)} %pad_add_fusion.meta_ref, ...), custom_call_target="tpu_custom_call" | custom-call | flops 2147483648 | bytes 5242880 | tf_op jit(solution)/shard_map/project/pallas_call | solution.py:95
  27.0 0.7 copy-done.8
  27.7 1.5 %collective-permute-start.10 = (bf16[128,1024]{1,0:T(8,128)(2,1)S(1)}, bf16[128,1024]{1,0:T(8,128)(2,1)S(1)}, u32[]{:S(2)}, u32[]{:S(2)}) collective-permute-start(bf16[128,1024]{1,0:T(8,128)(2,1)S(1)} %get-tuple-element.53), channel_id=1, source_target_pairs={{0,2},{1,3},{2,0},{3,1},{4,6},{5,7},{6,4},{7,5},{8,10},{9,11},{10,... | collective-permute-start | bytes 786440 | tf_op jit(solution)/shard_map/ppermute | solution.py:416
  29.2 1.5 %collective-permute-start.11 = (bf16[128,1024]{1,0:T(8,128)(2,1)}, bf16[128,1024]{1,0:T(8,128)(2,1)S(1)}, u32[]{:S(2)}, u32[]{:S(2)}) collective-permute-start(bf16[128,1024]{1,0:T(8,128)(2,1)} %get-tuple-element.54), channel_id=1, source_target_pairs={{0,4},{1,5},{2,6},{3,7},{4,0},{5,1},{6,2},{7,3},{8,12},{9,13},{10,... | collective-permute-start | bytes 786440 | tf_op jit(solution)/shard_map/ppermute | solution.py:416
  30.8 0.6 broadcast.53
  31.4 0.6 reduce.3
  32.1 0.5 collective-permute-start.7
  32.6 0.6 collective-permute-done.2.refs_2_
  33.2 2.4 %collective-permute-start.8 = (bf16[128,1024]{1,0:T(8,128)(2,1)}, bf16[128,1024]{1,0:T(8,128)(2,1)S(1)}, u32[]{:S(2)}, u32[]{:S(2)}) collective-permute-start(bf16[128,1024]{1,0:T(8,128)(2,1)} %get-tuple-element.50), channel_id=1, source_target_pairs={{0,4},{1,5},{2,6},{3,7},{4,0},{5,1},{6,2},{7,3},{8,12},{9,13},{10,... | collective-permute-start | bytes 786440 | tf_op jit(solution)/shard_map/ppermute | solution.py:416
  35.6 1.6 %select.12 = (bf16[8,128,128]{2,1,0:T(8,128)(2,1)}, bf16[8,128,128]{2,1,0:T(8,128)(2,1)S(1)}, bf16[8,128,128]{2,1,0:T(8,128)(2,1)S(1)}) custom-call(s32[4]{0:T(128)S(1)} %pad_add_fusion.meta_ref, s32[32]{0:T(128)S(1)} %reshape.57.asked_ref, bf16[128,1024]{1,0:T(8,128)(2,1)S(1)} %get-tuple-element.41.refs_0_, ...), custom_call_target="tpu_custom_call" | custom-call | bytes 2097152 | tf_op jit(solution)/shard_map/select/pallas_call | solution.py:150
  37.3 0.7 copy-done.6
  38.0 0.7 copy-done.7
  38.6 2.9 %collective-permute-start.12 = (bf16[128,1024]{1,0:T(8,128)(2,1)}, bf16[128,1024]{1,0:T(8,128)(2,1)S(1)}, u32[]{:S(2)}, u32[]{:S(2)}) collective-permute-start(bf16[128,1024]{1,0:T(8,128)(2,1)} %copy-done.8), channel_id=1, source_target_pairs={{0,6},{1,7},{2,4},{3,5},{4,2},{5,3},{6,0},{7,1},{8,14},{9,15},{10,... | collective-permute-start | bytes 786440 | tf_op jit(solution)/shard_map/ppermute | solution.py:416
  41.6 1.7 %collective-permute-start.4 = (bf16[8,128,128]{2,1,0:T(8,128)(2,1)}, bf16[8,128,128]{2,1,0:T(8,128)(2,1)S(1)}, u32[]{:S(2)}, u32[]{:S(2)}) collective-permute-start(bf16[8,128,128]{2,1,0:T(8,128)(2,1)} %get-tuple-element.45), channel_id=1, source_target_pairs={{0,8},{8,16},{16,24},{24,0},{1,9},{9,17},{17,25},{25,1},{2,10},{10... | collective-permute-start | bytes 786440 | tf_op jit(solution)/shard_map/ppermute | solution.py:412
  43.3 0.1 copy.23
  43.4 0.1 reshape.56.pos_ref
  43.6 0.1 reshape.58.ids_ref
  43.7 11.7 %collective-permute-done.12.refs_7_.refs_3_ = bf16[128,1024]{1,0:T(8,128)(2,1)S(1)} collective-permute-done((bf16[128,1024]{1,0:T(8,128)(2,1)}, bf16[128,1024]{1,0:T(8,128)(2,1)S(1)}, u32[]{:S(2)}, u32[]{:S(2)}) %collective-permute-start.12) | collective-permute-done | bytes 262176 | tf_op jit(solution)/shard_map/ppermute | solution.py:416
  55.4 2.6 %collective-permute-start.5 = (bf16[8,128,128]{2,1,0:T(8,128)(2,1)}, bf16[8,128,128]{2,1,0:T(8,128)(2,1)S(1)}, u32[]{:S(2)}, u32[]{:S(2)}) collective-permute-start(bf16[8,128,128]{2,1,0:T(8,128)(2,1)} %copy-done.7), channel_id=1, source_target_pairs={{0,16},{8,24},{16,0},{24,8},{1,17},{9,25},{17,1},{25,9},{2,18},{10... | collective-permute-start | bytes 786440 | tf_op jit(solution)/shard_map/ppermute | solution.py:412
  58.0 1.4 %select.13 = (bf16[8,128,128]{2,1,0:T(8,128)(2,1)S(1)}, bf16[8,128,128]{2,1,0:T(8,128)(2,1)S(1)}, bf16[8,128,128]{2,1,0:T(8,128)(2,1)S(1)}) custom-call(s32[4]{0:T(128)S(1)} %pad_add_fusion.meta_ref, s32[32]{0:T(128)S(1)} %reshape.57.asked_ref, bf16[128,1024]{1,0:T(8,128)(2,1)S(1)} %get-tuple-element.52.refs_4_.refs_0_, ...), custom_call_target="tpu_custom_call" | custom-call | bytes 2097152 | tf_op jit(solution)/shard_map/select/pallas_call | solution.py:150
  59.4 1.5 %collective-permute-start.6 = (bf16[8,128,128]{2,1,0:T(8,128)(2,1)}, bf16[8,128,128]{2,1,0:T(8,128)(2,1)S(1)}, u32[]{:S(2)}, u32[]{:S(2)}) collective-permute-start(bf16[8,128,128]{2,1,0:T(8,128)(2,1)} %copy-done.6), channel_id=1, source_target_pairs={{0,24},{8,0},{16,8},{24,16},{1,25},{9,1},{17,9},{25,17},{2,26},{10... | collective-permute-start | bytes 786440 | tf_op jit(solution)/shard_map/ppermute | solution.py:412
  61.0 0.6 collective-permute-start.20
  61.5 1.0 collective-permute-start.21
  62.5 2.9 %collective-permute-start.22 = (bf16[8,128,128]{2,1,0:T(8,128)(2,1)S(1)}, bf16[8,128,128]{2,1,0:T(8,128)(2,1)S(1)}, u32[]{:S(2)}, u32[]{:S(2)}) collective-permute-start(bf16[8,128,128]{2,1,0:T(8,128)(2,1)S(1)} %get-tuple-element.68), channel_id=1, source_target_pairs={{0,24},{8,0},{16,8},{24,16},{1,25},{9,1},{17,9},{25,17},{2,26},{10... | collective-permute-start | bytes 786440 | tf_op jit(solution)/shard_map/ppermute | solution.py:412
  65.4 0.9 copy-done.4
  66.3 19.7 %near_attention.1 = (f32[32,128,128]{2,1,0:T(8,128)S(1)}, f32[32,8,256]{2,1,0:T(8,128)S(1)}) custom-call(s32[4]{0:T(128)S(1)} %pad_add_fusion.meta_ref, s32[384]{0:T(512)S(1)} %reshape.58.ids_ref, bf16[128,1024]{1,0:T(8,128)(2,1)S(1)} %get-tuple-element.41.refs_0_, bf16[128,1024]{1,0:T(8,128)(2,1)S(1)} %collective-permute-done.1.refs_1_, ...), custom_call_target="tpu_custom_call" | custom-call | flops 12884901888 | bytes 4194304 | tf_op jit(solution)/shard_map/near_attention/pallas_call | solution.py:259
  86.1 9.6 %far_attention.2 = (bf16[64,512]{1,0:T(8,128)(2,1)S(1)}, bf16[64,512]{1,0:T(8,128)(2,1)S(1)}, bf16[64,512]{1,0:T(8,128)(2,1)S(1)}, bf16[64,512]{1,0:T(8,128)(2,1...) custom-call(s32[4]{0:T(128)S(1)} %pad_add_fusion.meta_ref, ...), custom_call_target="tpu_custom_call" | custom-call | flops 1073741824 | bytes 1572864 | tf_op jit(solution)/shard_map/far_attention/pallas_call | solution.py:356
  95.8 1.4 %collective-permute-start.14 = (bf16[64,512]{1,0:T(8,128)(2,1)S(1)}, bf16[64,512]{1,0:T(8,128)(2,1)S(1)}, u32[]{:S(2)}, u32[]{:S(2)}) collective-permute-start(bf16[64,512]{1,0:T(8,128)(2,1)S(1)} %get-tuple-element.60), channel_id=1, source_target_pairs={{0,2},{1,3},{2,0},{3,1},{4,6},{5,7},{6,4},{7,5},{8,10},{9,11},{10,... | collective-permute-start | bytes 196616 | tf_op jit(solution)/shard_map/ppermute | solution.py:416
  97.2 0.4 collective-permute-start.15
  97.6 0.5 collective-permute-start.16
  98.1 1.2 collective-permute-start.17
  99.3 9.8 %far_attention.3 = (bf16[64,512]{1,0:T(8,128)(2,1)S(1)}, bf16[64,512]{1,0:T(8,128)(2,1)S(1)}, bf16[64,512]{1,0:T(8,128)(2,1)S(1)}, bf16[64,512]{1,0:T(8,128)(2,1...) custom-call(s32[4]{0:T(128)S(1)} %pad_add_fusion.meta_ref, ...), custom_call_target="tpu_custom_call" | custom-call | flops 1073741824 | bytes 1572864 | tf_op jit(solution)/shard_map/far_attention/pallas_call | solution.py:356
  109.1 1.5 %collective-permute-start.18 = (bf16[64,512]{1,0:T(8,128)(2,1)S(1)}, bf16[64,512]{1,0:T(8,128)(2,1)S(1)}, u32[]{:S(2)}, u32[]{:S(2)}) collective-permute-start(bf16[64,512]{1,0:T(8,128)(2,1)S(1)} %get-tuple-element.64), channel_id=1, source_target_pairs={{0,6},{1,7},{2,4},{3,5},{4,2},{5,3},{6,0},{7,1},{8,14},{9,15},{10,... | collective-permute-start | bytes 196616 | tf_op jit(solution)/shard_map/ppermute | solution.py:416
  110.7 1.3 collective-permute-start.19
  111.9 0.3 collective-permute-start.23
  112.3 1.4 %collective-permute-start.24 = (bf16[64,512]{1,0:T(8,128)(2,1)S(1)}, bf16[64,512]{1,0:T(8,128)(2,1)S(1)}, u32[]{:S(2)}, u32[]{:S(2)}) collective-permute-start(bf16[64,512]{1,0:T(8,128)(2,1)S(1)} %get-tuple-element.71), channel_id=1, source_target_pairs={{0,2},{1,3},{2,0},{3,1},{4,6},{5,7},{6,4},{7,5},{8,10},{9,11},{10,... | collective-permute-start | bytes 196616 | tf_op jit(solution)/shard_map/ppermute | solution.py:416
  113.6 0.2 collective-permute-start.25
  113.8 0.8 collective-permute-done.18.refs_6_
  114.6 0.5 collective-permute-start.26
  115.1 0.5 collective-permute-done.19.refs_7_
  115.6 1.4 %collective-permute-start.27 = (bf16[64,512]{1,0:T(8,128)(2,1)S(1)}, bf16[64,512]{1,0:T(8,128)(2,1)S(1)}, u32[]{:S(2)}, u32[]{:S(2)}) collective-permute-start(bf16[64,512]{1,0:T(8,128)(2,1)S(1)} %get-tuple-element.74), channel_id=1, source_target_pairs={{0,5},{1,4},{2,7},{3,6},{4,1},{5,0},{6,3},{7,2},{8,13},{9,12},{10,... | collective-permute-start | bytes 196616 | tf_op jit(solution)/shard_map/ppermute | solution.py:416
  117.0 1.6 %collective-permute-start.28 = (bf16[64,512]{1,0:T(8,128)(2,1)S(1)}, bf16[64,512]{1,0:T(8,128)(2,1)S(1)}, u32[]{:S(2)}, u32[]{:S(2)}) collective-permute-start(bf16[64,512]{1,0:T(8,128)(2,1)S(1)} %get-tuple-element.75), channel_id=1, source_target_pairs={{0,6},{1,7},{2,4},{3,5},{4,2},{5,3},{6,0},{7,1},{8,14},{9,15},{10,... | collective-permute-start | bytes 196616 | tf_op jit(solution)/shard_map/ppermute | solution.py:416
  118.7 0.8 collective-permute-start.29
  119.5 0.4 collective-permute-done.27.refs_13_
  119.9 2.3 %collective-permute-done.28.refs_14_ = bf16[64,512]{1,0:T(8,128)(2,1)S(1)} collective-permute-done((bf16[64,512]{1,0:T(8,128)(2,1)S(1)}, bf16[64,512]{1,0:T(8,128)(2,1)S(1)}, u32[]{:S(2)}, u32[]{:S(2)}) %collective-permute-start.28) | collective-permute-done | bytes 65568 | tf_op jit(solution)/shard_map/ppermute | solution.py:416
  122.2 1.5 %collective-permute-done.29.refs_15_ = bf16[64,512]{1,0:T(8,128)(2,1)S(1)} collective-permute-done((bf16[64,512]{1,0:T(8,128)(2,1)S(1)}, bf16[64,512]{1,0:T(8,128)(2,1)S(1)}, u32[]{:S(2)}, u32[]{:S(2)}) %collective-permute-start.29) | collective-permute-done | bytes 65568 | tf_op jit(solution)/shard_map/ppermute | solution.py:416
  123.7 4.5 %project_out.1 = bf16[512,1024]{1,0:T(8,128)(2,1)} custom-call(s32[4]{0:T(128)S(1)} %pad_add_fusion.meta_ref, bf16[64,512]{1,0:T(8,128)(2,1)S(1)} %get-tuple-element.58.refs_0_, bf16[64,512]{1,0:T(8,128)(2,1)S(1)} %collective-permute-done.13.refs_1_, bf16[64,512]{1,0:T(8,128)(2,1)S(1)} %collective-permute-done.14.refs_2_, ...), custom_call_target="tpu_custom_call" | custom-call | flops 1073741824 | bytes 4194304 | tf_op jit(solution)/shard_map/project_out/pallas_call | solution.py:396
  (54 shorter events, 0.8 us)
Async XLA Ops:
  0.0 9.7 %collective-permute-start = (bf16[512,1024]{1,0:T(8,128)(2,1)}, bf16[512,1024]{1,0:T(8,128)(2,1)S(1)}, u32[]{:S(2)}, u32[]{:S(2)}) collective-permute-start(bf16[512,1024]{1,0:T(8,128)(2,1)} %own_ref.3), channel_id=1, source_target_pairs={{0,1},{1,0},{2,3},{3,2},{4,5},{5,4},{6,7},{7,6},{8,9},{9,8},{10,11... | collective-permute-start | bytes 3145736 | tf_op jit(solution)/shard_map/ppermute | solution.py:416
  3.5 27.3 %all-to-all-start = ((s32[4,1,8]{2,1,0:T(1,128)}), s32[4,1,8]{2,1,0:T(1,128)S(1)}, u32[]{:S(2)}, u32[]{:S(2)}) async-start(s32[4,1,8]{2,1,0:T(1,128)} %bitcast.6), calls=%async_computation | async-start | bytes 4096 | tf_op jit(solution)/shard_map/all_to_all | solution.py:445
  9.7 2.8 %copy-start = (bf16[1024,3072]{1,0:T(8,128)(2,1)S(1)}, bf16[1024,3072]{1,0:T(8,128)(2,1)}, u32[]{:S(2)}) copy-start(bf16[1024,3072]{1,0:T(8,128)(2,1)} %w_ref.3) | copy-start | bytes 18874372
  12.5 1.2 copy-start.1
  17.5 14.6 %collective-permute-start.1 = (bf16[128,1024]{1,0:T(8,128)(2,1)}, bf16[128,1024]{1,0:T(8,128)(2,1)S(1)}, u32[]{:S(2)}, u32[]{:S(2)}) collective-permute-start(bf16[128,1024]{1,0:T(8,128)(2,1)} %get-tuple-element.42), channel_id=1, source_target_pairs={{0,2},{1,3},{2,0},{3,1},{4,6},{5,7},{6,4},{7,5},{8,10},{9,11},{10,... | collective-permute-start | bytes 786440 | tf_op jit(solution)/shard_map/ppermute | solution.py:416
  19.1 14.2 %collective-permute-start.2 = (bf16[128,1024]{1,0:T(8,128)(2,1)}, bf16[128,1024]{1,0:T(8,128)(2,1)S(1)}, u32[]{:S(2)}, u32[]{:S(2)}) collective-permute-start(bf16[128,1024]{1,0:T(8,128)(2,1)} %get-tuple-element.43), channel_id=1, source_target_pairs={{0,4},{1,5},{2,6},{3,7},{4,0},{5,1},{6,2},{7,3},{8,12},{9,13},{10,... | collective-permute-start | bytes 786440 | tf_op jit(solution)/shard_map/ppermute | solution.py:416
  20.6 10.2 %copy-start.9 = (s32[32,16]{0,1:T(8,128)S(1)}, s32[32,16]{0,1:T(8,128)}, u32[]{:S(2)}) copy-start(s32[32,16]{0,1:T(8,128)} %param.8) | copy-start | bytes 6148
  20.6 22.7 %copy-start.5 = (s32[32]{0:T(128)S(1)}, s32[32]{0:T(128)}, u32[]{:S(2)}) copy-start(s32[32]{0:T(128)} %counts_ref.3) | copy-start | bytes 388
  20.6 15.0 %collective-permute-start.3 = (bf16[128,1024]{1,0:T(8,128)(2,1)S(1)}, bf16[128,1024]{1,0:T(8,128)(2,1)S(1)}, u32[]{:S(2)}, u32[]{:S(2)}) collective-permute-start(bf16[128,1024]{1,0:T(8,128)(2,1)S(1)} %get-tuple-element.44), channel_id=1, source_target_pairs={{0,6},{1,7},{2,4},{3,5},{4,2},{5,3},{6,0},{7,1},{8,14},{9,15},{10,... | collective-permute-start | bytes 786440 | tf_op jit(solution)/shard_map/ppermute | solution.py:416
  27.0 0.7 copy-start.8
  27.7 10.9 %collective-permute-start.10 = (bf16[128,1024]{1,0:T(8,128)(2,1)S(1)}, bf16[128,1024]{1,0:T(8,128)(2,1)S(1)}, u32[]{:S(2)}, u32[]{:S(2)}) collective-permute-start(bf16[128,1024]{1,0:T(8,128)(2,1)S(1)} %get-tuple-element.53), channel_id=1, source_target_pairs={{0,2},{1,3},{2,0},{3,1},{4,6},{5,7},{6,4},{7,5},{8,10},{9,11},{10,... | collective-permute-start | bytes 786440 | tf_op jit(solution)/shard_map/ppermute | solution.py:416
  29.2 12.3 %collective-permute-start.11 = (bf16[128,1024]{1,0:T(8,128)(2,1)}, bf16[128,1024]{1,0:T(8,128)(2,1)S(1)}, u32[]{:S(2)}, u32[]{:S(2)}) collective-permute-start(bf16[128,1024]{1,0:T(8,128)(2,1)} %get-tuple-element.54), channel_id=1, source_target_pairs={{0,4},{1,5},{2,6},{3,7},{4,0},{5,1},{6,2},{7,3},{8,12},{9,13},{10,... | collective-permute-start | bytes 786440 | tf_op jit(solution)/shard_map/ppermute | solution.py:416
  32.1 27.3 %collective-permute-start.7 = (bf16[128,1024]{1,0:T(8,128)(2,1)}, bf16[128,1024]{1,0:T(8,128)(2,1)S(1)}, u32[]{:S(2)}, u32[]{:S(2)}) collective-permute-start(bf16[128,1024]{1,0:T(8,128)(2,1)} %get-tuple-element.49), channel_id=1, source_target_pairs={{0,2},{1,3},{2,0},{3,1},{4,6},{5,7},{6,4},{7,5},{8,10},{9,11},{10,... | collective-permute-start | bytes 786440 | tf_op jit(solution)/shard_map/ppermute | solution.py:416
  33.2 27.7 %collective-permute-start.8 = (bf16[128,1024]{1,0:T(8,128)(2,1)}, bf16[128,1024]{1,0:T(8,128)(2,1)S(1)}, u32[]{:S(2)}, u32[]{:S(2)}) collective-permute-start(bf16[128,1024]{1,0:T(8,128)(2,1)} %get-tuple-element.50), channel_id=1, source_target_pairs={{0,4},{1,5},{2,6},{3,7},{4,0},{5,1},{6,2},{7,3},{8,12},{9,13},{10,... | collective-permute-start | bytes 786440 | tf_op jit(solution)/shard_map/ppermute | solution.py:416
  35.6 25.9 %collective-permute-start.9 = (bf16[128,1024]{1,0:T(8,128)(2,1)}, bf16[128,1024]{1,0:T(8,128)(2,1)S(1)}, u32[]{:S(2)}, u32[]{:S(2)}) collective-permute-start(bf16[128,1024]{1,0:T(8,128)(2,1)} %get-tuple-element.51), channel_id=1, source_target_pairs={{0,6},{1,7},{2,4},{3,5},{4,2},{5,3},{6,0},{7,1},{8,14},{9,15},{10,... | collective-permute-start | bytes 786440 | tf_op jit(solution)/shard_map/ppermute | solution.py:416
  37.2 0.7 copy-start.6
  38.0 0.7 copy-start.7
  38.6 16.8 %collective-permute-start.12 = (bf16[128,1024]{1,0:T(8,128)(2,1)}, bf16[128,1024]{1,0:T(8,128)(2,1)S(1)}, u32[]{:S(2)}, u32[]{:S(2)}) collective-permute-start(bf16[128,1024]{1,0:T(8,128)(2,1)} %copy-done.8), channel_id=1, source_target_pairs={{0,6},{1,7},{2,4},{3,5},{4,2},{5,3},{6,0},{7,1},{8,14},{9,15},{10,... | collective-permute-start | bytes 786440 | tf_op jit(solution)/shard_map/ppermute | solution.py:416
  41.6 20.9 %collective-permute-start.4 = (bf16[8,128,128]{2,1,0:T(8,128)(2,1)}, bf16[8,128,128]{2,1,0:T(8,128)(2,1)S(1)}, u32[]{:S(2)}, u32[]{:S(2)}) collective-permute-start(bf16[8,128,128]{2,1,0:T(8,128)(2,1)} %get-tuple-element.45), channel_id=1, source_target_pairs={{0,8},{8,16},{16,24},{24,0},{1,9},{9,17},{17,25},{25,1},{2,10},{10... | collective-permute-start | bytes 786440 | tf_op jit(solution)/shard_map/ppermute | solution.py:412
  55.4 10.0 %copy-start.3 = (bf16[128,1024]{1,0:T(8,128)(2,1)}, bf16[128,1024]{1,0:T(8,128)(2,1)S(1)}, u32[]{:S(2)}) copy-start(bf16[128,1024]{1,0:T(8,128)(2,1)S(1)} %collective-permute-done.12.refs_7_.refs_3_) | copy-start | bytes 786436
  55.4 30.7 %collective-permute-start.5 = (bf16[8,128,128]{2,1,0:T(8,128)(2,1)}, bf16[8,128,128]{2,1,0:T(8,128)(2,1)S(1)}, u32[]{:S(2)}, u32[]{:S(2)}) collective-permute-start(bf16[8,128,128]{2,1,0:T(8,128)(2,1)} %copy-done.7), channel_id=1, source_target_pairs={{0,16},{8,24},{16,0},{24,8},{1,17},{9,25},{17,1},{25,9},{2,18},{10... | collective-permute-start | bytes 786440 | tf_op jit(solution)/shard_map/ppermute | solution.py:412
  59.4 26.6 %collective-permute-start.6 = (bf16[8,128,128]{2,1,0:T(8,128)(2,1)}, bf16[8,128,128]{2,1,0:T(8,128)(2,1)S(1)}, u32[]{:S(2)}, u32[]{:S(2)}) collective-permute-start(bf16[8,128,128]{2,1,0:T(8,128)(2,1)} %copy-done.6), channel_id=1, source_target_pairs={{0,24},{8,0},{16,8},{24,16},{1,25},{9,1},{17,9},{25,17},{2,26},{10... | collective-permute-start | bytes 786440 | tf_op jit(solution)/shard_map/ppermute | solution.py:412
  61.0 36.2 %collective-permute-start.20 = (bf16[8,128,128]{2,1,0:T(8,128)(2,1)S(1)}, bf16[8,128,128]{2,1,0:T(8,128)(2,1)S(1)}, u32[]{:S(2)}, u32[]{:S(2)}) collective-permute-start(bf16[8,128,128]{2,1,0:T(8,128)(2,1)S(1)} %get-tuple-element.66), channel_id=1, source_target_pairs={{0,8},{8,16},{16,24},{24,0},{1,9},{9,17},{17,25},{25,1},{2,10},{10... | collective-permute-start | bytes 786440 | tf_op jit(solution)/shard_map/ppermute | solution.py:412
  61.5 36.1 %collective-permute-start.21 = (bf16[8,128,128]{2,1,0:T(8,128)(2,1)S(1)}, bf16[8,128,128]{2,1,0:T(8,128)(2,1)S(1)}, u32[]{:S(2)}, u32[]{:S(2)}) collective-permute-start(bf16[8,128,128]{2,1,0:T(8,128)(2,1)S(1)} %get-tuple-element.67), channel_id=1, source_target_pairs={{0,16},{8,24},{16,0},{24,8},{1,17},{9,25},{17,1},{25,9},{2,18},{10... | collective-permute-start | bytes 786440 | tf_op jit(solution)/shard_map/ppermute | solution.py:412
  62.5 35.7 %collective-permute-start.22 = (bf16[8,128,128]{2,1,0:T(8,128)(2,1)S(1)}, bf16[8,128,128]{2,1,0:T(8,128)(2,1)S(1)}, u32[]{:S(2)}, u32[]{:S(2)}) collective-permute-start(bf16[8,128,128]{2,1,0:T(8,128)(2,1)S(1)} %get-tuple-element.68), channel_id=1, source_target_pairs={{0,24},{8,0},{16,8},{24,16},{1,25},{9,1},{17,9},{25,17},{2,26},{10... | collective-permute-start | bytes 786440 | tf_op jit(solution)/shard_map/ppermute | solution.py:412
  65.4 1.0 copy-start.4
  95.7 13.5 %collective-permute-start.13 = (bf16[64,512]{1,0:T(8,128)(2,1)S(1)}, bf16[64,512]{1,0:T(8,128)(2,1)S(1)}, u32[]{:S(2)}, u32[]{:S(2)}) collective-permute-start(bf16[64,512]{1,0:T(8,128)(2,1)S(1)} %get-tuple-element.59), channel_id=1, source_target_pairs={{0,1},{1,0},{2,3},{3,2},{4,5},{5,4},{6,7},{7,6},{8,9},{9,8},{10,11... | collective-permute-start | bytes 196616 | tf_op jit(solution)/shard_map/ppermute | solution.py:416
  95.8 14.9 %collective-permute-start.14 = (bf16[64,512]{1,0:T(8,128)(2,1)S(1)}, bf16[64,512]{1,0:T(8,128)(2,1)S(1)}, u32[]{:S(2)}, u32[]{:S(2)}) collective-permute-start(bf16[64,512]{1,0:T(8,128)(2,1)S(1)} %get-tuple-element.60), channel_id=1, source_target_pairs={{0,2},{1,3},{2,0},{3,1},{4,6},{5,7},{6,4},{7,5},{8,10},{9,11},{10,... | collective-permute-start | bytes 196616 | tf_op jit(solution)/shard_map/ppermute | solution.py:416
  97.2 14.7 %collective-permute-start.15 = (bf16[64,512]{1,0:T(8,128)(2,1)S(1)}, bf16[64,512]{1,0:T(8,128)(2,1)S(1)}, u32[]{:S(2)}, u32[]{:S(2)}) collective-permute-start(bf16[64,512]{1,0:T(8,128)(2,1)S(1)} %get-tuple-element.61), channel_id=1, source_target_pairs={{0,3},{1,2},{2,1},{3,0},{4,7},{5,6},{6,5},{7,4},{8,11},{9,10},{10,... | collective-permute-start | bytes 196616 | tf_op jit(solution)/shard_map/ppermute | solution.py:416
  97.6 14.6 %collective-permute-start.16 = (bf16[64,512]{1,0:T(8,128)(2,1)S(1)}, bf16[64,512]{1,0:T(8,128)(2,1)S(1)}, u32[]{:S(2)}, u32[]{:S(2)}) collective-permute-start(bf16[64,512]{1,0:T(8,128)(2,1)S(1)} %get-tuple-element.62), channel_id=1, source_target_pairs={{0,4},{1,5},{2,6},{3,7},{4,0},{5,1},{6,2},{7,3},{8,12},{9,13},{10,... | collective-permute-start | bytes 196616 | tf_op jit(solution)/shard_map/ppermute | solution.py:416
  98.1 25.5 %copy-start.2 = (bf16[1024,1024]{1,0:T(8,128)(2,1)S(1)}, bf16[1024,1024]{1,0:T(8,128)(2,1)}, u32[]{:S(2)}) copy-start(bf16[1024,1024]{1,0:T(8,128)(2,1)} %refs_16_.1) | copy-start | bytes 6291460
  98.1 15.5 %collective-permute-start.17 = (bf16[64,512]{1,0:T(8,128)(2,1)S(1)}, bf16[64,512]{1,0:T(8,128)(2,1)S(1)}, u32[]{:S(2)}, u32[]{:S(2)}) collective-permute-start(bf16[64,512]{1,0:T(8,128)(2,1)S(1)} %get-tuple-element.63), channel_id=1, source_target_pairs={{0,5},{1,4},{2,7},{3,6},{4,1},{5,0},{6,3},{7,2},{8,13},{9,12},{10,... | collective-permute-start | bytes 196616 | tf_op jit(solution)/shard_map/ppermute | solution.py:416
  109.1 5.4 %collective-permute-start.18 = (bf16[64,512]{1,0:T(8,128)(2,1)S(1)}, bf16[64,512]{1,0:T(8,128)(2,1)S(1)}, u32[]{:S(2)}, u32[]{:S(2)}) collective-permute-start(bf16[64,512]{1,0:T(8,128)(2,1)S(1)} %get-tuple-element.64), channel_id=1, source_target_pairs={{0,6},{1,7},{2,4},{3,5},{4,2},{5,3},{6,0},{7,1},{8,14},{9,15},{10,... | collective-permute-start | bytes 196616 | tf_op jit(solution)/shard_map/ppermute | solution.py:416
  110.7 5.0 %collective-permute-start.19 = (bf16[64,512]{1,0:T(8,128)(2,1)S(1)}, bf16[64,512]{1,0:T(8,128)(2,1)S(1)}, u32[]{:S(2)}, u32[]{:S(2)}) collective-permute-start(bf16[64,512]{1,0:T(8,128)(2,1)S(1)} %get-tuple-element.65), channel_id=1, source_target_pairs={{0,7},{1,6},{2,5},{3,4},{4,3},{5,2},{6,1},{7,0},{8,15},{9,14},{10,... | collective-permute-start | bytes 196616 | tf_op jit(solution)/shard_map/ppermute | solution.py:416
  111.9 5.1 %collective-permute-start.23 = (bf16[64,512]{1,0:T(8,128)(2,1)S(1)}, bf16[64,512]{1,0:T(8,128)(2,1)S(1)}, u32[]{:S(2)}, u32[]{:S(2)}) collective-permute-start(bf16[64,512]{1,0:T(8,128)(2,1)S(1)} %get-tuple-element.70), channel_id=1, source_target_pairs={{0,1},{1,0},{2,3},{3,2},{4,5},{5,4},{6,7},{7,6},{8,9},{9,8},{10,11... | collective-permute-start | bytes 196616 | tf_op jit(solution)/shard_map/ppermute | solution.py:416
  112.3 6.4 %collective-permute-start.24 = (bf16[64,512]{1,0:T(8,128)(2,1)S(1)}, bf16[64,512]{1,0:T(8,128)(2,1)S(1)}, u32[]{:S(2)}, u32[]{:S(2)}) collective-permute-start(bf16[64,512]{1,0:T(8,128)(2,1)S(1)} %get-tuple-element.71), channel_id=1, source_target_pairs={{0,2},{1,3},{2,0},{3,1},{4,6},{5,7},{6,4},{7,5},{8,10},{9,11},{10,... | collective-permute-start | bytes 196616 | tf_op jit(solution)/shard_map/ppermute | solution.py:416
  113.6 5.8 %collective-permute-start.25 = (bf16[64,512]{1,0:T(8,128)(2,1)S(1)}, bf16[64,512]{1,0:T(8,128)(2,1)S(1)}, u32[]{:S(2)}, u32[]{:S(2)}) collective-permute-start(bf16[64,512]{1,0:T(8,128)(2,1)S(1)} %get-tuple-element.72), channel_id=1, source_target_pairs={{0,3},{1,2},{2,1},{3,0},{4,7},{5,6},{6,5},{7,4},{8,11},{9,10},{10,... | collective-permute-start | bytes 196616 | tf_op jit(solution)/shard_map/ppermute | solution.py:416
  114.6 4.9 %collective-permute-start.26 = (bf16[64,512]{1,0:T(8,128)(2,1)S(1)}, bf16[64,512]{1,0:T(8,128)(2,1)S(1)}, u32[]{:S(2)}, u32[]{:S(2)}) collective-permute-start(bf16[64,512]{1,0:T(8,128)(2,1)S(1)} %get-tuple-element.73), channel_id=1, source_target_pairs={{0,4},{1,5},{2,6},{3,7},{4,0},{5,1},{6,2},{7,3},{8,12},{9,13},{10,... | collective-permute-start | bytes 196616 | tf_op jit(solution)/shard_map/ppermute | solution.py:416
  115.6 4.3 %collective-permute-start.27 = (bf16[64,512]{1,0:T(8,128)(2,1)S(1)}, bf16[64,512]{1,0:T(8,128)(2,1)S(1)}, u32[]{:S(2)}, u32[]{:S(2)}) collective-permute-start(bf16[64,512]{1,0:T(8,128)(2,1)S(1)} %get-tuple-element.74), channel_id=1, source_target_pairs={{0,5},{1,4},{2,7},{3,6},{4,1},{5,0},{6,3},{7,2},{8,13},{9,12},{10,... | collective-permute-start | bytes 196616 | tf_op jit(solution)/shard_map/ppermute | solution.py:416
  117.0 5.2 %collective-permute-start.28 = (bf16[64,512]{1,0:T(8,128)(2,1)S(1)}, bf16[64,512]{1,0:T(8,128)(2,1)S(1)}, u32[]{:S(2)}, u32[]{:S(2)}) collective-permute-start(bf16[64,512]{1,0:T(8,128)(2,1)S(1)} %get-tuple-element.75), channel_id=1, source_target_pairs={{0,6},{1,7},{2,4},{3,5},{4,2},{5,3},{6,0},{7,1},{8,14},{9,15},{10,... | collective-permute-start | bytes 196616 | tf_op jit(solution)/shard_map/ppermute | solution.py:416
  118.7 5.0 %collective-permute-start.29 = (bf16[64,512]{1,0:T(8,128)(2,1)S(1)}, bf16[64,512]{1,0:T(8,128)(2,1)S(1)}, u32[]{:S(2)}, u32[]{:S(2)}) collective-permute-start(bf16[64,512]{1,0:T(8,128)(2,1)S(1)} %get-tuple-element.76), channel_id=1, source_target_pairs={{0,7},{1,6},{2,5},{3,4},{4,3},{5,2},{6,1},{7,0},{8,15},{9,14},{10,... | collective-permute-start | bytes 196616 | tf_op jit(solution)/shard_map/ppermute | solution.py:416

commit v2 on v1

v2 whole, which is shorter than its diff:
```python
import jax
import jax.numpy as jnp
from jax import lax
from jax.experimental import pallas as pl
from jax.experimental.pallas import tpu as pltpu
from jax.sharding import PartitionSpec as P

D = 1024
HEADS = 16
HD = 64
BLK = 128
KVB = 16
REMOTE = 4
NEAR = KVB - REMOTE
LOG2E = 1.4426950408889634
F32 = jnp.float32
BF16 = jnp.bfloat16

ANY = pl.BlockSpec(memory_space=pl.ANY)
SMEM = pl.BlockSpec(memory_space=pltpu.SMEM)
VMEM = pl.BlockSpec(memory_space=pltpu.VMEM)


def params(mib):
    return pltpu.CompilerParams(vmem_limit_bytes=mib * 1024 * 1024)


def cost(flops, byts, trans=0):
    return pl.CostEstimate(flops=flops, bytes_accessed=byts, transcendentals=trans)


def nt_dot(a, b):
    return lax.dot_general(a, b, (((1,), (1,)), ((), ())), preferred_element_type=F32)


def project(parts, heads_dev, npair, meta, own, other, w_qkv):
    rows = own.shape[0]
    group = 3 * HD * heads_dev
    shared = group % 128 != 0
    slab = 2 * group if shared else group
    top = slab if shared else max(s + n for part in parts for s, n in part)
    width = -(-top // 128) * 128
    heights = [sum(n for _, n in part) for part in parts]
    total = sum(heights)

    def body(meta_ref, own_ref, other_ref, w_ref, *refs):
        outs = refs[: len(parts) * npair]
        x, w, wt, turned, sems = refs[len(parts) * npair :]
        pair = meta_ref[0]
        core = meta_ref[1]
        loads = []
        for j in range(npair):
            dest = pair ^ j
            start = dest * slab if shared else (2 * dest + core) * slab
            loads.append(
                pltpu.make_async_copy(
                    w_ref.at[:, pl.ds(pl.multiple_of(start, 128), width)], w.at[j], sems.at[j]
                )
            )
        here = pl.multiple_of(core * rows, 128)
        there = pl.multiple_of((1 - core) * rows, 128)
        loads.append(pltpu.make_async_copy(own_ref, x.at[pl.ds(here, rows)], sems.at[npair]))
        loads.append(pltpu.make_async_copy(other_ref, x.at[pl.ds(there, rows)], sems.at[npair + 1]))
        for load in loads:
            load.start()
        for j in range(npair):
            loads[j].wait()
            if shared:
                turned[...] = w[j].T
            else:
                full = w[j].T
            at = j * total
            for part in parts:
                for s, n in part:
                    if shared:
                        off = pl.multiple_of(core * group + s, HD)
                        wt[at : at + n, :] = turned[pl.ds(off, n), :]
                    else:
                        wt[at : at + n, :] = full[s : s + n, :]
                    at += n
        loads[npair].wait()
        loads[npair + 1].wait()
        step = 256
        for r in range(0, 2 * rows, step):
            res = nt_dot(wt[...], x[r : r + step, :]).astype(BF16)
            for j in range(npair):
                at = j * total
                for k in range(len(parts)):
                    outs[k * npair + j][:, r : r + step] = res[at : at + heights[k], :]
                    at += heights[k]

    shapes = [jax.ShapeDtypeStruct((heights[k], 2 * rows), BF16) for k in range(len(parts)) for _ in range(npair)]
    outs = pl.pallas_call(
        body,
        out_shape=shapes,
        in_specs=[SMEM, ANY, ANY, ANY],
        out_specs=[VMEM] * len(shapes),
        scratch_shapes=[
            pltpu.VMEM((2 * rows, D), BF16),
            pltpu.VMEM((npair, D, width), BF16),
            pltpu.VMEM((npair * total, D), BF16),
            pltpu.VMEM((width, D) if shared else (16, 128), BF16),
            pltpu.SemaphoreType.DMA((npair + 2,)),
        ],
        compiler_params=params(60),
        cost_estimate=cost(2 * 2 * rows * D * total * npair, 4 * rows * D + 2 * D * width * npair),
        name="project",
    )(meta, own, other, w_qkv)
    return [list(outs[k * npair : (k + 1) * npair]) for k in range(len(parts))]


def select(npair, ncl, cap, meta, asked, tables, row):
    wide = tables[0].shape[1]
    per = wide // BLK

    def body(meta_ref, asked_ref, *refs):
        tabs = refs[:npair]
        outs = refs[npair : npair + ncl - 1]
        held, in_sems, out_sems = refs[npair + ncl - 1 :]
        pair = meta_ref[0]
        cluster = meta_ref[2]
        loads = [
            pltpu.make_async_copy(tabs[j].at[pl.ds(row, 2 * HD)], held.at[pair ^ j], in_sems.at[j])
            for j in range(npair)
        ]
        for load in loads:
            load.start()
        for load in loads:
            load.wait()
        sends = []
        for s in range(1, ncl):
            dest = lax.rem(cluster + s, ncl)
            for i in range(cap):
                block = asked_ref[dest, 0, i]
                lane = pl.multiple_of(lax.rem(block, per) * BLK, BLK)
                sends.append(
                    pltpu.make_async_copy(
                        held.at[block // per, :, pl.ds(lane, BLK)],
                        outs[s - 1].at[i],
                        out_sems.at[(s - 1) * cap + i],
                    )
                )
        for send in sends:
            send.start()
        for send in sends:
            send.wait()

    shape = jax.ShapeDtypeStruct((cap, 2 * HD, BLK), BF16)
    return pl.pallas_call(
        body,
        out_shape=[shape] * (ncl - 1),
        in_specs=[SMEM, SMEM] + [ANY] * npair,
        out_specs=[ANY] * (ncl - 1),
        scratch_shapes=[
            pltpu.VMEM((npair, 2 * HD, wide), BF16),
            pltpu.SemaphoreType.DMA((npair,)),
            pltpu.SemaphoreType.DMA(((ncl - 1) * cap,)),
        ],
        compiler_params=params(40),
        cost_estimate=cost(0, 4 * npair * 2 * HD * wide),
        name="select",
    )(meta, asked, *tables)


def query_matrix(heads_dev, q, per, b):
    lane = pl.multiple_of(lax.rem(b, per) * BLK, BLK)
    x = q[b // per, :, pl.ds(lane, BLK)] * jnp.asarray(HD**-0.5, BF16)
    zero = jnp.zeros((HD, BLK), BF16)
    if heads_dev == 1:
        return jnp.concatenate([x, zero], axis=0)
    left = jnp.concatenate([x[:HD], zero], axis=0)
    right = jnp.concatenate([zero, x[HD:]], axis=0)
    return jnp.concatenate([left, right], axis=1)


def near_attention(heads_dev, npair, meta, ids, first_kv, rest):
    wide = rest[0].shape[1]
    per = wide // BLK
    nblk = npair * per
    feats = heads_dev * HD
    low_q = (heads_dev - 1) * 2 * HD
    cols = heads_dev * BLK
    keys = NEAR * BLK

    def body(meta_ref, ids_ref, *refs):
        tabs = refs[:npair]
        rests = refs[npair : 2 * npair]
        out_ref, stat_ref, kv, q, ktab, vtab, s_a, s_b, sems = refs[2 * npair :]
        pair = meta_ref[0]
        loads = []
        for j in range(npair):
            at = pair ^ j
            loads.append(pltpu.make_async_copy(tabs[j], kv.at[0, at], sems.at[j]))
            for h in range(1, heads_dev):
                loads.append(
                    pltpu.make_async_copy(
                        rests[j].at[pl.ds((h - 1) * 2 * HD, 2 * HD)], kv.at[h, at], sems.at[h * npair + j]
                    )
                )
            loads.append(
                pltpu.make_async_copy(
                    rests[j].at[pl.ds(low_q, feats)], q.at[at], sems.at[heads_dev * npair + j]
                )
            )
        for load in loads:
            load.start()
        for load in loads:
            load.wait()

        def build(p, carry):
            for i in range(per):
                at = slice(i * BLK, (i + 1) * BLK)
                pieces = [kv[h, p, :, at] for h in range(heads_dev)]
                if heads_dev == 1:
                    ktab[p * per + i] = pieces[0].T
                else:
                    ktab[p * per + i] = jnp.concatenate([x[:HD] for x in pieces], axis=0).T
                vtab[p * per + i] = jnp.concatenate([x[HD:] for x in pieces], axis=0)
            return carry

        lax.fori_loop(0, npair, build, 0)

        def first(b, held):
            qm = query_matrix(heads_dev, q, per, b)
            top = None
            for j in range(NEAR):
                s = jnp.dot(ktab[ids_ref[b * NEAR + j]], qm, preferred_element_type=F32)
                held[j * BLK : (j + 1) * BLK, :] = s
                part = jnp.max(s.reshape(BLK // 8, 8, cols), axis=0)
                top = part if top is None else jnp.maximum(top, part)
            return jnp.max(top, axis=0, keepdims=True)

        def second(b, held, top):
            acc = None
            total = None
            for c in range(0, NEAR, 4):
                p = jnp.exp2((held[c * BLK : (c + 4) * BLK, :] - top) * LOG2E)
                part = jnp.sum(p.reshape(4 * BLK // 8, 8, cols), axis=0)
                total = part if total is None else total + part
                v = jnp.concatenate([vtab[ids_ref[b * NEAR + c + i]] for i in range(4)], axis=1)
                o = jnp.dot(v, p.astype(BF16), preferred_element_type=F32)
                acc = o if acc is None else acc + o
            out_ref[b] = jnp.concatenate(
                [
                    acc[h * HD : (h + 1) * HD, h * BLK : (h + 1) * BLK]
                    for h in range(heads_dev)
                ],
                axis=0,
            )
            stat_ref[b, 0:1, :] = top
            stat_ref[b, 1:2, :] = jnp.sum(total, axis=0, keepdims=True)

        def step(i, top):
            b = 2 * i
            top_b = first(b + 1, s_b)
            second(b, s_a, top)
            top_a = first(jnp.minimum(b + 2, nblk - 1), s_a)
            second(b + 1, s_b, top_b)
            return top_a

        lax.fori_loop(0, nblk // 2, step, first(0, s_a))

    flops = nblk * keys * BLK * feats * 4 * heads_dev
    return pl.pallas_call(
        body,
        out_shape=[
            jax.ShapeDtypeStruct((nblk, feats, BLK), F32),
            jax.ShapeDtypeStruct((nblk, 8, cols), F32),
        ],
        in_specs=[SMEM, SMEM] + [ANY] * (2 * npair),
        out_specs=[VMEM, VMEM],
        scratch_shapes=[
            pltpu.VMEM((heads_dev, npair, 2 * HD, wide), BF16),
            pltpu.VMEM((npair, feats, wide), BF16),
            pltpu.VMEM((nblk, BLK, 2 * HD), BF16),
            pltpu.VMEM((nblk, feats, BLK), BF16),
            pltpu.VMEM((keys, cols), F32),
            pltpu.VMEM((keys, cols), F32),
            pltpu.SemaphoreType.DMA((npair * (heads_dev + 1),)),
        ],
        compiler_params=params(40),
        cost_estimate=cost(2 * flops, 8 * nblk * BLK * feats, nblk * keys * cols),
        name="near_attention",
    )(meta, ids, *first_kv, *rest)


def far_attention(heads_dev, npair, seq_size, ncl, cap, meta, pos, counts, tables, rest, near, stats):
    wide = rest[0].shape[1]
    per = wide // BLK
    nblk = npair * per
    low_q = (heads_dev - 1) * 2 * HD
    dev_blocks = nblk // seq_size
    feats = heads_dev * HD
    cols = heads_dev * BLK
    keys = REMOTE * BLK
    shifts = ncl - 1

    def body(meta_ref, pos_ref, counts_ref, *refs):
        tabs = refs[: heads_dev * shifts]
        refs = refs[heads_dev * shifts :]
        rests = refs[:npair]
        near_ref, stat_ref = refs[npair : npair + 2]
        outs = refs[npair + 2 : npair + 2 + seq_size]
        kv, q, ktab, vtab, old, s_a, s_b, sems = refs[npair + 2 + seq_size :]
        pair = meta_ref[0]
        cluster = meta_ref[2]
        seq = meta_ref[3]
        loads = []
        for h in range(heads_dev):
            for s in range(shifts):
                origin = lax.rem(cluster + ncl - 1 - s, ncl) * cap
                n = h * shifts + s
                loads.append(pltpu.make_async_copy(tabs[n], kv.at[h, pl.ds(origin, cap)], sems.at[n]))
        for j in range(npair):
            loads.append(
                pltpu.make_async_copy(
                    rests[j].at[pl.ds(low_q, feats)], q.at[pair ^ j], sems.at[heads_dev * shifts + j]
                )
            )
        late = []
        for k in range(seq_size):
            at = pl.ds((seq ^ k) * dev_blocks, dev_blocks)
            late.append(
                pltpu.make_async_copy(near_ref.at[at], old.at[at], sems.at[heads_dev * shifts + npair + k])
            )
        for load in loads + late:
            load.start()
        for load in loads:
            load.wait()

        def build(s, carry):
            origin = lax.rem(cluster + ncl - s, ncl) * cap
            for i in range(cap):
                pieces = [kv[h, origin + i] for h in range(heads_dev)]
                if heads_dev == 1:
                    ktab[origin + i] = pieces[0].T
                else:
                    ktab[origin + i] = jnp.concatenate([x[:HD] for x in pieces], axis=0).T
                vtab[origin + i] = jnp.concatenate([x[HD:] for x in pieces], axis=0)
            return carry

        lax.fori_loop(1, ncl, build, 0)

        def first(b, held):
            qm = query_matrix(heads_dev, q, per, b)
            valid = counts_ref[b] - NEAR
            top = None
            for j in range(REMOTE):
                s = jnp.dot(ktab[pos_ref[b * REMOTE + j]], qm, preferred_element_type=F32)
                if j:
                    s = jnp.where(j < valid, s, -1e30)
                held[j * BLK : (j + 1) * BLK, :] = s
                part = jnp.max(s.reshape(BLK // 8, 8, cols), axis=0)
                top = part if top is None else jnp.maximum(top, part)
            return jnp.max(top, axis=0, keepdims=True)

        def second(b, held, top):
            was = stat_ref[b, 0:1, :]
            top = jnp.maximum(was, top)
            fade = jnp.exp2((was - top) * LOG2E)
            p = jnp.exp2((held[...] - top) * LOG2E)
            part = jnp.sum(p.reshape(keys // 8, 8, cols), axis=0)
            total = stat_ref[b, 1:2, :] * fade + jnp.sum(part, axis=0, keepdims=True)
            v = jnp.concatenate([vtab[pos_ref[b * REMOTE + j]] for j in range(REMOTE)], axis=1)
            acc = jnp.dot(v, p.astype(BF16), preferred_element_type=F32)
            inv = 1.0 / total
            kept = fade * inv
            res = []
            for h in range(heads_dev):
                at, lane = slice(h * HD, (h + 1) * HD), slice(h * BLK, (h + 1) * BLK)
                res.append(acc[at, lane] * inv[:, lane] + old[b, at, :] * kept[:, lane])
            return jnp.concatenate(res, axis=0).astype(BF16)

        steps = [(k, i) for k in range(seq_size) for i in range(dev_blocks)]
        starts = [(seq ^ k) * dev_blocks + i for k, i in steps]
        helds = (s_a, s_b)
        top = first(starts[0], s_a)
        for n, (k, i) in enumerate(steps):
            if i == 0:
                late[k].wait()
            ahead = first(starts[n + 1], helds[(n + 1) % 2]) if n + 1 < len(steps) else None
            outs[k][:, i * BLK : (i + 1) * BLK] = second(starts[n], helds[n % 2], top)
            top = ahead

    flops = nblk * keys * BLK * feats * 4 * heads_dev
    return pl.pallas_call(
        body,
        out_shape=[jax.ShapeDtypeStruct((feats, dev_blocks * BLK), BF16)] * seq_size,
        in_specs=[SMEM, SMEM, SMEM] + [ANY] * (heads_dev * shifts + npair) + [ANY, VMEM],
        out_specs=[VMEM] * seq_size,
        scratch_shapes=[
            pltpu.VMEM((heads_dev, ncl * cap, 2 * HD, BLK), BF16),
            pltpu.VMEM((npair, feats, wide), BF16),
            pltpu.VMEM((ncl * cap, BLK, 2 * HD), BF16),
            pltpu.VMEM((ncl * cap, feats, BLK), BF16),
            pltpu.VMEM((nblk, feats, BLK), F32),
            pltpu.VMEM((keys, cols), F32),
            pltpu.VMEM((keys, cols), F32),
            pltpu.SemaphoreType.DMA((heads_dev * shifts + npair + seq_size,)),
        ],
        compiler_params=params(40),
        cost_estimate=cost(flops, 6 * nblk * BLK * feats, nblk * keys * cols),
        name="far_attention",
    )(meta, pos, counts, *[x for t in tables for x in t], *rest, near, stats)


def project_out(seq_size, meta, pieces, w_out):
    feats, rows = pieces[0].shape
    step = 128

    def body(meta_ref, *refs):
        parts = refs[:seq_size]
        w_ref, out_ref, at, out, sems = refs[seq_size:]
        seq = meta_ref[3]
        loads = []
        for k in range(seq_size):
            row = pl.multiple_of((seq ^ k) * feats, feats)
            loads.append(pltpu.make_async_copy(parts[k], at.at[pl.ds(row, feats)], sems.at[k]))
        for load in loads:
            load.start()
        for load in loads:
            load.wait()
        stores = []
        for n, r in enumerate(range(0, rows, step)):
            out[r : r + step, :] = jnp.dot(
                at[:, r : r + step].T, w_ref[...], preferred_element_type=F32
            ).astype(BF16)
            rows_at = pl.ds(r, step)
            stores.append(pltpu.make_async_copy(out.at[rows_at], out_ref.at[rows_at], sems.at[seq_size + n]))
            stores[-1].start()
        for store in stores:
            store.wait()

    return pl.pallas_call(
        body,
        out_shape=jax.ShapeDtypeStruct((rows, D), BF16),
        in_specs=[SMEM] + [ANY] * seq_size + [VMEM],
        out_specs=ANY,
        scratch_shapes=[
            pltpu.VMEM((HEADS * HD, rows), BF16),
            pltpu.VMEM((rows, D), BF16),
            pltpu.SemaphoreType.DMA((seq_size + rows // step,)),
        ],
        compiler_params=params(40),
        cost_estimate=cost(2 * rows * D * D, 2 * D * D + 4 * rows * D),
        name="project_out",
    )(meta, *pieces, w_out)


def shifted(x, axis, size, shift):
    return lax.ppermute(x, axis, [(i, (i + shift) % size) for i in range(size)])


def crossed(x, size, k):
    return lax.ppermute(x, "seq", [(i, i ^ k) for i in range(size)])


def wanted_blocks(kv_ids, counts, ncl, nblk):
    cap = nblk // 4
    remote_ids = kv_ids[:, NEAR:]
    valid = jnp.arange(NEAR, KVB, dtype=jnp.int32)[None, :] < counts[:, None]
    every = jnp.arange(ncl * nblk, dtype=jnp.int32)
    present = jnp.any(
        (remote_ids.reshape(-1)[:, None] == every[None, :]) & valid.reshape(-1)[:, None], axis=0
    )
    present = present.astype(jnp.int32).reshape(ncl, nblk)
    rank = jnp.cumsum(present, axis=1) - 1
    chosen = (rank[:, None, :] == jnp.arange(cap, dtype=jnp.int32)[None, :, None]) & (
        present[:, None, :] > 0
    )
    wanted = jnp.sum(jnp.where(chosen, jnp.arange(nblk, dtype=jnp.int32)[None, None, :], 0), axis=2)
    place = (remote_ids // nblk) * cap + jnp.sum(
        jnp.where(remote_ids[:, :, None] == every[None, None, :], rank.reshape(-1)[None, None, :], 0),
        axis=2,
    )
    return jnp.pad(wanted[:, None, :], ((0, 0), (0, 7), (0, 128 - cap))), jnp.where(valid, place, place[:, :1]).reshape(-1)


def on_device(nodes, w_qkv, w_out, kv_ids, counts):
    seq_size = lax.axis_size("seq")
    ncl = lax.axis_size("cluster")
    heads_dev = HEADS // seq_size
    npair = seq_size // 2
    nblk = seq_size * nodes.shape[0] // BLK
    cap = nblk // 4
    seq = lax.axis_index("seq")
    cluster = lax.axis_index("cluster")
    meta = jnp.stack([seq // 2, seq % 2, cluster, seq]).astype(jnp.int32)

    other = crossed(nodes, seq_size, 1)
    wanted, pos = wanted_blocks(kv_ids, counts, ncl, nblk)
    wanted, own = lax.optimization_barrier((wanted, nodes))

    q_span = [(3 * h * HD, HD) for h in range(heads_dev)]
    spans = [[((3 * h + 1) * HD, 2 * HD)] for h in range(heads_dev)]
    (first_kv,) = project(spans[:1], heads_dev, npair, meta, own, other, w_qkv)
    (rest,) = project([sum(spans[1:] + [q_span], [])], heads_dev, npair, meta, nodes, other, w_qkv)
    wanted, rest = lax.optimization_barrier((wanted, rest))
    asked = lax.all_to_all(wanted, "cluster", split_axis=0, concat_axis=0, tiled=True)
    first_kv = [x if j == 0 else crossed(x, seq_size, 2 * j) for j, x in enumerate(first_kv)]
    rest = [x if j == 0 else crossed(x, seq_size, 2 * j) for j, x in enumerate(rest)]
    far = []
    for h in range(heads_dev):
        tables, row = (first_kv, 0) if h == 0 else (rest, (h - 1) * 2 * HD)
        picked = select(npair, ncl, cap, meta, asked, tables, row)
        far.append([shifted(x, "cluster", ncl, s + 1) for s, x in enumerate(picked)])
    near_ids = (kv_ids[:, :NEAR] - cluster * nblk).reshape(-1)
    near, stats = near_attention(heads_dev, npair, meta, near_ids, first_kv, rest)
    outs = far_attention(
        heads_dev, npair, seq_size, ncl, cap, meta, pos, counts, far, rest, near, stats
    )
    pieces = [x if k == 0 else crossed(x, seq_size, k) for k, x in enumerate(outs)]
    return project_out(seq_size, meta, pieces, w_out)


def solution(mesh):
    placed = (P(("cluster", "seq"), None), P(), P(), P("cluster", None), P("cluster"))
    return jax.shard_map(
        on_device,
        mesh=mesh,
        in_specs=placed,
        out_specs=P(("cluster", "seq"), None),
        check_vma=False,
    )
```

time: 129 us -> 112 us (0.87)
  starting transfers between devices: 41.5 us -> 31.4 us
  Pallas kernels: 56.4 us -> 48.8 us
  local copies, waits for them, and re-layouts: 9.38 us -> 5.7 us
  waiting for transfers between devices: 17.8 us -> 21.1 us
    ppermute x24 -> x14, starting transfers between devices: 25.4 us -> 13.6 us  [crossed(): return lax.ppermute(x, 'seq', [(i, i ^ k) for i in range(size)])]
    pallas_call x2 -> x1, Pallas kernels: 19.4 us -> 9.5 us  [far_attention(): pl.pallas_call(body, out_shape=[jax.ShapeDtypeStruct((feats, dev_blocks *...]
    unnamed x20 -> x18, local copies, waits for them, and re-layouts: 7.08 us -> 3.43 us
    pallas_call x2, Pallas kernels: 9.71 us -> 12 us  [project(): pl.pallas_call(body, out_shape=shapes, in_specs=[SMEM, ANY, ANY, ANY], ou...]
    ppermute x6, starting transfers between devices: 10.2 us -> 12.5 us  [shifted(): return lax.ppermute(x, axis, [(i, (i + shift) % size) for i in range(size)])]
    ppermute x24 -> x14, waiting for transfers between devices: 17.8 us -> 19.7 us  [crossed(): return lax.ppermute(x, 'seq', [(i, i ^ k) for i in range(size)])]
    all_to_all x1, waiting for transfers between devices: 0.01 us -> 1.42 us  [on_device(): lax.all_to_all(wanted, 'cluster', split_axis=0, concat_axis=0, tiled=True)]
  transfers between devices with their start and end apart: 31 -> 21, of which waited for: 7 -> 6; matrix products, arithmetic and copies ran while one was open for 4% -> 5% of each run, Pallas kernels for 40% -> 27%
where the time goes in v2:
time: 112 us; the launch traced here: 111 us
  Pallas kernels  48.8 us (44%)
  starting transfers between devices  31.4 us (28%)
  waiting for transfers between devices  21.1 us (19%)
  local copies, waits for them, and re-layouts  5.7 us (5%)
  other arithmetic  3.52 us (3%)
    pallas_call x1, Pallas kernels, near_attention(): pl.pallas_call(body, out_shape=[jax.ShapeDtypeStruct((nblk, feats, BLK),...  19.8 us
    ppermute x14, waiting for transfers between devices, crossed(): return lax.ppermute(x, 'seq', [(i, i ^ k) for i in range(size)])  19.7 us
    ppermute x14, starting transfers between devices, crossed(): return lax.ppermute(x, 'seq', [(i, i ^ k) for i in range(size)])  13.6 us
    ppermute x6, starting transfers between devices, shifted(): return lax.ppermute(x, axis, [(i, (i + shift) % size) for i in range(size)])  12.5 us
    pallas_call x2, Pallas kernels, project(): pl.pallas_call(body, out_shape=shapes, in_specs=[SMEM, ANY, ANY, ANY], ou...  12 us
    pallas_call x1, Pallas kernels, far_attention(): pl.pallas_call(body, out_shape=[jax.ShapeDtypeStruct((feats, dev_blocks *...  9.5 us
    all_to_all x1, starting transfers between devices, on_device(): lax.all_to_all(wanted, 'cluster', split_axis=0, concat_axis=0, tiled=True)  5.29 us
    pallas_call x1, Pallas kernels, project_out(): pl.pallas_call(body, out_shape=jax.ShapeDtypeStruct((rows, D), BF16), in_...  4.02 us
  transfers between devices with their start and end apart: 21, of which 6 were waited for; matrix products, arithmetic and copies ran while one was open for 5% of the time, Pallas kernels for 27%

profile of v2, /device:TPU:0, one launch (start us, length us, event | category | flops | bytes accessed | tf_op | source)
XLA Modules:
  0.0 110.8 jit_solution(6678130347248342464)
XLA Ops:
  0.0 0.5 collective-permute-start
  0.5 0.7 broadcast_compare_fusion.1
  1.2 0.7 slice.9
  1.9 0.1 copy.18
  2.0 0.1 lt.30
  2.1 0.1 copy.17
  2.2 0.1 eq.46
  2.3 0.1 fusion.1
  2.4 0.1 reshape.52
  2.5 0.2 reduce_window_sum.11
  2.7 0.1 sub.25
  2.8 0.2 select_reduce_fusion.1
  3.0 0.6 pad.4
  3.6 0.6 pad_add_fusion.meta_ref
  4.2 0.7 slice_subtract_fusion
  4.9 0.0 collective-permute-done.other_ref
  4.9 1.0 copy-done.8
  5.9 5.1 %project.3 = (bf16[128,1024]{1,0:T(8,128)(2,1)}, bf16[128,1024]{1,0:T(8,128)(2,1)}, bf16[128,1024]{1,0:T(8,128)(2,1)}, bf16[128,1024]{1,0:T(8,128)(2,1)}) custom-call(s32[4]{0:T(128)} %pad_add_fusion.meta_ref, bf16[512,1024]{1,0:T(8,128)(2,1)} %own_ref.2, bf16[512,1024]{1,0:T(8,128)(2,1)} %copy-done.8, bf16[1024,3072]{1,0:T(8,128)(2,1)} %w_ref.3), custom_call_target="tpu_custom_call" | custom-call | flops 1073741824 | bytes 4194304 | tf_op jit(solution)/shard_map/project/pallas_call | solution.py:93
  11.0 2.6 %collective-permute-start.1 = (bf16[128,1024]{1,0:T(8,128)(2,1)}, bf16[128,1024]{1,0:T(8,128)(2,1)S(1)}, u32[]{:S(2)}, u32[]{:S(2)}) collective-permute-start(bf16[128,1024]{1,0:T(8,128)(2,1)} %get-tuple-element.44), channel_id=1, source_target_pairs={{0,2},{1,3},{2,0},{3,1},{4,6},{5,7},{6,4},{7,5},{8,10},{9,11},{10,... | collective-permute-start | bytes 786440 | tf_op jit(solution)/shard_map/ppermute | solution.py:455
  13.5 0.2 select_reduce_fusion
  13.7 1.6 %collective-permute-start.2 = (bf16[128,1024]{1,0:T(8,128)(2,1)}, bf16[128,1024]{1,0:T(8,128)(2,1)S(1)}, u32[]{:S(2)}, u32[]{:S(2)}) collective-permute-start(bf16[128,1024]{1,0:T(8,128)(2,1)} %get-tuple-element.45), channel_id=1, source_target_pairs={{0,4},{1,5},{2,6},{3,7},{4,0},{5,1},{6,2},{7,3},{8,12},{9,13},{10,... | collective-permute-start | bytes 786440 | tf_op jit(solution)/shard_map/ppermute | solution.py:455
  15.3 0.1 collective-permute-start.3
  15.4 6.9 %project.2 = (bf16[256,1024]{1,0:T(8,128)(2,1)}, bf16[256,1024]{1,0:T(8,128)(2,1)}, bf16[256,1024]{1,0:T(8,128)(2,1)}, bf16[256,1024]{1,0:T(8,128)(2,1)}) custom-call(s32[4]{0:T(128)} %pad_add_fusion.meta_ref, bf16[512,1024]{1,0:T(8,128)(2,1)} %own_ref.2, bf16[512,1024]{1,0:T(8,128)(2,1)} %copy-done.8, bf16[1024,3072]{1,0:T(8,128)(2,1)} %w_ref.3), custom_call_target="tpu_custom_call" | custom-call | flops 2147483648 | bytes 5242880 | tf_op jit(solution)/shard_map/project/pallas_call | solution.py:93
  22.3 5.3 %all-to-all-start = ((s32[4,8,128]{2,1,0:T(8,128)}), s32[4,8,128]{2,1,0:T(8,128)S(1)}, u32[]{:S(2)}, u32[]{:S(2)}) async-start(s32[4,8,128]{2,1,0:T(8,128)} %pad.4), calls=%async_computation | async-start | bytes 32768 | tf_op jit(solution)/shard_map/all_to_all | solution.py:499
  27.6 1.5 %collective-permute-start.7 = (bf16[256,1024]{1,0:T(8,128)(2,1)}, bf16[256,1024]{1,0:T(8,128)(2,1)S(1)}, u32[]{:S(2)}, u32[]{:S(2)}) collective-permute-start(bf16[256,1024]{1,0:T(8,128)(2,1)} %get-tuple-element.51), channel_id=1, source_target_pairs={{0,2},{1,3},{2,0},{3,1},{4,6},{5,7},{6,4},{7,5},{8,10},{9,11},{10,... | collective-permute-start | bytes 1572872 | tf_op jit(solution)/shard_map/ppermute | solution.py:455
  29.1 1.5 %collective-permute-start.8 = (bf16[256,1024]{1,0:T(8,128)(2,1)}, bf16[256,1024]{1,0:T(8,128)(2,1)S(1)}, u32[]{:S(2)}, u32[]{:S(2)}) collective-permute-start(bf16[256,1024]{1,0:T(8,128)(2,1)} %get-tuple-element.52), channel_id=1, source_target_pairs={{0,4},{1,5},{2,6},{3,7},{4,0},{5,1},{6,2},{7,3},{8,12},{9,13},{10,... | collective-permute-start | bytes 1572872 | tf_op jit(solution)/shard_map/ppermute | solution.py:455
  30.6 0.5 collective-permute-start.9
  31.1 0.7 fusion.5
  31.8 1.4 %all-to-all-done.asked_ref = s32[4,8,128]{2,1,0:T(8,128)S(1)} async-done(((s32[4,8,128]{2,1,0:T(8,128)}), s32[4,8,128]{2,1,0:T(8,128)S(1)}, u32[]{:S(2)}, u32[]{:S(2)}) %all-to-all-start) | async-done | bytes 16416 | tf_op jit(solution)/shard_map/all_to_all | solution.py:499
  33.2 1.9 %select.13 = (bf16[8,128,128]{2,1,0:T(8,128)(2,1)}, bf16[8,128,128]{2,1,0:T(8,128)(2,1)S(1)}, bf16[8,128,128]{2,1,0:T(8,128)(2,1)S(1)}) custom-call(s32[4]{0:T(128)S(1)} %copy-done.4, s32[4,8,128]{2,1,0:T(8,128)S(1)} %all-to-all-done.asked_ref, bf16[128,1024]{1,0:T(8,128)(2,1)S(1)} %copy-done.3, bf16[128,1024]{1,0:T(8,128)(2,1)S(1)} %collective-permute-done.1.refs_1_, ...), custom_call_target="tpu_custom_call" | custom-call | bytes 2097152 | tf_op jit(solution)/shard_map/select/pallas_call | solution.py:149
  35.2 0.7 copy-done.6
  35.8 0.7 copy-done.7
  36.5 0.7 collective-permute-start.4
  37.2 0.1 copy.21
  37.3 0.1 reshape.51.ids_ref
  37.4 0.1 broadcast_select_fusion
  37.5 0.1 copy.19
  37.6 0.1 reshape.50.pos_ref
  37.7 2.4 %collective-permute-start.5 = (bf16[8,128,128]{2,1,0:T(8,128)(2,1)}, bf16[8,128,128]{2,1,0:T(8,128)(2,1)S(1)}, u32[]{:S(2)}, u32[]{:S(2)}) collective-permute-start(bf16[8,128,128]{2,1,0:T(8,128)(2,1)} %copy-done.7), channel_id=1, source_target_pairs={{0,16},{8,24},{16,0},{24,8},{1,17},{9,25},{17,1},{25,9},{2,18},{10... | collective-permute-start | bytes 786440 | tf_op jit(solution)/shard_map/ppermute | solution.py:451
  40.1 2.6 %collective-permute-done.7.refs_1_.refs_5_.refs_7_ = bf16[256,1024]{1,0:T(8,128)(2,1)S(1)} collective-permute-done((bf16[256,1024]{1,0:T(8,128)(2,1)}, bf16[256,1024]{1,0:T(8,128)(2,1)S(1)}, u32[]{:S(2)}, u32[]{:S(2)}) %collective-permute-start.7) | collective-permute-done | bytes 524320 | tf_op jit(solution)/shard_map/ppermute | solution.py:455
  42.7 3.8 %collective-permute-start.6 = (bf16[8,128,128]{2,1,0:T(8,128)(2,1)}, bf16[8,128,128]{2,1,0:T(8,128)(2,1)S(1)}, u32[]{:S(2)}, u32[]{:S(2)}) collective-permute-start(bf16[8,128,128]{2,1,0:T(8,128)(2,1)} %copy-done.6), channel_id=1, source_target_pairs={{0,24},{8,0},{16,8},{24,16},{1,25},{9,1},{17,9},{25,17},{2,26},{10... | collective-permute-start | bytes 786440 | tf_op jit(solution)/shard_map/ppermute | solution.py:451
  46.5 7.0 %collective-permute-done.8.refs_2_.refs_6_.refs_8_ = bf16[256,1024]{1,0:T(8,128)(2,1)S(1)} collective-permute-done((bf16[256,1024]{1,0:T(8,128)(2,1)}, bf16[256,1024]{1,0:T(8,128)(2,1)S(1)}, u32[]{:S(2)}, u32[]{:S(2)}) %collective-permute-start.8) | collective-permute-done | bytes 524320 | tf_op jit(solution)/shard_map/ppermute | solution.py:455
  53.5 0.0 collective-permute-done.9.refs_3_.refs_7_.refs_9_
  53.5 1.0 copy-done.1
  54.5 1.6 %select.14 = (bf16[8,128,128]{2,1,0:T(8,128)(2,1)S(1)}, bf16[8,128,128]{2,1,0:T(8,128)(2,1)S(1)}, bf16[8,128,128]{2,1,0:T(8,128)(2,1)S(1)}) custom-call(s32[4]{0:T(128)S(1)} %copy-done.4, s32[4,8,128]{2,1,0:T(8,128)S(1)} %all-to-all-done.asked_ref, bf16[256,1024]{1,0:T(8,128)(2,1)S(1)} %copy-done.1, ...), custom_call_target="tpu_custom_call" | custom-call | bytes 2097152 | tf_op jit(solution)/shard_map/select/pallas_call | solution.py:149
  56.1 1.8 %collective-permute-start.10 = (bf16[8,128,128]{2,1,0:T(8,128)(2,1)S(1)}, bf16[8,128,128]{2,1,0:T(8,128)(2,1)S(1)}, u32[]{:S(2)}, u32[]{:S(2)}) collective-permute-start(bf16[8,128,128]{2,1,0:T(8,128)(2,1)S(1)} %get-tuple-element.54), channel_id=1, source_target_pairs={{0,8},{8,16},{16,24},{24,0},{1,9},{9,17},{17,25},{25,1},{2,10},{10... | collective-permute-start | bytes 786440 | tf_op jit(solution)/shard_map/ppermute | solution.py:451
  57.9 2.4 %collective-permute-start.11 = (bf16[8,128,128]{2,1,0:T(8,128)(2,1)S(1)}, bf16[8,128,128]{2,1,0:T(8,128)(2,1)S(1)}, u32[]{:S(2)}, u32[]{:S(2)}) collective-permute-start(bf16[8,128,128]{2,1,0:T(8,128)(2,1)S(1)} %get-tuple-element.55), channel_id=1, source_target_pairs={{0,16},{8,24},{16,0},{24,8},{1,17},{9,25},{17,1},{25,9},{2,18},{10... | collective-permute-start | bytes 786440 | tf_op jit(solution)/shard_map/ppermute | solution.py:451
  60.3 0.0 collective-permute-done.4.refs_0_
  60.3 1.5 %collective-permute-start.12 = (bf16[8,128,128]{2,1,0:T(8,128)(2,1)S(1)}, bf16[8,128,128]{2,1,0:T(8,128)(2,1)S(1)}, u32[]{:S(2)}, u32[]{:S(2)}) collective-permute-start(bf16[8,128,128]{2,1,0:T(8,128)(2,1)S(1)} %get-tuple-element.56), channel_id=1, source_target_pairs={{0,24},{8,0},{16,8},{24,16},{1,25},{9,1},{17,9},{25,17},{2,26},{10... | collective-permute-start | bytes 786440 | tf_op jit(solution)/shard_map/ppermute | solution.py:451
  61.8 19.8 %near_attention.1 = (f32[32,128,128]{2,1,0:T(8,128)S(1)}, f32[32,8,256]{2,1,0:T(8,128)S(1)}) custom-call(s32[4]{0:T(128)S(1)} %copy-done.4, s32[384]{0:T(512)S(1)} %reshape.51.ids_ref, bf16[128,1024]{1,0:T(8,128)(2,1)S(1)} %copy-done.3, bf16[128,1024]{1,0:T(8,128)(2,1)S(1)} %collective-permute-done.1.refs_1_, ...), custom_call_target="tpu_custom_call" | custom-call | flops 12884901888 | bytes 4194304 | tf_op jit(solution)/shard_map/near_attention/pallas_call | solution.py:264
  81.5 0.0 collective-permute-done.5.refs_1_
  81.6 0.0 copy-start
  81.6 9.5 %far_attention.1 = (bf16[128,512]{1,0:T(8,128)(2,1)S(1)}, bf16[128,512]{1,0:T(8,128)(2,1)S(1)}, bf16[128,512]{1,0:T(8,128)(2,1)S(1)}, bf16[128,512]{1,0:T(8,128)...) custom-call(s32[4]{0:T(128)S(1)} %copy-done.4, ...), custom_call_target="tpu_custom_call" | custom-call | flops 2147483648 | bytes 3145728 | tf_op jit(solution)/shard_map/far_attention/pallas_call | solution.py:386
  91.1 0.1 collective-permute-start.13
  91.2 1.3 %collective-permute-start.14 = (bf16[128,512]{1,0:T(8,128)(2,1)S(1)}, bf16[128,512]{1,0:T(8,128)(2,1)S(1)}, u32[]{:S(2)}, u32[]{:S(2)}) collective-permute-start(bf16[128,512]{1,0:T(8,128)(2,1)S(1)} %get-tuple-element.61), channel_id=1, source_target_pairs={{0,2},{1,3},{2,0},{3,1},{4,6},{5,7},{6,4},{7,5},{8,10},{9,11},{10,... | collective-permute-start | bytes 393224 | tf_op jit(solution)/shard_map/ppermute | solution.py:455
  92.5 0.6 collective-permute-start.15
  93.1 1.5 %collective-permute-start.16 = (bf16[128,512]{1,0:T(8,128)(2,1)S(1)}, bf16[128,512]{1,0:T(8,128)(2,1)S(1)}, u32[]{:S(2)}, u32[]{:S(2)}) collective-permute-start(bf16[128,512]{1,0:T(8,128)(2,1)S(1)} %get-tuple-element.63), channel_id=1, source_target_pairs={{0,4},{1,5},{2,6},{3,7},{4,0},{5,1},{6,2},{7,3},{8,12},{9,13},{10,... | collective-permute-start | bytes 393224 | tf_op jit(solution)/shard_map/ppermute | solution.py:455
  94.6 0.2 collective-permute-start.17
  94.8 1.5 %collective-permute-start.18 = (bf16[128,512]{1,0:T(8,128)(2,1)S(1)}, bf16[128,512]{1,0:T(8,128)(2,1)S(1)}, u32[]{:S(2)}, u32[]{:S(2)}) collective-permute-start(bf16[128,512]{1,0:T(8,128)(2,1)S(1)} %get-tuple-element.65), channel_id=1, source_target_pairs={{0,6},{1,7},{2,4},{3,5},{4,2},{5,3},{6,0},{7,1},{8,14},{9,15},{10,... | collective-permute-start | bytes 393224 | tf_op jit(solution)/shard_map/ppermute | solution.py:455
  96.2 1.3 %collective-permute-done.14.refs_2_ = bf16[128,512]{1,0:T(8,128)(2,1)S(1)} collective-permute-done((bf16[128,512]{1,0:T(8,128)(2,1)S(1)}, bf16[128,512]{1,0:T(8,128)(2,1)S(1)}, u32[]{:S(2)}, u32[]{:S(2)}) %collective-permute-start.14) | collective-permute-done | bytes 131104 | tf_op jit(solution)/shard_map/ppermute | solution.py:455
  97.6 0.3 collective-permute-start.19
  97.9 1.6 %collective-permute-done.15.refs_3_ = bf16[128,512]{1,0:T(8,128)(2,1)S(1)} collective-permute-done((bf16[128,512]{1,0:T(8,128)(2,1)S(1)}, bf16[128,512]{1,0:T(8,128)(2,1)S(1)}, u32[]{:S(2)}, u32[]{:S(2)}) %collective-permute-start.15) | collective-permute-done | bytes 131104 | tf_op jit(solution)/shard_map/ppermute | solution.py:455
  99.5 7.2 %collective-permute-done.17.refs_5_ = bf16[128,512]{1,0:T(8,128)(2,1)S(1)} collective-permute-done((bf16[128,512]{1,0:T(8,128)(2,1)S(1)}, bf16[128,512]{1,0:T(8,128)(2,1)S(1)}, u32[]{:S(2)}, u32[]{:S(2)}) %collective-permute-start.17) | collective-permute-done | bytes 131104 | tf_op jit(solution)/shard_map/ppermute | solution.py:455
  106.7 4.0 %project_out.1 = bf16[512,1024]{1,0:T(8,128)(2,1)} custom-call(s32[4]{0:T(128)S(1)} %copy-done.4, bf16[128,512]{1,0:T(8,128)(2,1)S(1)} %get-tuple-element.59.refs_0_, bf16[128,512]{1,0:T(8,128)(2,1)S(1)} %collective-permute-done.13.refs_1_, bf16[128,512]{1,0:T(8,128)(2,1)S(1)} %collective-permute-done.14.refs_2_, ...), custom_call_target="tpu_custom_call" | custom-call | flops 1073741824 | bytes 4194304 | tf_op jit(solution)/shard_map/project_out/pallas_call | solution.py:434
  (29 shorter events, 0.1 us)
Async XLA Ops:
  0.0 4.9 %collective-permute-start = (bf16[512,1024]{1,0:T(8,128)(2,1)}, bf16[512,1024]{1,0:T(8,128)(2,1)S(1)}, u32[]{:S(2)}, u32[]{:S(2)}) collective-permute-start(bf16[512,1024]{1,0:T(8,128)(2,1)} %own_ref.2), channel_id=1, source_target_pairs={{0,1},{1,0},{2,3},{3,2},{4,5},{5,4},{6,7},{7,6},{8,9},{9,8},{10,11... | collective-permute-start | bytes 3145736 | tf_op jit(solution)/shard_map/ppermute | solution.py:455
  4.9 1.0 copy-start.8
  11.0 19.6 %collective-permute-start.1 = (bf16[128,1024]{1,0:T(8,128)(2,1)}, bf16[128,1024]{1,0:T(8,128)(2,1)S(1)}, u32[]{:S(2)}, u32[]{:S(2)}) collective-permute-start(bf16[128,1024]{1,0:T(8,128)(2,1)} %get-tuple-element.44), channel_id=1, source_target_pairs={{0,2},{1,3},{2,0},{3,1},{4,6},{5,7},{6,4},{7,5},{8,10},{9,11},{10,... | collective-permute-start | bytes 786440 | tf_op jit(solution)/shard_map/ppermute | solution.py:455
  13.7 19.5 %collective-permute-start.2 = (bf16[128,1024]{1,0:T(8,128)(2,1)}, bf16[128,1024]{1,0:T(8,128)(2,1)S(1)}, u32[]{:S(2)}, u32[]{:S(2)}) collective-permute-start(bf16[128,1024]{1,0:T(8,128)(2,1)} %get-tuple-element.45), channel_id=1, source_target_pairs={{0,4},{1,5},{2,6},{3,7},{4,0},{5,1},{6,2},{7,3},{8,12},{9,13},{10,... | collective-permute-start | bytes 786440 | tf_op jit(solution)/shard_map/ppermute | solution.py:455
  15.3 17.9 %copy-start.3 = (bf16[128,1024]{1,0:T(8,128)(2,1)S(1)}, bf16[128,1024]{1,0:T(8,128)(2,1)}, u32[]{:S(2)}) copy-start(bf16[128,1024]{1,0:T(8,128)(2,1)} %get-tuple-element.43.refs_0_) | copy-start | bytes 786436
  15.3 17.9 %copy-start.4 = (s32[4]{0:T(128)S(1)}, s32[4]{0:T(128)}, u32[]{:S(2)}) copy-start(s32[4]{0:T(128)} %pad_add_fusion.meta_ref) | copy-start | bytes 52
  15.3 22.1 %copy-start.5 = (s32[32]{0:T(128)S(1)}, s32[32]{0:T(128)}, u32[]{:S(2)}) copy-start(s32[32]{0:T(128)} %counts_ref.1) | copy-start | bytes 388
  15.3 17.9 %collective-permute-start.3 = (bf16[128,1024]{1,0:T(8,128)(2,1)}, bf16[128,1024]{1,0:T(8,128)(2,1)S(1)}, u32[]{:S(2)}, u32[]{:S(2)}) collective-permute-start(bf16[128,1024]{1,0:T(8,128)(2,1)} %get-tuple-element.46), channel_id=1, source_target_pairs={{0,6},{1,7},{2,4},{3,5},{4,2},{5,3},{6,0},{7,1},{8,14},{9,15},{10,... | collective-permute-start | bytes 786440 | tf_op jit(solution)/shard_map/ppermute | solution.py:455
  22.3 39.5 %copy-start.2 = (bf16[256,1024]{1,0:T(8,128)(2,1)S(1)}, bf16[256,1024]{1,0:T(8,128)(2,1)}, u32[]{:S(2)}) copy-start(bf16[256,1024]{1,0:T(8,128)(2,1)} %get-tuple-element.50.refs_0_.refs_4_.refs_6_) | copy-start | bytes 1572868
  22.3 10.9 %all-to-all-start = ((s32[4,8,128]{2,1,0:T(8,128)}), s32[4,8,128]{2,1,0:T(8,128)S(1)}, u32[]{:S(2)}, u32[]{:S(2)}) async-start(s32[4,8,128]{2,1,0:T(8,128)} %pad.4), calls=%async_computation | async-start | bytes 32768 | tf_op jit(solution)/shard_map/all_to_all | solution.py:499
  27.6 15.1 %collective-permute-start.7 = (bf16[256,1024]{1,0:T(8,128)(2,1)}, bf16[256,1024]{1,0:T(8,128)(2,1)S(1)}, u32[]{:S(2)}, u32[]{:S(2)}) collective-permute-start(bf16[256,1024]{1,0:T(8,128)(2,1)} %get-tuple-element.51), channel_id=1, source_target_pairs={{0,2},{1,3},{2,0},{3,1},{4,6},{5,7},{6,4},{7,5},{8,10},{9,11},{10,... | collective-permute-start | bytes 1572872 | tf_op jit(solution)/shard_map/ppermute | solution.py:455
  29.1 24.4 %collective-permute-start.8 = (bf16[256,1024]{1,0:T(8,128)(2,1)}, bf16[256,1024]{1,0:T(8,128)(2,1)S(1)}, u32[]{:S(2)}, u32[]{:S(2)}) collective-permute-start(bf16[256,1024]{1,0:T(8,128)(2,1)} %get-tuple-element.52), channel_id=1, source_target_pairs={{0,4},{1,5},{2,6},{3,7},{4,0},{5,1},{6,2},{7,3},{8,12},{9,13},{10,... | collective-permute-start | bytes 1572872 | tf_op jit(solution)/shard_map/ppermute | solution.py:455
  30.6 22.9 %collective-permute-start.9 = (bf16[256,1024]{1,0:T(8,128)(2,1)}, bf16[256,1024]{1,0:T(8,128)(2,1)S(1)}, u32[]{:S(2)}, u32[]{:S(2)}) collective-permute-start(bf16[256,1024]{1,0:T(8,128)(2,1)} %get-tuple-element.53), channel_id=1, source_target_pairs={{0,6},{1,7},{2,4},{3,5},{4,2},{5,3},{6,0},{7,1},{8,14},{9,15},{10,... | collective-permute-start | bytes 1572872 | tf_op jit(solution)/shard_map/ppermute | solution.py:455
  35.1 0.7 copy-start.6
  35.8 0.7 copy-start.7
  36.5 23.8 %collective-permute-start.4 = (bf16[8,128,128]{2,1,0:T(8,128)(2,1)}, bf16[8,128,128]{2,1,0:T(8,128)(2,1)S(1)}, u32[]{:S(2)}, u32[]{:S(2)}) collective-permute-start(bf16[8,128,128]{2,1,0:T(8,128)(2,1)} %get-tuple-element.47), channel_id=1, source_target_pairs={{0,8},{8,16},{16,24},{24,0},{1,9},{9,17},{17,25},{25,1},{2,10},{10... | collective-permute-start | bytes 786440 | tf_op jit(solution)/shard_map/ppermute | solution.py:451
  37.7 43.9 %collective-permute-start.5 = (bf16[8,128,128]{2,1,0:T(8,128)(2,1)}, bf16[8,128,128]{2,1,0:T(8,128)(2,1)S(1)}, u32[]{:S(2)}, u32[]{:S(2)}) collective-permute-start(bf16[8,128,128]{2,1,0:T(8,128)(2,1)} %copy-done.7), channel_id=1, source_target_pairs={{0,16},{8,24},{16,0},{24,8},{1,17},{9,25},{17,1},{25,9},{2,18},{10... | collective-permute-start | bytes 786440 | tf_op jit(solution)/shard_map/ppermute | solution.py:451
  42.7 38.9 %collective-permute-start.6 = (bf16[8,128,128]{2,1,0:T(8,128)(2,1)}, bf16[8,128,128]{2,1,0:T(8,128)(2,1)S(1)}, u32[]{:S(2)}, u32[]{:S(2)}) collective-permute-start(bf16[8,128,128]{2,1,0:T(8,128)(2,1)} %copy-done.6), channel_id=1, source_target_pairs={{0,24},{8,0},{16,8},{24,16},{1,25},{9,1},{17,9},{25,17},{2,26},{10... | collective-permute-start | bytes 786440 | tf_op jit(solution)/shard_map/ppermute | solution.py:451
  53.5 1.0 copy-start.1
  56.1 25.4 %collective-permute-start.10 = (bf16[8,128,128]{2,1,0:T(8,128)(2,1)S(1)}, bf16[8,128,128]{2,1,0:T(8,128)(2,1)S(1)}, u32[]{:S(2)}, u32[]{:S(2)}) collective-permute-start(bf16[8,128,128]{2,1,0:T(8,128)(2,1)S(1)} %get-tuple-element.54), channel_id=1, source_target_pairs={{0,8},{8,16},{16,24},{24,0},{1,9},{9,17},{17,25},{25,1},{2,10},{10... | collective-permute-start | bytes 786440 | tf_op jit(solution)/shard_map/ppermute | solution.py:451
  57.9 23.6 %collective-permute-start.11 = (bf16[8,128,128]{2,1,0:T(8,128)(2,1)S(1)}, bf16[8,128,128]{2,1,0:T(8,128)(2,1)S(1)}, u32[]{:S(2)}, u32[]{:S(2)}) collective-permute-start(bf16[8,128,128]{2,1,0:T(8,128)(2,1)S(1)} %get-tuple-element.55), channel_id=1, source_target_pairs={{0,16},{8,24},{16,0},{24,8},{1,17},{9,25},{17,1},{25,9},{2,18},{10... | collective-permute-start | bytes 786440 | tf_op jit(solution)/shard_map/ppermute | solution.py:451
  60.3 21.3 %collective-permute-start.12 = (bf16[8,128,128]{2,1,0:T(8,128)(2,1)S(1)}, bf16[8,128,128]{2,1,0:T(8,128)(2,1)S(1)}, u32[]{:S(2)}, u32[]{:S(2)}) collective-permute-start(bf16[8,128,128]{2,1,0:T(8,128)(2,1)S(1)} %get-tuple-element.56), channel_id=1, source_target_pairs={{0,24},{8,0},{16,8},{24,16},{1,25},{9,1},{17,9},{25,17},{2,26},{10... | collective-permute-start | bytes 786440 | tf_op jit(solution)/shard_map/ppermute | solution.py:451
  81.6 25.1 %copy-start = (bf16[1024,1024]{1,0:T(8,128)(2,1)S(1)}, bf16[1024,1024]{1,0:T(8,128)(2,1)}, u32[]{:S(2)}) copy-start(bf16[1024,1024]{1,0:T(8,128)(2,1)} %refs_8_.1) | copy-start | bytes 6291460
  91.1 3.6 %collective-permute-start.13 = (bf16[128,512]{1,0:T(8,128)(2,1)S(1)}, bf16[128,512]{1,0:T(8,128)(2,1)S(1)}, u32[]{:S(2)}, u32[]{:S(2)}) collective-permute-start(bf16[128,512]{1,0:T(8,128)(2,1)S(1)} %get-tuple-element.60), channel_id=1, source_target_pairs={{0,1},{1,0},{2,3},{3,2},{4,5},{5,4},{6,7},{7,6},{8,9},{9,8},{10,11... | collective-permute-start | bytes 393224 | tf_op jit(solution)/shard_map/ppermute | solution.py:455
  91.2 6.4 %collective-permute-start.14 = (bf16[128,512]{1,0:T(8,128)(2,1)S(1)}, bf16[128,512]{1,0:T(8,128)(2,1)S(1)}, u32[]{:S(2)}, u32[]{:S(2)}) collective-permute-start(bf16[128,512]{1,0:T(8,128)(2,1)S(1)} %get-tuple-element.61), channel_id=1, source_target_pairs={{0,2},{1,3},{2,0},{3,1},{4,6},{5,7},{6,4},{7,5},{8,10},{9,11},{10,... | collective-permute-start | bytes 393224 | tf_op jit(solution)/shard_map/ppermute | solution.py:455
  92.5 7.0 %collective-permute-start.15 = (bf16[128,512]{1,0:T(8,128)(2,1)S(1)}, bf16[128,512]{1,0:T(8,128)(2,1)S(1)}, u32[]{:S(2)}, u32[]{:S(2)}) collective-permute-start(bf16[128,512]{1,0:T(8,128)(2,1)S(1)} %get-tuple-element.62), channel_id=1, source_target_pairs={{0,3},{1,2},{2,1},{3,0},{4,7},{5,6},{6,5},{7,4},{8,11},{9,10},{10,... | collective-permute-start | bytes 393224 | tf_op jit(solution)/shard_map/ppermute | solution.py:455
  93.1 6.4 %collective-permute-start.16 = (bf16[128,512]{1,0:T(8,128)(2,1)S(1)}, bf16[128,512]{1,0:T(8,128)(2,1)S(1)}, u32[]{:S(2)}, u32[]{:S(2)}) collective-permute-start(bf16[128,512]{1,0:T(8,128)(2,1)S(1)} %get-tuple-element.63), channel_id=1, source_target_pairs={{0,4},{1,5},{2,6},{3,7},{4,0},{5,1},{6,2},{7,3},{8,12},{9,13},{10,... | collective-permute-start | bytes 393224 | tf_op jit(solution)/shard_map/ppermute | solution.py:455
  94.6 12.1 %collective-permute-start.17 = (bf16[128,512]{1,0:T(8,128)(2,1)S(1)}, bf16[128,512]{1,0:T(8,128)(2,1)S(1)}, u32[]{:S(2)}, u32[]{:S(2)}) collective-permute-start(bf16[128,512]{1,0:T(8,128)(2,1)S(1)} %get-tuple-element.64), channel_id=1, source_target_pairs={{0,5},{1,4},{2,7},{3,6},{4,1},{5,0},{6,3},{7,2},{8,13},{9,12},{10,... | collective-permute-start | bytes 393224 | tf_op jit(solution)/shard_map/ppermute | solution.py:455
  94.8 11.9 %collective-permute-start.18 = (bf16[128,512]{1,0:T(8,128)(2,1)S(1)}, bf16[128,512]{1,0:T(8,128)(2,1)S(1)}, u32[]{:S(2)}, u32[]{:S(2)}) collective-permute-start(bf16[128,512]{1,0:T(8,128)(2,1)S(1)} %get-tuple-element.65), channel_id=1, source_target_pairs={{0,6},{1,7},{2,4},{3,5},{4,2},{5,3},{6,0},{7,1},{8,14},{9,15},{10,... | collective-permute-start | bytes 393224 | tf_op jit(solution)/shard_map/ppermute | solution.py:455
  97.6 9.1 %collective-permute-start.19 = (bf16[128,512]{1,0:T(8,128)(2,1)S(1)}, bf16[128,512]{1,0:T(8,128)(2,1)S(1)}, u32[]{:S(2)}, u32[]{:S(2)}) collective-permute-start(bf16[128,512]{1,0:T(8,128)(2,1)S(1)} %get-tuple-element.66), channel_id=1, source_target_pairs={{0,7},{1,6},{2,5},{3,4},{4,3},{5,2},{6,1},{7,0},{8,15},{9,14},{10,... | collective-permute-start | bytes 393224 | tf_op jit(solution)/shard_map/ppermute | solution.py:455

commit v3 on v2

--- a/solution.py
+++ b/solution.py
@@ -12,6 +12,8 @@
 KVB = 16
 REMOTE = 4
 NEAR = KVB - REMOTE
+NEAR_UNROLL = 4
+FAR_UNROLL = 8
 LOG2E = 1.4426950408889634
 F32 = jnp.float32
 BF16 = jnp.bfloat16
@@ -45,7 +47,7 @@
 
     def body(meta_ref, own_ref, other_ref, w_ref, *refs):
         outs = refs[: len(parts) * npair]
-        x, w, wt, turned, sems = refs[len(parts) * npair :]
+        x, w, wt, turned, made, sems = refs[len(parts) * npair :]
         pair = meta_ref[0]
         core = meta_ref[1]
         loads = []
@@ -78,31 +80,44 @@
                     else:
                         wt[at : at + n, :] = full[s : s + n, :]
                     at += n
-        loads[npair].wait()
-        loads[npair + 1].wait()
         step = 256
-        for r in range(0, 2 * rows, step):
-            res = nt_dot(wt[...], x[r : r + step, :]).astype(BF16)
-            for j in range(npair):
-                at = j * total
-                for k in range(len(parts)):
-                    outs[k * npair + j][:, r : r + step] = res[at : at + heights[k], :]
-                    at += heights[k]
+        stores = []
+        for half in range(2):
+            loads[npair + half].wait()
+            for r in range(0, rows, step):
+                at_rows = pl.multiple_of((here if half == 0 else there) + r, step)
+                res = nt_dot(wt[...], x[pl.ds(at_rows, step), :]).astype(BF16)
+                made[:, half * rows + r : half * rows + r + step] = res
+                for j in range(npair):
+                    at = j * total
+                    for k in range(len(parts)):
+                        stores.append(
+                            pltpu.make_async_copy(
+                                made.at[at : at + heights[k], half * rows + r : half * rows + r + step],
+                                outs[k * npair + j].at[:, pl.ds(at_rows, step)],
+                                sems.at[npair + 2 + len(stores)],
+                            )
+                        )
+                        stores[-1].start()
+                        at += heights[k]
+        for store in stores:
+            store.wait()
 
     shapes = [jax.ShapeDtypeStruct((heights[k], 2 * rows), BF16) for k in range(len(parts)) for _ in range(npair)]
     outs = pl.pallas_call(
         body,
         out_shape=shapes,
         in_specs=[SMEM, ANY, ANY, ANY],
-        out_specs=[VMEM] * len(shapes),
+        out_specs=[ANY] * len(shapes),
         scratch_shapes=[
             pltpu.VMEM((2 * rows, D), BF16),
             pltpu.VMEM((npair, D, width), BF16),
             pltpu.VMEM((npair * total, D), BF16),
             pltpu.VMEM((width, D) if shared else (16, 128), BF16),
-            pltpu.SemaphoreType.DMA((npair + 2,)),
+            pltpu.VMEM((npair * total, 2 * rows), BF16),
+            pltpu.SemaphoreType.DMA((npair + 2 + npair * len(parts) * 2 * rows // 256,)),
         ],
-        compiler_params=params(60),
+        compiler_params=params(55),
         cost_estimate=cost(2 * 2 * rows * D * total * npair, 4 * rows * D + 2 * D * width * npair),
         name="project",
     )(meta, own, other, w_qkv)
@@ -129,9 +144,8 @@
             load.wait()
         sends = []
         for s in range(1, ncl):
-            dest = lax.rem(cluster + s, ncl)
             for i in range(cap):
-                block = asked_ref[dest, 0, i]
+                block = asked_ref[lax.rem(cluster + s, ncl), 0, i]
                 lane = pl.multiple_of(lax.rem(block, per) * BLK, BLK)
                 sends.append(
                     pltpu.make_async_copy(
@@ -185,8 +199,9 @@
     def body(meta_ref, ids_ref, *refs):
         tabs = refs[:npair]
         rests = refs[npair : 2 * npair]
-        out_ref, stat_ref, kv, q, ktab, vtab, s_a, s_b, sems = refs[2 * npair :]
+        out_ref, stat_ref, kv, q, ktab, vtab, s_a, s_b, t_a, t_b, sems = refs[2 * npair :]
         pair = meta_ref[0]
+        base = meta_ref[2] * nblk
         loads = []
         for j in range(npair):
             at = pair ^ j
@@ -220,45 +235,53 @@
 
         lax.fori_loop(0, npair, build, 0)
 
-        def first(b, held):
-            qm = query_matrix(heads_dev, q, per, b)
-            top = None
-            for j in range(NEAR):
-                s = jnp.dot(ktab[ids_ref[b * NEAR + j]], qm, preferred_element_type=F32)
+        def scores(b, qm, held, c, best):
+            for j in range(c, c + 4):
+                s = jnp.dot(ktab[ids_ref[j, b] - base], qm, preferred_element_type=F32)
                 held[j * BLK : (j + 1) * BLK, :] = s
                 part = jnp.max(s.reshape(BLK // 8, 8, cols), axis=0)
-                top = part if top is None else jnp.maximum(top, part)
-            return jnp.max(top, axis=0, keepdims=True)
-
-        def second(b, held, top):
-            acc = None
-            total = None
+                best = part if best is None else jnp.maximum(best, part)
+            return best
+
+        def values(b, held, top, c, acc, total):
+            p = jnp.exp2((held[c * BLK : (c + 4) * BLK, :] - top) * LOG2E)
+            part = jnp.sum(p.reshape(4 * BLK // 8, 8, cols), axis=0)
+            v = jnp.concatenate([vtab[ids_ref[c + i, b] - base] for i in range(4)], axis=1)
+            o = jnp.dot(v, p.astype(BF16), preferred_element_type=F32)
+            return (o, part) if acc is None else (acc + o, total + part)
+
+        def stage(start, held, top_ref, held_after, top_after):
+            for u in range(NEAR_UNROLL):
+                b = start + u
+                after = jnp.minimum(b + NEAR_UNROLL, nblk - 1)
+                qm = query_matrix(heads_dev, q, per, after)
+                top = top_ref[u]
+                acc = total = best = None
+                for c in range(0, NEAR, 4):
+                    best = scores(after, qm, held_after.at[u], c, best)
+                    acc, total = values(b, held.at[u], top, c, acc, total)
+                top_after[u] = jnp.max(best, axis=0, keepdims=True)
+                out_ref[b] = jnp.concatenate(
+                    [acc[h * HD : (h + 1) * HD, h * BLK : (h + 1) * BLK] for h in range(heads_dev)],
+                    axis=0,
+                )
+                stat_ref[b, 0:1, :] = top
+                stat_ref[b, 1:2, :] = jnp.sum(total, axis=0, keepdims=True)
+
+        for u in range(NEAR_UNROLL):
+            qm = query_matrix(heads_dev, q, per, u)
+            best = None
             for c in range(0, NEAR, 4):
-                p = jnp.exp2((held[c * BLK : (c + 4) * BLK, :] - top) * LOG2E)
-                part = jnp.sum(p.reshape(4 * BLK // 8, 8, cols), axis=0)
-                total = part if total is None else total + part
-                v = jnp.concatenate([vtab[ids_ref[b * NEAR + c + i]] for i in range(4)], axis=1)
-                o = jnp.dot(v, p.astype(BF16), preferred_element_type=F32)
-                acc = o if acc is None else acc + o
-            out_ref[b] = jnp.concatenate(
-                [
-                    acc[h * HD : (h + 1) * HD, h * BLK : (h + 1) * BLK]
-                    for h in range(heads_dev)
-                ],
-                axis=0,
-            )
-            stat_ref[b, 0:1, :] = top
-            stat_ref[b, 1:2, :] = jnp.sum(total, axis=0, keepdims=True)
-
-        def step(i, top):
-            b = 2 * i
-            top_b = first(b + 1, s_b)
-            second(b, s_a, top)
-            top_a = first(jnp.minimum(b + 2, nblk - 1), s_a)
-            second(b + 1, s_b, top_b)
-            return top_a
-
-        lax.fori_loop(0, nblk // 2, step, first(0, s_a))
+                best = scores(u, qm, s_a.at[u], c, best)
+            t_a[u] = jnp.max(best, axis=0, keepdims=True)
+
+        def step(n, carry):
+            b = n * NEAR_UNROLL
+            pl.when(lax.rem(n, 2) == 0)(lambda: stage(b, s_a, t_a, s_b, t_b))
+            pl.when(lax.rem(n, 2) == 1)(lambda: stage(b, s_b, t_b, s_a, t_a))
+            return carry
+
+        lax.fori_loop(0, nblk // NEAR_UNROLL, step, 0)
 
     flops = nblk * keys * BLK * feats * 4 * heads_dev
     return pl.pallas_call(
@@ -274,8 +297,10 @@
             pltpu.VMEM((npair, feats, wide), BF16),
             pltpu.VMEM((nblk, BLK, 2 * HD), BF16),
             pltpu.VMEM((nblk, feats, BLK), BF16),
-            pltpu.VMEM((keys, cols), F32),
-            pltpu.VMEM((keys, cols), F32),
+            pltpu.VMEM((NEAR_UNROLL, keys, cols), F32),
+            pltpu.VMEM((NEAR_UNROLL, keys, cols), F32),
+            pltpu.VMEM((NEAR_UNROLL, 1, cols), F32),
+            pltpu.VMEM((NEAR_UNROLL, 1, cols), F32),
             pltpu.SemaphoreType.DMA((npair * (heads_dev + 1),)),
         ],
         compiler_params=params(40),
@@ -301,7 +326,7 @@
         rests = refs[:npair]
         near_ref, stat_ref = refs[npair : npair + 2]
         outs = refs[npair + 2 : npair + 2 + seq_size]
-        kv, q, ktab, vtab, old, s_a, s_b, sems = refs[npair + 2 + seq_size :]
+        kv, q, ktab, vtab, old, s_a, s_b, t_a, t_b, att, sems = refs[npair + 2 + seq_size :]
         pair = meta_ref[0]
         cluster = meta_ref[2]
         seq = meta_ref[3]
@@ -341,46 +366,70 @@
 
         lax.fori_loop(1, ncl, build, 0)
 
-        def first(b, held):
-            qm = query_matrix(heads_dev, q, per, b)
+        for load in late:
+            load.wait()
+
+        def block_of(n):
+            return (seq ^ (n // dev_blocks)) * dev_blocks + lax.rem(n, dev_blocks)
+
+        def scores(b, qm, held, c, best):
             valid = counts_ref[b] - NEAR
-            top = None
-            for j in range(REMOTE):
-                s = jnp.dot(ktab[pos_ref[b * REMOTE + j]], qm, preferred_element_type=F32)
+            for j in range(c, c + 4):
+                s = jnp.dot(ktab[pos_ref[j, b]], qm, preferred_element_type=F32)
                 if j:
                     s = jnp.where(j < valid, s, -1e30)
                 held[j * BLK : (j + 1) * BLK, :] = s
                 part = jnp.max(s.reshape(BLK // 8, 8, cols), axis=0)
-                top = part if top is None else jnp.maximum(top, part)
-            return jnp.max(top, axis=0, keepdims=True)
-
-        def second(b, held, top):
-            was = stat_ref[b, 0:1, :]
-            top = jnp.maximum(was, top)
-            fade = jnp.exp2((was - top) * LOG2E)
-            p = jnp.exp2((held[...] - top) * LOG2E)
-            part = jnp.sum(p.reshape(keys // 8, 8, cols), axis=0)
-            total = stat_ref[b, 1:2, :] * fade + jnp.sum(part, axis=0, keepdims=True)
-            v = jnp.concatenate([vtab[pos_ref[b * REMOTE + j]] for j in range(REMOTE)], axis=1)
-            acc = jnp.dot(v, p.astype(BF16), preferred_element_type=F32)
-            inv = 1.0 / total
-            kept = fade * inv
-            res = []
-            for h in range(heads_dev):
-                at, lane = slice(h * HD, (h + 1) * HD), slice(h * BLK, (h + 1) * BLK)
-                res.append(acc[at, lane] * inv[:, lane] + old[b, at, :] * kept[:, lane])
-            return jnp.concatenate(res, axis=0).astype(BF16)
-
-        steps = [(k, i) for k in range(seq_size) for i in range(dev_blocks)]
-        starts = [(seq ^ k) * dev_blocks + i for k, i in steps]
-        helds = (s_a, s_b)
-        top = first(starts[0], s_a)
-        for n, (k, i) in enumerate(steps):
-            if i == 0:
-                late[k].wait()
-            ahead = first(starts[n + 1], helds[(n + 1) % 2]) if n + 1 < len(steps) else None
-            outs[k][:, i * BLK : (i + 1) * BLK] = second(starts[n], helds[n % 2], top)
-            top = ahead
+                best = part if best is None else jnp.maximum(best, part)
+            return best
+
+        def values(b, held, top, c, acc, total):
+            p = jnp.exp2((held[c * BLK : (c + 4) * BLK, :] - top) * LOG2E)
+            part = jnp.sum(p.reshape(4 * BLK // 8, 8, cols), axis=0)
+            v = jnp.concatenate([vtab[pos_ref[c + i, b]] for i in range(4)], axis=1)
+            o = jnp.dot(v, p.astype(BF16), preferred_element_type=F32)
+            return (o, part) if acc is None else (acc + o, total + part)
+
+        def stage(start, held, top_ref, held_after, top_after):
+            for u in range(FAR_UNROLL):
+                n = start + u
+                b = block_of(n)
+                after = block_of(jnp.minimum(n + FAR_UNROLL, nblk - 1))
+                qm = query_matrix(heads_dev, q, per, after)
+                was = stat_ref[b, 0:1, :]
+                top = jnp.maximum(was, top_ref[u])
+                acc = total_f = best = None
+                for c in range(0, REMOTE, 4):
+                    best = scores(after, qm, held_after.at[u], c, best)
+                    acc, total_f = values(b, held.at[u], top, c, acc, total_f)
+                top_after[u] = jnp.max(best, axis=0, keepdims=True)
+                fade = jnp.exp2((was - top) * LOG2E)
+                inv = 1.0 / (stat_ref[b, 1:2, :] * fade + jnp.sum(total_f, axis=0, keepdims=True))
+                kept = fade * inv
+                res = []
+                for h in range(heads_dev):
+                    at, lane = slice(h * HD, (h + 1) * HD), slice(h * BLK, (h + 1) * BLK)
+                    res.append(acc[at, lane] * inv[:, lane] + old[b, at, :] * kept[:, lane])
+                att[n] = jnp.concatenate(res, axis=0).astype(BF16)
+
+        for u in range(FAR_UNROLL):
+            b = block_of(u)
+            qm = query_matrix(heads_dev, q, per, b)
+            best = None
+            for c in range(0, REMOTE, 4):
+                best = scores(b, qm, s_a.at[u], c, best)
+            t_a[u] = jnp.max(best, axis=0, keepdims=True)
+
+        def step(i, carry):
+            n = i * FAR_UNROLL
+            pl.when(lax.rem(i, 2) == 0)(lambda: stage(n, s_a, t_a, s_b, t_b))
+            pl.when(lax.rem(i, 2) == 1)(lambda: stage(n, s_b, t_b, s_a, t_a))
+            return carry
+
+        lax.fori_loop(0, nblk // FAR_UNROLL, step, 0)
+        for k in range(seq_size):
+            for i in range(dev_blocks):
+                outs[k][:, i * BLK : (i + 1) * BLK] = att[k * dev_blocks + i]
 
     flops = nblk * keys * BLK * feats * 4 * heads_dev
     return pl.pallas_call(
@@ -394,8 +443,11 @@
             pltpu.VMEM((ncl * cap, BLK, 2 * HD), BF16),
             pltpu.VMEM((ncl * cap, feats, BLK), BF16),
             pltpu.VMEM((nblk, feats, BLK), F32),
-            pltpu.VMEM((keys, cols), F32),
-            pltpu.VMEM((keys, cols), F32),
+            pltpu.VMEM((FAR_UNROLL, keys, cols), F32),
+            pltpu.VMEM((FAR_UNROLL, keys, cols), F32),
+            pltpu.VMEM((FAR_UNROLL, 1, cols), F32),
+            pltpu.VMEM((FAR_UNROLL, 1, cols), F32),
+            pltpu.VMEM((nblk, feats, BLK), BF16),
             pltpu.SemaphoreType.DMA((heads_dev * shifts + npair + seq_size,)),
         ],
         compiler_params=params(40),
@@ -455,25 +507,65 @@
     return lax.ppermute(x, "seq", [(i, i ^ k) for i in range(size)])
 
 
-def wanted_blocks(kv_ids, counts, ncl, nblk):
+def block_lists(ncl, nblk, slots, counts):
     cap = nblk // 4
-    remote_ids = kv_ids[:, NEAR:]
-    valid = jnp.arange(NEAR, KVB, dtype=jnp.int32)[None, :] < counts[:, None]
-    every = jnp.arange(ncl * nblk, dtype=jnp.int32)
-    present = jnp.any(
-        (remote_ids.reshape(-1)[:, None] == every[None, :]) & valid.reshape(-1)[:, None], axis=0
-    )
-    present = present.astype(jnp.int32).reshape(ncl, nblk)
-    rank = jnp.cumsum(present, axis=1) - 1
-    chosen = (rank[:, None, :] == jnp.arange(cap, dtype=jnp.int32)[None, :, None]) & (
-        present[:, None, :] > 0
-    )
-    wanted = jnp.sum(jnp.where(chosen, jnp.arange(nblk, dtype=jnp.int32)[None, None, :], 0), axis=2)
-    place = (remote_ids // nblk) * cap + jnp.sum(
-        jnp.where(remote_ids[:, :, None] == every[None, None, :], rank.reshape(-1)[None, None, :], 0),
-        axis=2,
-    )
-    return jnp.pad(wanted[:, None, :], ((0, 0), (0, 7), (0, 128 - cap))), jnp.where(valid, place, place[:, :1]).reshape(-1)
+
+    def body(slots_ref, counts_ref, meta_ref, pos_ref, wanted_ref):
+        seq = lax.axis_index("seq")
+        cluster = lax.axis_index("cluster")
+        meta_ref[0] = seq // 2
+        meta_ref[1] = lax.rem(seq, 2)
+        meta_ref[2] = cluster
+        meta_ref[3] = seq
+        valid = [counts_ref[...] > NEAR + j for j in range(REMOTE)]
+        ids = [slots_ref[NEAR + j : NEAR + j + 1, :] for j in range(REMOTE)]
+        spot = [jnp.zeros((1, nblk), F32) for _ in range(REMOTE)]
+        row = lax.broadcasted_iota(jnp.int32, (nblk, nblk), 0)
+        before = (row >= lax.broadcasted_iota(jnp.int32, (nblk, nblk), 1)).astype(F32)
+        local = lax.broadcasted_iota(jnp.int32, (nblk, 128), 0).astype(F32)
+        lane = lax.broadcasted_iota(jnp.int32, (nblk, 128), 1).astype(F32)
+        for c in range(ncl):
+            hits = [ids[j] - c * nblk == row for j in range(REMOTE)]
+            named = jnp.zeros((nblk, nblk), F32)
+            for j in range(REMOTE):
+                named = jnp.maximum(named, jnp.where(hits[j] & valid[j], 1.0, 0.0))
+            present = jnp.max(named, axis=1, keepdims=True)
+            wide = jnp.broadcast_to(present, (nblk, 128))
+            rank = jnp.dot(before, wide, preferred_element_type=F32) - 1.0
+            chosen = jnp.sum(jnp.where((rank == lane) & (wide > 0.0), local, 0.0), axis=0, keepdims=True)
+            wanted_ref[c] = jnp.broadcast_to(chosen, (8, 128)).astype(jnp.int32)
+            place = rank[:, :nblk] + float(c * cap)
+            for j in range(REMOTE):
+                spot[j] = spot[j] + jnp.sum(jnp.where(hits[j], place, 0.0), axis=0, keepdims=True)
+        for j in range(REMOTE):
+            pos_ref[j : j + 1, :] = jnp.where(valid[j], spot[j], spot[0]).astype(jnp.int32)
+
+    return pl.pallas_call(
+        body,
+        out_shape=[
+            jax.ShapeDtypeStruct((4,), jnp.int32),
+            jax.ShapeDtypeStruct((REMOTE, nblk), jnp.int32),
+            jax.ShapeDtypeStruct((ncl, 8, 128), jnp.int32),
+        ],
+        in_specs=[VMEM, VMEM],
+        out_specs=[SMEM, VMEM, VMEM],
+        compiler_params=params(40),
+        cost_estimate=cost(0, 4096),
+        name="block_lists",
+    )(slots, counts.reshape(1, nblk))
+
+
+def farthest_first(n):
+    return sorted(range(1, n), key=lambda k: (-bin(k).count("1"), k))
+
+
+def exchange(parts, earlier, seq_size):
+    parts = list(parts)
+    if earlier is not None:
+        parts[1], earlier[-1] = lax.optimization_barrier((parts[1], earlier[-1]))
+    for j in farthest_first(len(parts)):
+        parts[j] = crossed(parts[j], seq_size, 2 * j)
+    return parts
 
 
 def on_device(nodes, w_qkv, w_out, kv_ids, counts):
@@ -483,33 +575,36 @@
     npair = seq_size // 2
     nblk = seq_size * nodes.shape[0] // BLK
     cap = nblk // 4
-    seq = lax.axis_index("seq")
-    cluster = lax.axis_index("cluster")
-    meta = jnp.stack([seq // 2, seq % 2, cluster, seq]).astype(jnp.int32)
-
     other = crossed(nodes, seq_size, 1)
-    wanted, pos = wanted_blocks(kv_ids, counts, ncl, nblk)
-    wanted, own = lax.optimization_barrier((wanted, nodes))
-
+    slots = kv_ids.T
+    meta, pos, wanted = block_lists(ncl, nblk, slots, counts)
     q_span = [(3 * h * HD, HD) for h in range(heads_dev)]
     spans = [[((3 * h + 1) * HD, 2 * HD)] for h in range(heads_dev)]
-    (first_kv,) = project(spans[:1], heads_dev, npair, meta, own, other, w_qkv)
+    (first_kv,) = project(spans[:1], heads_dev, npair, meta, nodes, other, w_qkv)
+    wanted, first_kv = lax.optimization_barrier((wanted, first_kv))
+    asked = lax.all_to_all(wanted, "cluster", split_axis=0, concat_axis=0, tiled=True)
     (rest,) = project([sum(spans[1:] + [q_span], [])], heads_dev, npair, meta, nodes, other, w_qkv)
-    wanted, rest = lax.optimization_barrier((wanted, rest))
-    asked = lax.all_to_all(wanted, "cluster", split_axis=0, concat_axis=0, tiled=True)
-    first_kv = [x if j == 0 else crossed(x, seq_size, 2 * j) for j, x in enumerate(first_kv)]
-    rest = [x if j == 0 else crossed(x, seq_size, 2 * j) for j, x in enumerate(rest)]
+    asked, rest = lax.optimization_barrier((asked, rest))
+    first_kv = exchange(first_kv, None, seq_size)
+    rest = exchange(rest, first_kv, seq_size)
     far = []
     for h in range(heads_dev):
         tables, row = (first_kv, 0) if h == 0 else (rest, (h - 1) * 2 * HD)
-        picked = select(npair, ncl, cap, meta, asked, tables, row)
+        picked = list(select(npair, ncl, cap, meta, asked, tables, row))
+        gate = rest[-1] if h == 0 else far[h - 1][0]
+        picked[-1], gate = lax.optimization_barrier((picked[-1], gate))
+        if h == 0:
+            rest[-1] = gate
+        else:
+            far[h - 1][0] = gate
         far.append([shifted(x, "cluster", ncl, s + 1) for s, x in enumerate(picked)])
-    near_ids = (kv_ids[:, :NEAR] - cluster * nblk).reshape(-1)
-    near, stats = near_attention(heads_dev, npair, meta, near_ids, first_kv, rest)
+    near, stats = near_attention(heads_dev, npair, meta, slots, first_kv, rest)
     outs = far_attention(
         heads_dev, npair, seq_size, ncl, cap, meta, pos, counts, far, rest, near, stats
     )
-    pieces = [x if k == 0 else crossed(x, seq_size, k) for k, x in enumerate(outs)]
+    pieces = list(outs)
+    for k in sorted(range(1, seq_size), key=lambda k: (-bin(k // 2).count("1"), k)):
+        pieces[k] = crossed(pieces[k], seq_size, k)
     return project_out(seq_size, meta, pieces, w_out)
 
 

time: 112 us -> 108 us (0.964)
  waiting for transfers between devices: 21.1 us -> 29.2 us
  Pallas kernels: 48.8 us -> 42.2 us
  other arithmetic: 3.52 us -> 0 us
  local copies, waits for them, and re-layouts: 5.7 us -> 3.9 us
    ppermute x6, waiting for transfers between devices: 0.02 us -> 6.63 us  [shifted(): return lax.ppermute(x, axis, [(i, (i + shift) % size) for i in range(size)])]
    pallas_call x1, Pallas kernels: 19.8 us -> 14.8 us  [near_attention(): pl.pallas_call(body, out_shape=[jax.ShapeDtypeStruct((nblk, feats, BLK),...]
    ppermute x14, waiting for transfers between devices: 19.7 us -> 22.6 us  [crossed(): return lax.ppermute(x, 'seq', [(i, i ^ k) for i in range(size)])]
    pallas_call x1, Pallas kernels: 9.5 us -> 7.25 us  [far_attention(): pl.pallas_call(body, out_shape=[jax.ShapeDtypeStruct((feats, dev_blocks *...]
    all_to_all x1, waiting for transfers between devices: 1.42 us -> 0.01 us  [on_device(): lax.all_to_all(wanted, 'cluster', split_axis=0, concat_axis=0, tiled=True)]
    unnamed x18 -> x22, local copies, waits for them, and re-layouts: 3.43 us -> 3.9 us
  transfers between devices with their start and end apart: 21 -> 21, of which waited for: 6 -> 7; matrix products, arithmetic and copies ran while one was open for 5% -> 0% of each run, Pallas kernels for 27% -> 24%
where the time goes in v3:
time: 108 us; the launch traced here: 107 us
  Pallas kernels  42.2 us (39%)
  starting transfers between devices  31.6 us (29%)
  waiting for transfers between devices  29.2 us (27%)
  local copies, waits for them, and re-layouts  3.9 us (4%)
    ppermute x14, waiting for transfers between devices, crossed(): return lax.ppermute(x, 'seq', [(i, i ^ k) for i in range(size)])  22.6 us
    pallas_call x1, Pallas kernels, near_attention(): pl.pallas_call(body, out_shape=[jax.ShapeDtypeStruct((nblk, feats, BLK),...  14.8 us
    ppermute x14, starting transfers between devices, crossed(): return lax.ppermute(x, 'seq', [(i, i ^ k) for i in range(size)])  13.7 us
    ppermute x6, starting transfers between devices, shifted(): return lax.ppermute(x, axis, [(i, (i + shift) % size) for i in range(size)])  13 us
    pallas_call x2, Pallas kernels, project(): pl.pallas_call(body, out_shape=shapes, in_specs=[SMEM, ANY, ANY, ANY], ou...  11.9 us
    pallas_call x1, Pallas kernels, far_attention(): pl.pallas_call(body, out_shape=[jax.ShapeDtypeStruct((feats, dev_blocks *...  7.25 us
    ppermute x6, waiting for transfers between devices, shifted(): return lax.ppermute(x, axis, [(i, (i + shift) % size) for i in range(size)])  6.63 us
    all_to_all x1, starting transfers between devices, on_device(): lax.all_to_all(wanted, 'cluster', split_axis=0, concat_axis=0, tiled=True)  4.87 us
  transfers between devices with their start and end apart: 21, of which 7 were waited for; matrix products, arithmetic and copies ran while one was open for 0% of the time, Pallas kernels for 24%

profile of v3, /device:TPU:0, one launch (start us, length us, event | category | flops | bytes accessed | tf_op | source)
XLA Modules:
  0.0 107.3 jit_solution(15577811857535643069)
XLA Ops:
  0.0 0.5 collective-permute-start
  0.5 0.7 copy-done.6
  1.2 0.7 copy-done.8
  1.8 0.9 block_lists.1
  2.7 0.0 copy-start.4
  2.7 0.5 copy-done.4
  3.2 0.0 collective-permute-done.other_ref
  3.2 1.0 copy-done.10
  4.2 5.1 %project.2 = (bf16[128,1024]{1,0:T(8,128)(2,1)}, bf16[128,1024]{1,0:T(8,128)(2,1)}, bf16[128,1024]{1,0:T(8,128)(2,1)}, bf16[128,1024]{1,0:T(8,128)(2,1)}) custom-call(s32[4]{0:T(128)} %copy-done.4, bf16[512,1024]{1,0:T(8,128)(2,1)} %own_ref.3, bf16[512,1024]{1,0:T(8,128)(2,1)} %copy-done.10, bf16[1024,3072]{1,0:T(8,128)(2,1)} %w_ref.3), custom_call_target="tpu_custom_call" | custom-call | flops 1073741824 | bytes 4194304 | tf_op jit(solution)/shard_map/project/pallas_call | solution.py:107
  9.3 3.6 %collective-permute-start.1 = (bf16[128,1024]{1,0:T(8,128)(2,1)}, bf16[128,1024]{1,0:T(8,128)(2,1)S(1)}, u32[]{:S(2)}, u32[]{:S(2)}) collective-permute-start(bf16[128,1024]{1,0:T(8,128)(2,1)} %get-tuple-element.63), channel_id=1, source_target_pairs={{0,6},{1,7},{2,4},{3,5},{4,2},{5,3},{6,0},{7,1},{8,14},{9,15},{10,... | collective-permute-start | bytes 786440 | tf_op jit(solution)/shard_map/ppermute | solution.py:507
  12.9 4.9 %all-to-all-start = ((s32[4,8,128]{2,1,0:T(8,128)}), s32[4,8,128]{2,1,0:T(8,128)S(1)}, u32[]{:S(2)}, u32[]{:S(2)}) async-start(s32[4,8,128]{2,1,0:T(8,128)} %get-tuple-element.55), calls=%async_computation | async-start | bytes 32768 | tf_op jit(solution)/shard_map/all_to_all | solution.py:585
  17.8 0.5 collective-permute-start.4
  18.4 0.5 collective-permute-start.5
  18.9 6.8 %project.3 = (bf16[256,1024]{1,0:T(8,128)(2,1)}, bf16[256,1024]{1,0:T(8,128)(2,1)}, bf16[256,1024]{1,0:T(8,128)(2,1)}, bf16[256,1024]{1,0:T(8,128)(2,1)}) custom-call(s32[4]{0:T(128)} %copy-done.4, bf16[512,1024]{1,0:T(8,128)(2,1)} %own_ref.3, bf16[512,1024]{1,0:T(8,128)(2,1)} %copy-done.10, bf16[1024,3072]{1,0:T(8,128)(2,1)} %w_ref.3), custom_call_target="tpu_custom_call" | custom-call | flops 2147483648 | bytes 5242880 | tf_op jit(solution)/shard_map/project/pallas_call | solution.py:107
  25.6 0.0 copy-start.2
  25.7 0.0 copy-start.7
  25.7 0.0 all-to-all-done.asked_ref
  25.7 2.5 %collective-permute-start.6 = (bf16[256,1024]{1,0:T(8,128)(2,1)}, bf16[256,1024]{1,0:T(8,128)(2,1)S(1)}, u32[]{:S(2)}, u32[]{:S(2)}) collective-permute-start(bf16[256,1024]{1,0:T(8,128)(2,1)} %get-tuple-element.71), channel_id=1, source_target_pairs={{0,6},{1,7},{2,4},{3,5},{4,2},{5,3},{6,0},{7,1},{8,14},{9,15},{10,... | collective-permute-start | bytes 1572872 | tf_op jit(solution)/shard_map/ppermute | solution.py:507
  28.2 0.5 collective-permute-start.3
  28.7 0.0 collective-permute-done.1.refs_3_
  28.7 0.5 collective-permute-start.2
  29.2 0.0 collective-permute-done.4.refs_1_
  29.2 0.0 collective-permute-done.5.refs_2_
  29.2 0.0 copy-done.3
  29.2 0.0 copy-done.5
  29.3 1.6 %select.2 = (bf16[8,128,128]{2,1,0:T(8,128)(2,1)S(1)}, bf16[8,128,128]{2,1,0:T(8,128)(2,1)S(1)}, bf16[8,128,128]{2,1,0:T(8,128)(2,1)S(1)}) custom-call(s32[4]{0:T(128)S(1)} %copy-done.5, s32[4,8,128]{2,1,0:T(8,128)S(1)} %all-to-all-done.asked_ref, bf16[128,1024]{1,0:T(8,128)(2,1)S(1)} %copy-done.3, bf16[128,1024]{1,0:T(8,128)(2,1)S(1)} %collective-permute-done.4.refs_1_, ...), custom_call_target="tpu_custom_call" | custom-call | bytes 2097152 | tf_op jit(solution)/shard_map/select/pallas_call | solution.py:163
  30.9 2.1 %collective-permute-start.7 = (bf16[8,128,128]{2,1,0:T(8,128)(2,1)S(1)}, bf16[8,128,128]{2,1,0:T(8,128)(2,1)S(1)}, u32[]{:S(2)}, u32[]{:S(2)}) collective-permute-start(bf16[8,128,128]{2,1,0:T(8,128)(2,1)S(1)} %get-tuple-element.74), channel_id=1, source_target_pairs={{0,8},{8,16},{16,24},{24,0},{1,9},{9,17},{17,25},{25,1},{2,10},{10... | collective-permute-start | bytes 786440 | tf_op jit(solution)/shard_map/ppermute | solution.py:503
  33.0 2.4 %collective-permute-start.8 = (bf16[8,128,128]{2,1,0:T(8,128)(2,1)S(1)}, bf16[8,128,128]{2,1,0:T(8,128)(2,1)S(1)}, u32[]{:S(2)}, u32[]{:S(2)}) collective-permute-start(bf16[8,128,128]{2,1,0:T(8,128)(2,1)S(1)} %get-tuple-element.76), channel_id=1, source_target_pairs={{0,16},{8,24},{16,0},{24,8},{1,17},{9,25},{17,1},{25,9},{2,18},{10... | collective-permute-start | bytes 786440 | tf_op jit(solution)/shard_map/ppermute | solution.py:503
  35.3 6.4 %collective-permute-done.6.refs_3_.refs_7_.refs_9_ = bf16[256,1024]{1,0:T(8,128)(2,1)S(1)} collective-permute-done((bf16[256,1024]{1,0:T(8,128)(2,1)}, bf16[256,1024]{1,0:T(8,128)(2,1)S(1)}, u32[]{:S(2)}, u32[]{:S(2)}) %collective-permute-start.6) | collective-permute-done | bytes 524320 | tf_op jit(solution)/shard_map/ppermute | solution.py:507
  41.8 3.8 %collective-permute-start.9 = (bf16[8,128,128]{2,1,0:T(8,128)(2,1)S(1)}, bf16[8,128,128]{2,1,0:T(8,128)(2,1)S(1)}, u32[]{:S(2)}, u32[]{:S(2)}) collective-permute-start(bf16[8,128,128]{2,1,0:T(8,128)(2,1)S(1)} %get-tuple-element.77), channel_id=1, source_target_pairs={{0,24},{8,0},{16,8},{24,16},{1,25},{9,1},{17,9},{25,17},{2,26},{10... | collective-permute-start | bytes 786440 | tf_op jit(solution)/shard_map/ppermute | solution.py:503
  45.6 5.6 %collective-permute-done.3.refs_2_.refs_6_.refs_8_ = bf16[256,1024]{1,0:T(8,128)(2,1)S(1)} collective-permute-done((bf16[256,1024]{1,0:T(8,128)(2,1)}, bf16[256,1024]{1,0:T(8,128)(2,1)S(1)}, u32[]{:S(2)}, u32[]{:S(2)}) %collective-permute-start.3) | collective-permute-done | bytes 524320 | tf_op jit(solution)/shard_map/ppermute | solution.py:507
  51.2 0.1 collective-permute-done.2.refs_1_.refs_5_.refs_7_
  51.3 1.0 copy-done.1
  52.3 1.6 %select.3 = (bf16[8,128,128]{2,1,0:T(8,128)(2,1)S(1)}, bf16[8,128,128]{2,1,0:T(8,128)(2,1)S(1)}, bf16[8,128,128]{2,1,0:T(8,128)(2,1)S(1)}) custom-call(s32[4]{0:T(128)S(1)} %copy-done.5, s32[4,8,128]{2,1,0:T(8,128)S(1)} %all-to-all-done.asked_ref, bf16[256,1024]{1,0:T(8,128)(2,1)S(1)} %copy-done.1, ...), custom_call_target="tpu_custom_call" | custom-call | bytes 2097152 | tf_op jit(solution)/shard_map/select/pallas_call | solution.py:163
  53.9 0.0 collective-permute-done.7.refs_0_
  54.0 3.6 %collective-permute-start.12 = (bf16[8,128,128]{2,1,0:T(8,128)(2,1)S(1)}, bf16[8,128,128]{2,1,0:T(8,128)(2,1)S(1)}, u32[]{:S(2)}, u32[]{:S(2)}) collective-permute-start(bf16[8,128,128]{2,1,0:T(8,128)(2,1)S(1)} %get-tuple-element.80), channel_id=1, source_target_pairs={{0,24},{8,0},{16,8},{24,16},{1,25},{9,1},{17,9},{25,17},{2,26},{10... | collective-permute-start | bytes 786440 | tf_op jit(solution)/shard_map/ppermute | solution.py:503
  57.5 0.0 collective-permute-start.10
  57.6 1.1 %collective-permute-start.11 = (bf16[8,128,128]{2,1,0:T(8,128)(2,1)S(1)}, bf16[8,128,128]{2,1,0:T(8,128)(2,1)S(1)}, u32[]{:S(2)}, u32[]{:S(2)}) collective-permute-start(bf16[8,128,128]{2,1,0:T(8,128)(2,1)S(1)} %get-tuple-element.79), channel_id=1, source_target_pairs={{0,16},{8,24},{16,0},{24,8},{1,17},{9,25},{17,1},{25,9},{2,18},{10... | collective-permute-start | bytes 786440 | tf_op jit(solution)/shard_map/ppermute | solution.py:503
  58.7 0.0 copy-done.2
  58.7 0.0 copy-done.7
  58.7 14.8 %near_attention.1 = (f32[32,128,128]{2,1,0:T(8,128)S(1)}, f32[32,8,256]{2,1,0:T(8,128)S(1)}) custom-call(s32[4]{0:T(128)S(1)} %copy-done.5, s32[16,32]{1,0:T(8,128)S(1)} %bitcast.3, bf16[128,1024]{1,0:T(8,128)(2,1)S(1)} %copy-done.3, bf16[128,1024]{1,0:T(8,128)(2,1)S(1)} %collective-permute-done.4.refs_1_, ...), custom_call_target="tpu_custom_call" | custom-call | flops 12884901888 | bytes 4194304 | tf_op jit(solution)/shard_map/near_attention/pallas_call | solution.py:287
  73.5 0.0 collective-permute-done.8.refs_1_
  73.5 0.0 collective-permute-done.9.refs_2_
  73.5 0.0 collective-permute-done.12.refs_5_
  73.5 0.0 collective-permute-done.10.refs_3_
  73.6 6.6 %collective-permute-done.11.refs_4_ = bf16[8,128,128]{2,1,0:T(8,128)(2,1)S(1)} collective-permute-done((bf16[8,128,128]{2,1,0:T(8,128)(2,1)S(1)}, bf16[8,128,128]{2,1,0:T(8,128)(2,1)S(1)}, u32[]{:S(2)}, u32[]{:S(2)}) %collective-permute-start.11) | collective-permute-done | bytes 262176 | tf_op jit(solution)/shard_map/ppermute | solution.py:503
  80.2 0.0 copy-done.9
  80.2 7.2 %far_attention.1 = (bf16[128,512]{1,0:T(8,128)(2,1)S(1)}, bf16[128,512]{1,0:T(8,128)(2,1)S(1)}, bf16[128,512]{1,0:T(8,128)(2,1)S(1)}, bf16[128,512]{1,0:T(8,128)...) custom-call(s32[4]{0:T(128)S(1)} %copy-done.5, ...), custom_call_target="tpu_custom_call" | custom-call | flops 2147483648 | bytes 3145728 | tf_op jit(solution)/shard_map/far_attention/pallas_call | solution.py:435
  87.4 0.1 collective-permute-start.13
  87.5 1.5 %collective-permute-start.14 = (bf16[128,512]{1,0:T(8,128)(2,1)S(1)}, bf16[128,512]{1,0:T(8,128)(2,1)S(1)}, u32[]{:S(2)}, u32[]{:S(2)}) collective-permute-start(bf16[128,512]{1,0:T(8,128)(2,1)S(1)} %get-tuple-element.85), channel_id=1, source_target_pairs={{0,2},{1,3},{2,0},{3,1},{4,6},{5,7},{6,4},{7,5},{8,10},{9,11},{10,... | collective-permute-start | bytes 393224 | tf_op jit(solution)/shard_map/ppermute | solution.py:507
  89.1 0.3 collective-permute-start.15
  89.4 1.5 %collective-permute-start.16 = (bf16[128,512]{1,0:T(8,128)(2,1)S(1)}, bf16[128,512]{1,0:T(8,128)(2,1)S(1)}, u32[]{:S(2)}, u32[]{:S(2)}) collective-permute-start(bf16[128,512]{1,0:T(8,128)(2,1)S(1)} %get-tuple-element.87), channel_id=1, source_target_pairs={{0,4},{1,5},{2,6},{3,7},{4,0},{5,1},{6,2},{7,3},{8,12},{9,13},{10,... | collective-permute-start | bytes 393224 | tf_op jit(solution)/shard_map/ppermute | solution.py:507
  90.9 0.2 collective-permute-start.17
  91.1 0.0 collective-permute-done.13.refs_1_
  91.1 1.3 %collective-permute-start.18 = (bf16[128,512]{1,0:T(8,128)(2,1)S(1)}, bf16[128,512]{1,0:T(8,128)(2,1)S(1)}, u32[]{:S(2)}, u32[]{:S(2)}) collective-permute-start(bf16[128,512]{1,0:T(8,128)(2,1)S(1)} %get-tuple-element.89), channel_id=1, source_target_pairs={{0,6},{1,7},{2,4},{3,5},{4,2},{5,3},{6,0},{7,1},{8,14},{9,15},{10,... | collective-permute-start | bytes 393224 | tf_op jit(solution)/shard_map/ppermute | solution.py:507
  92.3 1.5 %collective-permute-done.14.refs_2_ = bf16[128,512]{1,0:T(8,128)(2,1)S(1)} collective-permute-done((bf16[128,512]{1,0:T(8,128)(2,1)S(1)}, bf16[128,512]{1,0:T(8,128)(2,1)S(1)}, u32[]{:S(2)}, u32[]{:S(2)}) %collective-permute-start.14) | collective-permute-done | bytes 131104 | tf_op jit(solution)/shard_map/ppermute | solution.py:507
  93.9 0.2 collective-permute-start.19
  94.0 1.7 %collective-permute-done.15.refs_3_ = bf16[128,512]{1,0:T(8,128)(2,1)S(1)} collective-permute-done((bf16[128,512]{1,0:T(8,128)(2,1)S(1)}, bf16[128,512]{1,0:T(8,128)(2,1)S(1)}, u32[]{:S(2)}, u32[]{:S(2)}) %collective-permute-start.15) | collective-permute-done | bytes 131104 | tf_op jit(solution)/shard_map/ppermute | solution.py:507
  95.8 0.0 collective-permute-done.16.refs_4_
  95.8 7.2 %collective-permute-done.17.refs_5_ = bf16[128,512]{1,0:T(8,128)(2,1)S(1)} collective-permute-done((bf16[128,512]{1,0:T(8,128)(2,1)S(1)}, bf16[128,512]{1,0:T(8,128)(2,1)S(1)}, u32[]{:S(2)}, u32[]{:S(2)}) %collective-permute-start.17) | collective-permute-done | bytes 131104 | tf_op jit(solution)/shard_map/ppermute | solution.py:507
  103.0 0.0 collective-permute-done.18.refs_6_
  103.0 0.0 collective-permute-done.19.refs_7_
  103.0 0.0 copy-done
  103.0 4.1 %project_out.1 = bf16[512,1024]{1,0:T(8,128)(2,1)} custom-call(s32[4]{0:T(128)S(1)} %copy-done.5, bf16[128,512]{1,0:T(8,128)(2,1)S(1)} %get-tuple-element.83.refs_0_, bf16[128,512]{1,0:T(8,128)(2,1)S(1)} %collective-permute-done.13.refs_1_, bf16[128,512]{1,0:T(8,128)(2,1)S(1)} %collective-permute-done.14.refs_2_, ...), custom_call_target="tpu_custom_call" | custom-call | flops 1073741824 | bytes 4194304 | tf_op jit(solution)/shard_map/project_out/pallas_call | solution.py:486
  (8 shorter events, 0.0 us)
Async XLA Ops:
  0.0 3.2 %collective-permute-start = (bf16[512,1024]{1,0:T(8,128)(2,1)}, bf16[512,1024]{1,0:T(8,128)(2,1)S(1)}, u32[]{:S(2)}, u32[]{:S(2)}) collective-permute-start(bf16[512,1024]{1,0:T(8,128)(2,1)} %own_ref.3), channel_id=1, source_target_pairs={{0,1},{1,0},{2,3},{3,2},{4,5},{5,4},{6,7},{7,6},{8,9},{9,8},{10,11... | collective-permute-start | bytes 3145736 | tf_op jit(solution)/shard_map/ppermute | solution.py:507
  0.5 0.7 copy-start.6
  1.2 0.7 copy-start.8
  2.7 0.5 copy-start.4
  3.2 1.0 copy-start.10
  9.3 19.4 %collective-permute-start.1 = (bf16[128,1024]{1,0:T(8,128)(2,1)}, bf16[128,1024]{1,0:T(8,128)(2,1)S(1)}, u32[]{:S(2)}, u32[]{:S(2)}) collective-permute-start(bf16[128,1024]{1,0:T(8,128)(2,1)} %get-tuple-element.63), channel_id=1, source_target_pairs={{0,6},{1,7},{2,4},{3,5},{4,2},{5,3},{6,0},{7,1},{8,14},{9,15},{10,... | collective-permute-start | bytes 786440 | tf_op jit(solution)/shard_map/ppermute | solution.py:507
  12.9 12.7 %all-to-all-start = ((s32[4,8,128]{2,1,0:T(8,128)}), s32[4,8,128]{2,1,0:T(8,128)S(1)}, u32[]{:S(2)}, u32[]{:S(2)}) async-start(s32[4,8,128]{2,1,0:T(8,128)} %get-tuple-element.55), calls=%async_computation | async-start | bytes 32768 | tf_op jit(solution)/shard_map/all_to_all | solution.py:585
  17.8 11.4 %copy-start.3 = (bf16[128,1024]{1,0:T(8,128)(2,1)S(1)}, bf16[128,1024]{1,0:T(8,128)(2,1)}, u32[]{:S(2)}) copy-start(bf16[128,1024]{1,0:T(8,128)(2,1)} %get-tuple-element.66.refs_0_) | copy-start | bytes 786436
  17.8 11.4 %copy-start.5 = (s32[4]{0:T(128)S(1)}, s32[4]{0:T(128)}, u32[]{:S(2)}) copy-start(s32[4]{0:T(128)} %copy-done.4) | copy-start | bytes 52
  17.8 11.4 %collective-permute-start.4 = (bf16[128,1024]{1,0:T(8,128)(2,1)}, bf16[128,1024]{1,0:T(8,128)(2,1)S(1)}, u32[]{:S(2)}, u32[]{:S(2)}) collective-permute-start(bf16[128,1024]{1,0:T(8,128)(2,1)} %get-tuple-element.67), channel_id=1, source_target_pairs={{0,2},{1,3},{2,0},{3,1},{4,6},{5,7},{6,4},{7,5},{8,10},{9,11},{10,... | collective-permute-start | bytes 786440 | tf_op jit(solution)/shard_map/ppermute | solution.py:507
  18.4 10.9 %collective-permute-start.5 = (bf16[128,1024]{1,0:T(8,128)(2,1)}, bf16[128,1024]{1,0:T(8,128)(2,1)S(1)}, u32[]{:S(2)}, u32[]{:S(2)}) collective-permute-start(bf16[128,1024]{1,0:T(8,128)(2,1)} %get-tuple-element.68), channel_id=1, source_target_pairs={{0,4},{1,5},{2,6},{3,7},{4,0},{5,1},{6,2},{7,3},{8,12},{9,13},{10,... | collective-permute-start | bytes 786440 | tf_op jit(solution)/shard_map/ppermute | solution.py:507
  25.6 33.0 %copy-start.2 = (bf16[256,1024]{1,0:T(8,128)(2,1)S(1)}, bf16[256,1024]{1,0:T(8,128)(2,1)}, u32[]{:S(2)}) copy-start(bf16[256,1024]{1,0:T(8,128)(2,1)} %get-tuple-element.61.refs_0_.refs_4_.refs_6_) | copy-start | bytes 1572868
  25.7 33.0 %copy-start.7 = (s32[32,16]{0,1:T(8,128)S(1)}, s32[32,16]{0,1:T(8,128)}, u32[]{:S(2)}) copy-start(s32[32,16]{0,1:T(8,128)} %param.8) | copy-start | bytes 6148
  25.7 16.1 %collective-permute-start.6 = (bf16[256,1024]{1,0:T(8,128)(2,1)}, bf16[256,1024]{1,0:T(8,128)(2,1)S(1)}, u32[]{:S(2)}, u32[]{:S(2)}) collective-permute-start(bf16[256,1024]{1,0:T(8,128)(2,1)} %get-tuple-element.71), channel_id=1, source_target_pairs={{0,6},{1,7},{2,4},{3,5},{4,2},{5,3},{6,0},{7,1},{8,14},{9,15},{10,... | collective-permute-start | bytes 1572872 | tf_op jit(solution)/shard_map/ppermute | solution.py:507
  28.2 23.0 %collective-permute-start.3 = (bf16[256,1024]{1,0:T(8,128)(2,1)}, bf16[256,1024]{1,0:T(8,128)(2,1)S(1)}, u32[]{:S(2)}, u32[]{:S(2)}) collective-permute-start(bf16[256,1024]{1,0:T(8,128)(2,1)} %get-tuple-element.65), channel_id=1, source_target_pairs={{0,4},{1,5},{2,6},{3,7},{4,0},{5,1},{6,2},{7,3},{8,12},{9,13},{10,... | collective-permute-start | bytes 1572872 | tf_op jit(solution)/shard_map/ppermute | solution.py:507
  28.7 22.6 %collective-permute-start.2 = (bf16[256,1024]{1,0:T(8,128)(2,1)}, bf16[256,1024]{1,0:T(8,128)(2,1)S(1)}, u32[]{:S(2)}, u32[]{:S(2)}) collective-permute-start(bf16[256,1024]{1,0:T(8,128)(2,1)} %get-tuple-element.64), channel_id=1, source_target_pairs={{0,2},{1,3},{2,0},{3,1},{4,6},{5,7},{6,4},{7,5},{8,10},{9,11},{10,... | collective-permute-start | bytes 1572872 | tf_op jit(solution)/shard_map/ppermute | solution.py:507
  30.9 23.1 %collective-permute-start.7 = (bf16[8,128,128]{2,1,0:T(8,128)(2,1)S(1)}, bf16[8,128,128]{2,1,0:T(8,128)(2,1)S(1)}, u32[]{:S(2)}, u32[]{:S(2)}) collective-permute-start(bf16[8,128,128]{2,1,0:T(8,128)(2,1)S(1)} %get-tuple-element.74), channel_id=1, source_target_pairs={{0,8},{8,16},{16,24},{24,0},{1,9},{9,17},{17,25},{25,1},{2,10},{10... | collective-permute-start | bytes 786440 | tf_op jit(solution)/shard_map/ppermute | solution.py:503
  33.0 40.5 %collective-permute-start.8 = (bf16[8,128,128]{2,1,0:T(8,128)(2,1)S(1)}, bf16[8,128,128]{2,1,0:T(8,128)(2,1)S(1)}, u32[]{:S(2)}, u32[]{:S(2)}) collective-permute-start(bf16[8,128,128]{2,1,0:T(8,128)(2,1)S(1)} %get-tuple-element.76), channel_id=1, source_target_pairs={{0,16},{8,24},{16,0},{24,8},{1,17},{9,25},{17,1},{25,9},{2,18},{10... | collective-permute-start | bytes 786440 | tf_op jit(solution)/shard_map/ppermute | solution.py:503
  41.8 31.8 %collective-permute-start.9 = (bf16[8,128,128]{2,1,0:T(8,128)(2,1)S(1)}, bf16[8,128,128]{2,1,0:T(8,128)(2,1)S(1)}, u32[]{:S(2)}, u32[]{:S(2)}) collective-permute-start(bf16[8,128,128]{2,1,0:T(8,128)(2,1)S(1)} %get-tuple-element.77), channel_id=1, source_target_pairs={{0,24},{8,0},{16,8},{24,16},{1,25},{9,1},{17,9},{25,17},{2,26},{10... | collective-permute-start | bytes 786440 | tf_op jit(solution)/shard_map/ppermute | solution.py:503
  51.3 1.0 copy-start.1
  54.0 19.6 %collective-permute-start.12 = (bf16[8,128,128]{2,1,0:T(8,128)(2,1)S(1)}, bf16[8,128,128]{2,1,0:T(8,128)(2,1)S(1)}, u32[]{:S(2)}, u32[]{:S(2)}) collective-permute-start(bf16[8,128,128]{2,1,0:T(8,128)(2,1)S(1)} %get-tuple-element.80), channel_id=1, source_target_pairs={{0,24},{8,0},{16,8},{24,16},{1,25},{9,1},{17,9},{25,17},{2,26},{10... | collective-permute-start | bytes 786440 | tf_op jit(solution)/shard_map/ppermute | solution.py:503
  57.5 16.0 %collective-permute-start.10 = (bf16[8,128,128]{2,1,0:T(8,128)(2,1)S(1)}, bf16[8,128,128]{2,1,0:T(8,128)(2,1)S(1)}, u32[]{:S(2)}, u32[]{:S(2)}) collective-permute-start(bf16[8,128,128]{2,1,0:T(8,128)(2,1)S(1)} %get-tuple-element.78), channel_id=1, source_target_pairs={{0,8},{8,16},{16,24},{24,0},{1,9},{9,17},{17,25},{25,1},{2,10},{10... | collective-permute-start | bytes 786440 | tf_op jit(solution)/shard_map/ppermute | solution.py:503
  57.6 22.6 %copy-start.9 = (s32[32]{0:T(128)S(1)}, s32[32]{0:T(128)}, u32[]{:S(2)}) copy-start(s32[32]{0:T(128)} %counts_ref.1) | copy-start | bytes 388
  57.6 22.6 %collective-permute-start.11 = (bf16[8,128,128]{2,1,0:T(8,128)(2,1)S(1)}, bf16[8,128,128]{2,1,0:T(8,128)(2,1)S(1)}, u32[]{:S(2)}, u32[]{:S(2)}) collective-permute-start(bf16[8,128,128]{2,1,0:T(8,128)(2,1)S(1)} %get-tuple-element.79), channel_id=1, source_target_pairs={{0,16},{8,24},{16,0},{24,8},{1,17},{9,25},{17,1},{25,9},{2,18},{10... | collective-permute-start | bytes 786440 | tf_op jit(solution)/shard_map/ppermute | solution.py:503
  80.2 22.8 %copy-start = (bf16[1024,1024]{1,0:T(8,128)(2,1)S(1)}, bf16[1024,1024]{1,0:T(8,128)(2,1)}, u32[]{:S(2)}) copy-start(bf16[1024,1024]{1,0:T(8,128)(2,1)} %refs_8_.1) | copy-start | bytes 6291460
  87.4 3.6 %collective-permute-start.13 = (bf16[128,512]{1,0:T(8,128)(2,1)S(1)}, bf16[128,512]{1,0:T(8,128)(2,1)S(1)}, u32[]{:S(2)}, u32[]{:S(2)}) collective-permute-start(bf16[128,512]{1,0:T(8,128)(2,1)S(1)} %get-tuple-element.84), channel_id=1, source_target_pairs={{0,1},{1,0},{2,3},{3,2},{4,5},{5,4},{6,7},{7,6},{8,9},{9,8},{10,11... | collective-permute-start | bytes 393224 | tf_op jit(solution)/shard_map/ppermute | solution.py:507
  87.5 6.4 %collective-permute-start.14 = (bf16[128,512]{1,0:T(8,128)(2,1)S(1)}, bf16[128,512]{1,0:T(8,128)(2,1)S(1)}, u32[]{:S(2)}, u32[]{:S(2)}) collective-permute-start(bf16[128,512]{1,0:T(8,128)(2,1)S(1)} %get-tuple-element.85), channel_id=1, source_target_pairs={{0,2},{1,3},{2,0},{3,1},{4,6},{5,7},{6,4},{7,5},{8,10},{9,11},{10,... | collective-permute-start | bytes 393224 | tf_op jit(solution)/shard_map/ppermute | solution.py:507
  89.1 6.7 %collective-permute-start.15 = (bf16[128,512]{1,0:T(8,128)(2,1)S(1)}, bf16[128,512]{1,0:T(8,128)(2,1)S(1)}, u32[]{:S(2)}, u32[]{:S(2)}) collective-permute-start(bf16[128,512]{1,0:T(8,128)(2,1)S(1)} %get-tuple-element.86), channel_id=1, source_target_pairs={{0,3},{1,2},{2,1},{3,0},{4,7},{5,6},{6,5},{7,4},{8,11},{9,10},{10,... | collective-permute-start | bytes 393224 | tf_op jit(solution)/shard_map/ppermute | solution.py:507
  89.4 6.4 %collective-permute-start.16 = (bf16[128,512]{1,0:T(8,128)(2,1)S(1)}, bf16[128,512]{1,0:T(8,128)(2,1)S(1)}, u32[]{:S(2)}, u32[]{:S(2)}) collective-permute-start(bf16[128,512]{1,0:T(8,128)(2,1)S(1)} %get-tuple-element.87), channel_id=1, source_target_pairs={{0,4},{1,5},{2,6},{3,7},{4,0},{5,1},{6,2},{7,3},{8,12},{9,13},{10,... | collective-permute-start | bytes 393224 | tf_op jit(solution)/shard_map/ppermute | solution.py:507
  90.9 12.1 %collective-permute-start.17 = (bf16[128,512]{1,0:T(8,128)(2,1)S(1)}, bf16[128,512]{1,0:T(8,128)(2,1)S(1)}, u32[]{:S(2)}, u32[]{:S(2)}) collective-permute-start(bf16[128,512]{1,0:T(8,128)(2,1)S(1)} %get-tuple-element.88), channel_id=1, source_target_pairs={{0,5},{1,4},{2,7},{3,6},{4,1},{5,0},{6,3},{7,2},{8,13},{9,12},{10,... | collective-permute-start | bytes 393224 | tf_op jit(solution)/shard_map/ppermute | solution.py:507
  91.1 11.9 %collective-permute-start.18 = (bf16[128,512]{1,0:T(8,128)(2,1)S(1)}, bf16[128,512]{1,0:T(8,128)(2,1)S(1)}, u32[]{:S(2)}, u32[]{:S(2)}) collective-permute-start(bf16[128,512]{1,0:T(8,128)(2,1)S(1)} %get-tuple-element.89), channel_id=1, source_target_pairs={{0,6},{1,7},{2,4},{3,5},{4,2},{5,3},{6,0},{7,1},{8,14},{9,15},{10,... | collective-permute-start | bytes 393224 | tf_op jit(solution)/shard_map/ppermute | solution.py:507
  93.9 9.1 %collective-permute-start.19 = (bf16[128,512]{1,0:T(8,128)(2,1)S(1)}, bf16[128,512]{1,0:T(8,128)(2,1)S(1)}, u32[]{:S(2)}, u32[]{:S(2)}) collective-permute-start(bf16[128,512]{1,0:T(8,128)(2,1)S(1)} %get-tuple-element.90), channel_id=1, source_target_pairs={{0,7},{1,6},{2,5},{3,4},{4,3},{5,2},{6,1},{7,0},{8,15},{9,14},{10,... | collective-permute-start | bytes 393224 | tf_op jit(solution)/shard_map/ppermute | solution.py:507

commit v4 on v3

--- a/solution.py
+++ b/solution.py
@@ -35,7 +35,12 @@
     return lax.dot_general(a, b, (((1,), (1,)), ((), ())), preferred_element_type=F32)
 
 
-def project(parts, heads_dev, npair, meta, own, other, w_qkv):
+def place():
+    seq = lax.axis_index("seq")
+    return seq // 2, lax.rem(seq, 2), lax.axis_index("cluster"), seq
+
+
+def project(parts, heads_dev, npair, own, other, w_qkv):
     rows = own.shape[0]
     group = 3 * HD * heads_dev
     shared = group % 128 != 0
@@ -45,11 +50,10 @@
     heights = [sum(n for _, n in part) for part in parts]
     total = sum(heights)
 
-    def body(meta_ref, own_ref, other_ref, w_ref, *refs):
+    def body(own_ref, other_ref, w_ref, *refs):
         outs = refs[: len(parts) * npair]
         x, w, wt, turned, made, sems = refs[len(parts) * npair :]
-        pair = meta_ref[0]
-        core = meta_ref[1]
+        pair, core = place()[:2]
         loads = []
         for j in range(npair):
             dest = pair ^ j
@@ -107,7 +111,7 @@
     outs = pl.pallas_call(
         body,
         out_shape=shapes,
-        in_specs=[SMEM, ANY, ANY, ANY],
+        in_specs=[ANY, ANY, ANY],
         out_specs=[ANY] * len(shapes),
         scratch_shapes=[
             pltpu.VMEM((2 * rows, D), BF16),
@@ -120,20 +124,19 @@
         compiler_params=params(55),
         cost_estimate=cost(2 * 2 * rows * D * total * npair, 4 * rows * D + 2 * D * width * npair),
         name="project",
-    )(meta, own, other, w_qkv)
+    )(own, other, w_qkv)
     return [list(outs[k * npair : (k + 1) * npair]) for k in range(len(parts))]
 
 
-def select(npair, ncl, cap, meta, asked, tables, row):
+def select(npair, ncl, cap, asked, tables, row):
     wide = tables[0].shape[1]
     per = wide // BLK
 
-    def body(meta_ref, asked_ref, *refs):
+    def body(asked_ref, *refs):
         tabs = refs[:npair]
         outs = refs[npair : npair + ncl - 1]
         held, in_sems, out_sems = refs[npair + ncl - 1 :]
-        pair = meta_ref[0]
-        cluster = meta_ref[2]
+        pair, _, cluster, _ = place()
         loads = [
             pltpu.make_async_copy(tabs[j].at[pl.ds(row, 2 * HD)], held.at[pair ^ j], in_sems.at[j])
             for j in range(npair)
@@ -163,7 +166,7 @@
     return pl.pallas_call(
         body,
         out_shape=[shape] * (ncl - 1),
-        in_specs=[SMEM, SMEM] + [ANY] * npair,
+        in_specs=[SMEM] + [ANY] * npair,
         out_specs=[ANY] * (ncl - 1),
         scratch_shapes=[
             pltpu.VMEM((npair, 2 * HD, wide), BF16),
@@ -173,7 +176,7 @@
         compiler_params=params(40),
         cost_estimate=cost(0, 4 * npair * 2 * HD * wide),
         name="select",
-    )(meta, asked, *tables)
+    )(asked, *tables)
 
 
 def query_matrix(heads_dev, q, per, b):
@@ -187,7 +190,7 @@
     return jnp.concatenate([left, right], axis=1)
 
 
-def near_attention(heads_dev, npair, meta, ids, first_kv, rest):
+def near_attention(heads_dev, npair, ids, first_kv, rest):
     wide = rest[0].shape[1]
     per = wide // BLK
     nblk = npair * per
@@ -196,12 +199,12 @@
     cols = heads_dev * BLK
     keys = NEAR * BLK
 
-    def body(meta_ref, ids_ref, *refs):
+    def body(ids_ref, *refs):
         tabs = refs[:npair]
         rests = refs[npair : 2 * npair]
         out_ref, stat_ref, kv, q, ktab, vtab, s_a, s_b, t_a, t_b, sems = refs[2 * npair :]
-        pair = meta_ref[0]
-        base = meta_ref[2] * nblk
+        pair, _, cluster, _ = place()
+        base = cluster * nblk
         loads = []
         for j in range(npair):
             at = pair ^ j
@@ -290,7 +293,7 @@
             jax.ShapeDtypeStruct((nblk, feats, BLK), F32),
             jax.ShapeDtypeStruct((nblk, 8, cols), F32),
         ],
-        in_specs=[SMEM, SMEM] + [ANY] * (2 * npair),
+        in_specs=[SMEM] + [ANY] * (2 * npair),
         out_specs=[VMEM, VMEM],
         scratch_shapes=[
             pltpu.VMEM((heads_dev, npair, 2 * HD, wide), BF16),
@@ -306,10 +309,10 @@
         compiler_params=params(40),
         cost_estimate=cost(2 * flops, 8 * nblk * BLK * feats, nblk * keys * cols),
         name="near_attention",
-    )(meta, ids, *first_kv, *rest)
-
-
-def far_attention(heads_dev, npair, seq_size, ncl, cap, meta, pos, counts, tables, rest, near, stats):
+    )(ids, *first_kv, *rest)
+
+
+def far_attention(heads_dev, npair, seq_size, ncl, cap, pos, counts, tables, rest, near, stats):
     wide = rest[0].shape[1]
     per = wide // BLK
     nblk = npair * per
@@ -320,16 +323,14 @@
     keys = REMOTE * BLK
     shifts = ncl - 1
 
-    def body(meta_ref, pos_ref, counts_ref, *refs):
+    def body(pos_ref, counts_ref, *refs):
         tabs = refs[: heads_dev * shifts]
         refs = refs[heads_dev * shifts :]
         rests = refs[:npair]
         near_ref, stat_ref = refs[npair : npair + 2]
         outs = refs[npair + 2 : npair + 2 + seq_size]
         kv, q, ktab, vtab, old, s_a, s_b, t_a, t_b, att, sems = refs[npair + 2 + seq_size :]
-        pair = meta_ref[0]
-        cluster = meta_ref[2]
-        seq = meta_ref[3]
+        pair, _, cluster, seq = place()
         loads = []
         for h in range(heads_dev):
             for s in range(shifts):
@@ -435,7 +436,7 @@
     return pl.pallas_call(
         body,
         out_shape=[jax.ShapeDtypeStruct((feats, dev_blocks * BLK), BF16)] * seq_size,
-        in_specs=[SMEM, SMEM, SMEM] + [ANY] * (heads_dev * shifts + npair) + [ANY, VMEM],
+        in_specs=[SMEM, SMEM] + [ANY] * (heads_dev * shifts + npair) + [ANY, VMEM],
         out_specs=[VMEM] * seq_size,
         scratch_shapes=[
             pltpu.VMEM((heads_dev, ncl * cap, 2 * HD, BLK), BF16),
@@ -453,17 +454,17 @@
         compiler_params=params(40),
         cost_estimate=cost(flops, 6 * nblk * BLK * feats, nblk * keys * cols),
         name="far_attention",
-    )(meta, pos, counts, *[x for t in tables for x in t], *rest, near, stats)
-
-
-def project_out(seq_size, meta, pieces, w_out):
+    )(pos, counts, *[x for t in tables for x in t], *rest, near, stats)
+
+
+def project_out(seq_size, pieces, w_out):
     feats, rows = pieces[0].shape
     step = 128
 
-    def body(meta_ref, *refs):
+    def body(*refs):
         parts = refs[:seq_size]
         w_ref, out_ref, at, out, sems = refs[seq_size:]
-        seq = meta_ref[3]
+        seq = place()[3]
         loads = []
         for k in range(seq_size):
             row = pl.multiple_of((seq ^ k) * feats, feats)
@@ -486,7 +487,7 @@
     return pl.pallas_call(
         body,
         out_shape=jax.ShapeDtypeStruct((rows, D), BF16),
-        in_specs=[SMEM] + [ANY] * seq_size + [VMEM],
+        in_specs=[ANY] * seq_size + [VMEM],
         out_specs=ANY,
         scratch_shapes=[
             pltpu.VMEM((HEADS * HD, rows), BF16),
@@ -496,7 +497,7 @@
         compiler_params=params(40),
         cost_estimate=cost(2 * rows * D * D, 2 * D * D + 4 * rows * D),
         name="project_out",
-    )(meta, *pieces, w_out)
+    )(*pieces, w_out)
 
 
 def shifted(x, axis, size, shift):
@@ -510,13 +511,7 @@
 def block_lists(ncl, nblk, slots, counts):
     cap = nblk // 4
 
-    def body(slots_ref, counts_ref, meta_ref, pos_ref, wanted_ref):
-        seq = lax.axis_index("seq")
-        cluster = lax.axis_index("cluster")
-        meta_ref[0] = seq // 2
-        meta_ref[1] = lax.rem(seq, 2)
-        meta_ref[2] = cluster
-        meta_ref[3] = seq
+    def body(slots_ref, counts_ref, pos_ref, wanted_ref):
         valid = [counts_ref[...] > NEAR + j for j in range(REMOTE)]
         ids = [slots_ref[NEAR + j : NEAR + j + 1, :] for j in range(REMOTE)]
         spot = [jnp.zeros((1, nblk), F32) for _ in range(REMOTE)]
@@ -543,12 +538,11 @@
     return pl.pallas_call(
         body,
         out_shape=[
-            jax.ShapeDtypeStruct((4,), jnp.int32),
             jax.ShapeDtypeStruct((REMOTE, nblk), jnp.int32),
             jax.ShapeDtypeStruct((ncl, 8, 128), jnp.int32),
         ],
         in_specs=[VMEM, VMEM],
-        out_specs=[SMEM, VMEM, VMEM],
+        out_specs=[VMEM, VMEM],
         compiler_params=params(40),
         cost_estimate=cost(0, 4096),
         name="block_lists",
@@ -577,20 +571,20 @@
     cap = nblk // 4
     other = crossed(nodes, seq_size, 1)
     slots = kv_ids.T
-    meta, pos, wanted = block_lists(ncl, nblk, slots, counts)
+    pos, wanted = block_lists(ncl, nblk, slots, counts)
     q_span = [(3 * h * HD, HD) for h in range(heads_dev)]
     spans = [[((3 * h + 1) * HD, 2 * HD)] for h in range(heads_dev)]
-    (first_kv,) = project(spans[:1], heads_dev, npair, meta, nodes, other, w_qkv)
-    wanted, first_kv = lax.optimization_barrier((wanted, first_kv))
+    (first_kv,) = project(spans[:1], heads_dev, npair, nodes, other, w_qkv)
+    wanted, first_kv[0] = lax.optimization_barrier((wanted, first_kv[0]))
     asked = lax.all_to_all(wanted, "cluster", split_axis=0, concat_axis=0, tiled=True)
-    (rest,) = project([sum(spans[1:] + [q_span], [])], heads_dev, npair, meta, nodes, other, w_qkv)
+    (rest,) = project([sum(spans[1:] + [q_span], [])], heads_dev, npair, nodes, other, w_qkv)
     asked, rest = lax.optimization_barrier((asked, rest))
     first_kv = exchange(first_kv, None, seq_size)
     rest = exchange(rest, first_kv, seq_size)
     far = []
     for h in range(heads_dev):
         tables, row = (first_kv, 0) if h == 0 else (rest, (h - 1) * 2 * HD)
-        picked = list(select(npair, ncl, cap, meta, asked, tables, row))
+        picked = list(select(npair, ncl, cap, asked, tables, row))
         gate = rest[-1] if h == 0 else far[h - 1][0]
         picked[-1], gate = lax.optimization_barrier((picked[-1], gate))
         if h == 0:
@@ -598,14 +592,14 @@
         else:
             far[h - 1][0] = gate
         far.append([shifted(x, "cluster", ncl, s + 1) for s, x in enumerate(picked)])
-    near, stats = near_attention(heads_dev, npair, meta, slots, first_kv, rest)
+    near, stats = near_attention(heads_dev, npair, slots, first_kv, rest)
     outs = far_attention(
-        heads_dev, npair, seq_size, ncl, cap, meta, pos, counts, far, rest, near, stats
+        heads_dev, npair, seq_size, ncl, cap, pos, counts, far, rest, near, stats
     )
     pieces = list(outs)
     for k in sorted(range(1, seq_size), key=lambda k: (-bin(k // 2).count("1"), k)):
         pieces[k] = crossed(pieces[k], seq_size, k)
-    return project_out(seq_size, meta, pieces, w_out)
+    return project_out(seq_size, pieces, w_out)
 
 
 def solution(mesh):

time: 108 us -> 106 us (0.981)
  waiting for transfers between devices: 29.2 us -> 31.5 us
  Pallas kernels: 42.2 us -> 40.3 us
  local copies, waits for them, and re-layouts: 3.9 us -> 2.03 us
    ppermute x14, waiting for transfers between devices: 22.6 us -> 24.8 us  [crossed(): return lax.ppermute(x, 'seq', [(i, i ^ k) for i in range(size)])]
    unnamed x22 -> x14, local copies, waits for them, and re-layouts: 3.9 us -> 2.03 us
    pallas_call x5, Pallas kernels: 16 us -> 14.7 us  [the longest x2 10.6 us: project(): pl.pallas_call(body, out_shape=shapes, in_specs=[ANY, ANY, ANY], out_spec...]
  transfers between devices with their start and end apart: 21 -> 21, of which waited for: 7 -> 8; matrix products, arithmetic and copies ran while one was open for 0% -> 0% of each run, Pallas kernels for 24% -> 24%
where the time goes in v4:
time: 106 us
  Pallas kernels  40.3 us (38%)
  starting transfers between devices  31.9 us (30%)
  waiting for transfers between devices  31.5 us (30%)
  local copies, waits for them, and re-layouts  2.03 us (2%)
    ppermute x14, waiting for transfers between devices, crossed(): return lax.ppermute(x, 'seq', [(i, i ^ k) for i in range(size)])  24.8 us
    pallas_call x1, Pallas kernels, near_attention(): pl.pallas_call(body, out_shape=[jax.ShapeDtypeStruct((nblk, feats, BLK),...  14.8 us
    ppermute x14, starting transfers between devices, crossed(): return lax.ppermute(x, 'seq', [(i, i ^ k) for i in range(size)])  14 us
    ppermute x6, starting transfers between devices, shifted(): return lax.ppermute(x, axis, [(i, (i + shift) % size) for i in range(size)])  13 us
    pallas_call x2, Pallas kernels, project(): pl.pallas_call(body, out_shape=shapes, in_specs=[ANY, ANY, ANY], out_spec...  10.6 us
    pallas_call x1, Pallas kernels, far_attention(): pl.pallas_call(body, out_shape=[jax.ShapeDtypeStruct((feats, dev_blocks *...  7.25 us
    ppermute x6, waiting for transfers between devices, shifted(): return lax.ppermute(x, axis, [(i, (i + shift) % size) for i in range(size)])  6.63 us
    all_to_all x1, starting transfers between devices, on_device(): lax.all_to_all(wanted, 'cluster', split_axis=0, concat_axis=0, tiled=True)  4.87 us
  transfers between devices with their start and end apart: 21, of which 8 were waited for; matrix products, arithmetic and copies ran while one was open for 0% of the time, Pallas kernels for 24%

profile of v4, /device:TPU:0, one launch (start us, length us, event | category | flops | bytes accessed | tf_op | source)
XLA Modules:
  0.0 105.9 jit_solution(14362837474218259966)
XLA Ops:
  0.0 0.0 copy-start.5
  0.0 0.0 copy-start.4
  0.0 0.5 collective-permute-start
  0.5 2.5 %collective-permute-done.other_ref = bf16[512,1024]{1,0:T(8,128)(2,1)S(1)} collective-permute-done((bf16[512,1024]{1,0:T(8,128)(2,1)}, bf16[512,1024]{1,0:T(8,128)(2,1)S(1)}, u32[]{:S(2)}, u32[]{:S(2)}) %collective-permute-start) | collective-permute-done | bytes 1048608 | tf_op jit(solution)/shard_map/ppermute | solution.py:508
  3.0 0.0 copy-start.6
  3.0 1.0 copy-done.6
  3.9 4.4 %project.2 = (bf16[128,1024]{1,0:T(8,128)(2,1)}, bf16[128,1024]{1,0:T(8,128)(2,1)}, bf16[128,1024]{1,0:T(8,128)(2,1)}, bf16[128,1024]{1,0:T(8,128)(2,1)}) custom-call(bf16[512,1024]{1,0:T(8,128)(2,1)} %own_ref.3, bf16[512,1024]{1,0:T(8,128)(2,1)} %copy-done.6, bf16[1024,3072]{1,0:T(8,128)(2,1)} %w_ref.3), custom_call_target="tpu_custom_call" | custom-call | flops 1073741824 | bytes 4194304 | tf_op jit(solution)/shard_map/project/pallas_call | solution.py:111
  8.4 3.9 %collective-permute-start.1 = (bf16[128,1024]{1,0:T(8,128)(2,1)}, bf16[128,1024]{1,0:T(8,128)(2,1)S(1)}, u32[]{:S(2)}, u32[]{:S(2)}) collective-permute-start(bf16[128,1024]{1,0:T(8,128)(2,1)} %get-tuple-element.55), channel_id=1, source_target_pairs={{0,6},{1,7},{2,4},{3,5},{4,2},{5,3},{6,0},{7,1},{8,14},{9,15},{10,... | collective-permute-start | bytes 786440 | tf_op jit(solution)/shard_map/ppermute | solution.py:508
  12.3 0.0 copy-done.5
  12.3 0.0 copy-done.4
  12.3 0.9 block_lists.1
  13.1 4.9 %all-to-all-start = ((s32[4,8,128]{2,1,0:T(8,128)}), s32[4,8,128]{2,1,0:T(8,128)S(1)}, u32[]{:S(2)}, u32[]{:S(2)}) async-start(s32[4,8,128]{2,1,0:T(8,128)} %get-tuple-element.47), calls=%async_computation | async-start | bytes 32768 | tf_op jit(solution)/shard_map/all_to_all | solution.py:579
  18.0 0.5 collective-permute-start.4
  18.5 0.0 copy-start.3
  18.5 0.5 collective-permute-start.5
  19.1 6.1 %project.3 = (bf16[256,1024]{1,0:T(8,128)(2,1)}, bf16[256,1024]{1,0:T(8,128)(2,1)}, bf16[256,1024]{1,0:T(8,128)(2,1)}, bf16[256,1024]{1,0:T(8,128)(2,1)}) custom-call(bf16[512,1024]{1,0:T(8,128)(2,1)} %own_ref.3, bf16[512,1024]{1,0:T(8,128)(2,1)} %copy-done.6, bf16[1024,3072]{1,0:T(8,128)(2,1)} %w_ref.3), custom_call_target="tpu_custom_call" | custom-call | flops 2147483648 | bytes 5242880 | tf_op jit(solution)/shard_map/project/pallas_call | solution.py:111
  25.2 0.0 copy-start.2
  25.2 0.0 all-to-all-done.asked_ref
  25.2 2.5 %collective-permute-start.6 = (bf16[256,1024]{1,0:T(8,128)(2,1)}, bf16[256,1024]{1,0:T(8,128)(2,1)S(1)}, u32[]{:S(2)}, u32[]{:S(2)}) collective-permute-start(bf16[256,1024]{1,0:T(8,128)(2,1)} %get-tuple-element.63), channel_id=1, source_target_pairs={{0,6},{1,7},{2,4},{3,5},{4,2},{5,3},{6,0},{7,1},{8,14},{9,15},{10,... | collective-permute-start | bytes 1572872 | tf_op jit(solution)/shard_map/ppermute | solution.py:508
  27.7 0.5 collective-permute-start.3
  28.2 0.0 collective-permute-done.1.refs_3_
  28.2 0.5 collective-permute-start.2
  28.8 0.0 collective-permute-done.4.refs_1_
  28.8 0.0 collective-permute-done.5.refs_2_
  28.8 0.0 copy-done.3
  28.8 1.6 %select.2 = (bf16[8,128,128]{2,1,0:T(8,128)(2,1)S(1)}, bf16[8,128,128]{2,1,0:T(8,128)(2,1)S(1)}, bf16[8,128,128]{2,1,0:T(8,128)(2,1)S(1)}) custom-call(s32[4,8,128]{2,1,0:T(8,128)S(1)} %all-to-all-done.asked_ref, bf16[128,1024]{1,0:T(8,128)(2,1)S(1)} %copy-done.3, bf16[128,1024]{1,0:T(8,128)(2,1)S(1)} %collective-permute-done.4.refs_1_, ...), custom_call_target="tpu_custom_call" | custom-call | bytes 2097152 | tf_op jit(solution)/shard_map/select/pallas_call | solution.py:166
  30.4 2.1 %collective-permute-start.7 = (bf16[8,128,128]{2,1,0:T(8,128)(2,1)S(1)}, bf16[8,128,128]{2,1,0:T(8,128)(2,1)S(1)}, u32[]{:S(2)}, u32[]{:S(2)}) collective-permute-start(bf16[8,128,128]{2,1,0:T(8,128)(2,1)S(1)} %get-tuple-element.66), channel_id=1, source_target_pairs={{0,8},{8,16},{16,24},{24,0},{1,9},{9,17},{17,25},{25,1},{2,10},{10... | collective-permute-start | bytes 786440 | tf_op jit(solution)/shard_map/ppermute | solution.py:504
  32.5 2.4 %collective-permute-start.8 = (bf16[8,128,128]{2,1,0:T(8,128)(2,1)S(1)}, bf16[8,128,128]{2,1,0:T(8,128)(2,1)S(1)}, u32[]{:S(2)}, u32[]{:S(2)}) collective-permute-start(bf16[8,128,128]{2,1,0:T(8,128)(2,1)S(1)} %get-tuple-element.68), channel_id=1, source_target_pairs={{0,16},{8,24},{16,0},{24,8},{1,17},{9,25},{17,1},{25,9},{2,18},{10... | collective-permute-start | bytes 786440 | tf_op jit(solution)/shard_map/ppermute | solution.py:504
  34.9 6.4 %collective-permute-done.6.refs_3_.refs_7_.refs_9_ = bf16[256,1024]{1,0:T(8,128)(2,1)S(1)} collective-permute-done((bf16[256,1024]{1,0:T(8,128)(2,1)}, bf16[256,1024]{1,0:T(8,128)(2,1)S(1)}, u32[]{:S(2)}, u32[]{:S(2)}) %collective-permute-start.6) | collective-permute-done | bytes 524320 | tf_op jit(solution)/shard_map/ppermute | solution.py:508
  41.3 3.8 %collective-permute-start.9 = (bf16[8,128,128]{2,1,0:T(8,128)(2,1)S(1)}, bf16[8,128,128]{2,1,0:T(8,128)(2,1)S(1)}, u32[]{:S(2)}, u32[]{:S(2)}) collective-permute-start(bf16[8,128,128]{2,1,0:T(8,128)(2,1)S(1)} %get-tuple-element.69), channel_id=1, source_target_pairs={{0,24},{8,0},{16,8},{24,16},{1,25},{9,1},{17,9},{25,17},{2,26},{10... | collective-permute-start | bytes 786440 | tf_op jit(solution)/shard_map/ppermute | solution.py:504
  45.1 5.3 %collective-permute-done.3.refs_2_.refs_6_.refs_8_ = bf16[256,1024]{1,0:T(8,128)(2,1)S(1)} collective-permute-done((bf16[256,1024]{1,0:T(8,128)(2,1)}, bf16[256,1024]{1,0:T(8,128)(2,1)S(1)}, u32[]{:S(2)}, u32[]{:S(2)}) %collective-permute-start.3) | collective-permute-done | bytes 524320 | tf_op jit(solution)/shard_map/ppermute | solution.py:508
  50.5 0.1 collective-permute-done.2.refs_1_.refs_5_.refs_7_
  50.6 0.0 copy-start.1
  50.6 1.0 copy-done.1
  51.6 1.6 %select.3 = (bf16[8,128,128]{2,1,0:T(8,128)(2,1)S(1)}, bf16[8,128,128]{2,1,0:T(8,128)(2,1)S(1)}, bf16[8,128,128]{2,1,0:T(8,128)(2,1)S(1)}) custom-call(s32[4,8,128]{2,1,0:T(8,128)S(1)} %all-to-all-done.asked_ref, bf16[256,1024]{1,0:T(8,128)(2,1)S(1)} %copy-done.1, bf16[256,1024]{1,0:T(8,128)(2,1)S(1)} %collective-permute-done.2.refs_1_.refs_5_.refs_7_, ...), custom_call_target="tpu_custom_call" | custom-call | bytes 2097152 | tf_op jit(solution)/shard_map/select/pallas_call | solution.py:166
  53.2 0.0 collective-permute-done.7.refs_0_
  53.3 3.6 %collective-permute-start.12 = (bf16[8,128,128]{2,1,0:T(8,128)(2,1)S(1)}, bf16[8,128,128]{2,1,0:T(8,128)(2,1)S(1)}, u32[]{:S(2)}, u32[]{:S(2)}) collective-permute-start(bf16[8,128,128]{2,1,0:T(8,128)(2,1)S(1)} %get-tuple-element.72), channel_id=1, source_target_pairs={{0,24},{8,0},{16,8},{24,16},{1,25},{9,1},{17,9},{25,17},{2,26},{10... | collective-permute-start | bytes 786440 | tf_op jit(solution)/shard_map/ppermute | solution.py:504
  56.8 0.0 collective-permute-start.10
  56.8 1.1 %collective-permute-start.11 = (bf16[8,128,128]{2,1,0:T(8,128)(2,1)S(1)}, bf16[8,128,128]{2,1,0:T(8,128)(2,1)S(1)}, u32[]{:S(2)}, u32[]{:S(2)}) collective-permute-start(bf16[8,128,128]{2,1,0:T(8,128)(2,1)S(1)} %get-tuple-element.71), channel_id=1, source_target_pairs={{0,16},{8,24},{16,0},{24,8},{1,17},{9,25},{17,1},{25,9},{2,18},{10... | collective-permute-start | bytes 786440 | tf_op jit(solution)/shard_map/ppermute | solution.py:504
  58.0 0.0 copy-done.2
  58.0 14.8 %near_attention.1 = (f32[32,128,128]{2,1,0:T(8,128)S(1)}, f32[32,8,256]{2,1,0:T(8,128)S(1)}) custom-call(s32[16,32]{1,0:T(8,128)S(1)} %bitcast.3, bf16[128,1024]{1,0:T(8,128)(2,1)S(1)} %copy-done.3, bf16[128,1024]{1,0:T(8,128)(2,1)S(1)} %collective-permute-done.4.refs_1_, bf16[128,1024]{1,0:T(8,128)(2,1)S(1)} %collective-permute-done.5.refs_2_, ...), custom_call_target="tpu_custom_call" | custom-call | flops 12884901888 | bytes 4194304 | tf_op jit(solution)/shard_map/near_attention/pallas_call | solution.py:290
  72.8 0.0 collective-permute-done.8.refs_1_
  72.8 0.0 collective-permute-done.9.refs_2_
  72.8 0.0 collective-permute-done.12.refs_5_
  72.8 0.0 collective-permute-done.10.refs_3_
  72.9 6.6 %collective-permute-done.11.refs_4_ = bf16[8,128,128]{2,1,0:T(8,128)(2,1)S(1)} collective-permute-done((bf16[8,128,128]{2,1,0:T(8,128)(2,1)S(1)}, bf16[8,128,128]{2,1,0:T(8,128)(2,1)S(1)}, u32[]{:S(2)}, u32[]{:S(2)}) %collective-permute-start.11) | collective-permute-done | bytes 262176 | tf_op jit(solution)/shard_map/ppermute | solution.py:504
  79.5 0.0 copy-start
  79.5 7.2 %far_attention.1 = (bf16[128,512]{1,0:T(8,128)(2,1)S(1)}, bf16[128,512]{1,0:T(8,128)(2,1)S(1)}, bf16[128,512]{1,0:T(8,128)(2,1)S(1)}, bf16[128,512]{1,0:T(8,128)...) custom-call(s32[4,32]{1,0:T(4,128)S(1)} %get-tuple-element.44.pos_re, ...), custom_call_target="tpu_custom_call" | custom-call | flops 2147483648 | bytes 3145728 | tf_op jit(solution)/shard_map/far_attention/pallas_call | solution.py:436
  86.7 0.1 collective-permute-start.13
  86.8 1.5 %collective-permute-start.14 = (bf16[128,512]{1,0:T(8,128)(2,1)S(1)}, bf16[128,512]{1,0:T(8,128)(2,1)S(1)}, u32[]{:S(2)}, u32[]{:S(2)}) collective-permute-start(bf16[128,512]{1,0:T(8,128)(2,1)S(1)} %get-tuple-element.77), channel_id=1, source_target_pairs={{0,2},{1,3},{2,0},{3,1},{4,6},{5,7},{6,4},{7,5},{8,10},{9,11},{10,... | collective-permute-start | bytes 393224 | tf_op jit(solution)/shard_map/ppermute | solution.py:508
  88.4 0.3 collective-permute-start.15
  88.7 1.5 %collective-permute-start.16 = (bf16[128,512]{1,0:T(8,128)(2,1)S(1)}, bf16[128,512]{1,0:T(8,128)(2,1)S(1)}, u32[]{:S(2)}, u32[]{:S(2)}) collective-permute-start(bf16[128,512]{1,0:T(8,128)(2,1)S(1)} %get-tuple-element.79), channel_id=1, source_target_pairs={{0,4},{1,5},{2,6},{3,7},{4,0},{5,1},{6,2},{7,3},{8,12},{9,13},{10,... | collective-permute-start | bytes 393224 | tf_op jit(solution)/shard_map/ppermute | solution.py:508
  90.2 0.2 collective-permute-start.17
  90.4 0.0 collective-permute-done.13.refs_1_
  90.4 1.3 %collective-permute-start.18 = (bf16[128,512]{1,0:T(8,128)(2,1)S(1)}, bf16[128,512]{1,0:T(8,128)(2,1)S(1)}, u32[]{:S(2)}, u32[]{:S(2)}) collective-permute-start(bf16[128,512]{1,0:T(8,128)(2,1)S(1)} %get-tuple-element.81), channel_id=1, source_target_pairs={{0,6},{1,7},{2,4},{3,5},{4,2},{5,3},{6,0},{7,1},{8,14},{9,15},{10,... | collective-permute-start | bytes 393224 | tf_op jit(solution)/shard_map/ppermute | solution.py:508
  91.6 1.5 %collective-permute-done.14.refs_2_ = bf16[128,512]{1,0:T(8,128)(2,1)S(1)} collective-permute-done((bf16[128,512]{1,0:T(8,128)(2,1)S(1)}, bf16[128,512]{1,0:T(8,128)(2,1)S(1)}, u32[]{:S(2)}, u32[]{:S(2)}) %collective-permute-start.14) | collective-permute-done | bytes 131104 | tf_op jit(solution)/shard_map/ppermute | solution.py:508
  93.2 0.2 collective-permute-start.19
  93.4 1.7 %collective-permute-done.15.refs_3_ = bf16[128,512]{1,0:T(8,128)(2,1)S(1)} collective-permute-done((bf16[128,512]{1,0:T(8,128)(2,1)S(1)}, bf16[128,512]{1,0:T(8,128)(2,1)S(1)}, u32[]{:S(2)}, u32[]{:S(2)}) %collective-permute-start.15) | collective-permute-done | bytes 131104 | tf_op jit(solution)/shard_map/ppermute | solution.py:508
  95.1 0.0 collective-permute-done.16.refs_4_
  95.1 7.2 %collective-permute-done.17.refs_5_ = bf16[128,512]{1,0:T(8,128)(2,1)S(1)} collective-permute-done((bf16[128,512]{1,0:T(8,128)(2,1)S(1)}, bf16[128,512]{1,0:T(8,128)(2,1)S(1)}, u32[]{:S(2)}, u32[]{:S(2)}) %collective-permute-start.17) | collective-permute-done | bytes 131104 | tf_op jit(solution)/shard_map/ppermute | solution.py:508
  102.3 0.0 collective-permute-done.18.refs_6_
  102.3 0.0 collective-permute-done.19.refs_7_
  102.3 0.0 copy-done
  102.3 3.5 %project_out.1 = bf16[512,1024]{1,0:T(8,128)(2,1)} custom-call(bf16[128,512]{1,0:T(8,128)(2,1)S(1)} %get-tuple-element.75.refs_0_, bf16[128,512]{1,0:T(8,128)(2,1)S(1)} %collective-permute-done.13.refs_1_, bf16[128,512]{1,0:T(8,128)(2,1)S(1)} %collective-permute-done.14.refs_2_, bf16[128,512]{1,0:T(8,128)(2,1)S(1)} %collective-permute-done.15.refs_3_, ...), custom_call_target="tpu_custom_call" | custom-call | flops 1073741824 | bytes 4194304 | tf_op jit(solution)/shard_map/project_out/pallas_call | solution.py:487
Async XLA Ops:
  0.0 12.3 %copy-start.5 = (s32[32]{0:T(128)S(1)}, s32[32]{0:T(128)}, u32[]{:S(2)}) copy-start(s32[32]{0:T(128)} %counts_ref.1) | copy-start | bytes 388
  0.0 12.3 %copy-start.4 = (s32[32,16]{0,1:T(8,128)S(1)}, s32[32,16]{0,1:T(8,128)}, u32[]{:S(2)}) copy-start(s32[32,16]{0,1:T(8,128)} %param.8) | copy-start | bytes 6148
  0.0 3.0 %collective-permute-start = (bf16[512,1024]{1,0:T(8,128)(2,1)}, bf16[512,1024]{1,0:T(8,128)(2,1)S(1)}, u32[]{:S(2)}, u32[]{:S(2)}) collective-permute-start(bf16[512,1024]{1,0:T(8,128)(2,1)} %own_ref.3), channel_id=1, source_target_pairs={{0,1},{1,0},{2,3},{3,2},{4,5},{5,4},{6,7},{7,6},{8,9},{9,8},{10,11... | collective-permute-start | bytes 3145736 | tf_op jit(solution)/shard_map/ppermute | solution.py:508
  3.0 1.0 copy-start.6
  8.4 19.9 %collective-permute-start.1 = (bf16[128,1024]{1,0:T(8,128)(2,1)}, bf16[128,1024]{1,0:T(8,128)(2,1)S(1)}, u32[]{:S(2)}, u32[]{:S(2)}) collective-permute-start(bf16[128,1024]{1,0:T(8,128)(2,1)} %get-tuple-element.55), channel_id=1, source_target_pairs={{0,6},{1,7},{2,4},{3,5},{4,2},{5,3},{6,0},{7,1},{8,14},{9,15},{10,... | collective-permute-start | bytes 786440 | tf_op jit(solution)/shard_map/ppermute | solution.py:508
  13.1 12.1 %all-to-all-start = ((s32[4,8,128]{2,1,0:T(8,128)}), s32[4,8,128]{2,1,0:T(8,128)S(1)}, u32[]{:S(2)}, u32[]{:S(2)}) async-start(s32[4,8,128]{2,1,0:T(8,128)} %get-tuple-element.47), calls=%async_computation | async-start | bytes 32768 | tf_op jit(solution)/shard_map/all_to_all | solution.py:579
  18.0 10.8 %collective-permute-start.4 = (bf16[128,1024]{1,0:T(8,128)(2,1)}, bf16[128,1024]{1,0:T(8,128)(2,1)S(1)}, u32[]{:S(2)}, u32[]{:S(2)}) collective-permute-start(bf16[128,1024]{1,0:T(8,128)(2,1)} %get-tuple-element.59), channel_id=1, source_target_pairs={{0,2},{1,3},{2,0},{3,1},{4,6},{5,7},{6,4},{7,5},{8,10},{9,11},{10,... | collective-permute-start | bytes 786440 | tf_op jit(solution)/shard_map/ppermute | solution.py:508
  18.5 10.2 %copy-start.3 = (bf16[128,1024]{1,0:T(8,128)(2,1)S(1)}, bf16[128,1024]{1,0:T(8,128)(2,1)}, u32[]{:S(2)}) copy-start(bf16[128,1024]{1,0:T(8,128)(2,1)} %get-tuple-element.58.refs_0_) | copy-start | bytes 786436
  18.5 10.2 %collective-permute-start.5 = (bf16[128,1024]{1,0:T(8,128)(2,1)}, bf16[128,1024]{1,0:T(8,128)(2,1)S(1)}, u32[]{:S(2)}, u32[]{:S(2)}) collective-permute-start(bf16[128,1024]{1,0:T(8,128)(2,1)} %get-tuple-element.60), channel_id=1, source_target_pairs={{0,4},{1,5},{2,6},{3,7},{4,0},{5,1},{6,2},{7,3},{8,12},{9,13},{10,... | collective-permute-start | bytes 786440 | tf_op jit(solution)/shard_map/ppermute | solution.py:508
  25.2 32.8 %copy-start.2 = (bf16[256,1024]{1,0:T(8,128)(2,1)S(1)}, bf16[256,1024]{1,0:T(8,128)(2,1)}, u32[]{:S(2)}) copy-start(bf16[256,1024]{1,0:T(8,128)(2,1)} %get-tuple-element.53.refs_0_.refs_4_.refs_6_) | copy-start | bytes 1572868
  25.2 16.1 %collective-permute-start.6 = (bf16[256,1024]{1,0:T(8,128)(2,1)}, bf16[256,1024]{1,0:T(8,128)(2,1)S(1)}, u32[]{:S(2)}, u32[]{:S(2)}) collective-permute-start(bf16[256,1024]{1,0:T(8,128)(2,1)} %get-tuple-element.63), channel_id=1, source_target_pairs={{0,6},{1,7},{2,4},{3,5},{4,2},{5,3},{6,0},{7,1},{8,14},{9,15},{10,... | collective-permute-start | bytes 1572872 | tf_op jit(solution)/shard_map/ppermute | solution.py:508
  27.7 22.7 %collective-permute-start.3 = (bf16[256,1024]{1,0:T(8,128)(2,1)}, bf16[256,1024]{1,0:T(8,128)(2,1)S(1)}, u32[]{:S(2)}, u32[]{:S(2)}) collective-permute-start(bf16[256,1024]{1,0:T(8,128)(2,1)} %get-tuple-element.57), channel_id=1, source_target_pairs={{0,4},{1,5},{2,6},{3,7},{4,0},{5,1},{6,2},{7,3},{8,12},{9,13},{10,... | collective-permute-start | bytes 1572872 | tf_op jit(solution)/shard_map/ppermute | solution.py:508
  28.2 22.3 %collective-permute-start.2 = (bf16[256,1024]{1,0:T(8,128)(2,1)}, bf16[256,1024]{1,0:T(8,128)(2,1)S(1)}, u32[]{:S(2)}, u32[]{:S(2)}) collective-permute-start(bf16[256,1024]{1,0:T(8,128)(2,1)} %get-tuple-element.56), channel_id=1, source_target_pairs={{0,2},{1,3},{2,0},{3,1},{4,6},{5,7},{6,4},{7,5},{8,10},{9,11},{10,... | collective-permute-start | bytes 1572872 | tf_op jit(solution)/shard_map/ppermute | solution.py:508
  30.4 22.8 %collective-permute-start.7 = (bf16[8,128,128]{2,1,0:T(8,128)(2,1)S(1)}, bf16[8,128,128]{2,1,0:T(8,128)(2,1)S(1)}, u32[]{:S(2)}, u32[]{:S(2)}) collective-permute-start(bf16[8,128,128]{2,1,0:T(8,128)(2,1)S(1)} %get-tuple-element.66), channel_id=1, source_target_pairs={{0,8},{8,16},{16,24},{24,0},{1,9},{9,17},{17,25},{25,1},{2,10},{10... | collective-permute-start | bytes 786440 | tf_op jit(solution)/shard_map/ppermute | solution.py:504
  32.5 40.3 %collective-permute-start.8 = (bf16[8,128,128]{2,1,0:T(8,128)(2,1)S(1)}, bf16[8,128,128]{2,1,0:T(8,128)(2,1)S(1)}, u32[]{:S(2)}, u32[]{:S(2)}) collective-permute-start(bf16[8,128,128]{2,1,0:T(8,128)(2,1)S(1)} %get-tuple-element.68), channel_id=1, source_target_pairs={{0,16},{8,24},{16,0},{24,8},{1,17},{9,25},{17,1},{25,9},{2,18},{10... | collective-permute-start | bytes 786440 | tf_op jit(solution)/shard_map/ppermute | solution.py:504
  41.3 31.5 %collective-permute-start.9 = (bf16[8,128,128]{2,1,0:T(8,128)(2,1)S(1)}, bf16[8,128,128]{2,1,0:T(8,128)(2,1)S(1)}, u32[]{:S(2)}, u32[]{:S(2)}) collective-permute-start(bf16[8,128,128]{2,1,0:T(8,128)(2,1)S(1)} %get-tuple-element.69), channel_id=1, source_target_pairs={{0,24},{8,0},{16,8},{24,16},{1,25},{9,1},{17,9},{25,17},{2,26},{10... | collective-permute-start | bytes 786440 | tf_op jit(solution)/shard_map/ppermute | solution.py:504
  50.6 1.0 copy-start.1
  53.3 19.6 %collective-permute-start.12 = (bf16[8,128,128]{2,1,0:T(8,128)(2,1)S(1)}, bf16[8,128,128]{2,1,0:T(8,128)(2,1)S(1)}, u32[]{:S(2)}, u32[]{:S(2)}) collective-permute-start(bf16[8,128,128]{2,1,0:T(8,128)(2,1)S(1)} %get-tuple-element.72), channel_id=1, source_target_pairs={{0,24},{8,0},{16,8},{24,16},{1,25},{9,1},{17,9},{25,17},{2,26},{10... | collective-permute-start | bytes 786440 | tf_op jit(solution)/shard_map/ppermute | solution.py:504
  56.8 16.0 %collective-permute-start.10 = (bf16[8,128,128]{2,1,0:T(8,128)(2,1)S(1)}, bf16[8,128,128]{2,1,0:T(8,128)(2,1)S(1)}, u32[]{:S(2)}, u32[]{:S(2)}) collective-permute-start(bf16[8,128,128]{2,1,0:T(8,128)(2,1)S(1)} %get-tuple-element.70), channel_id=1, source_target_pairs={{0,8},{8,16},{16,24},{24,0},{1,9},{9,17},{17,25},{25,1},{2,10},{10... | collective-permute-start | bytes 786440 | tf_op jit(solution)/shard_map/ppermute | solution.py:504
  56.8 22.6 %collective-permute-start.11 = (bf16[8,128,128]{2,1,0:T(8,128)(2,1)S(1)}, bf16[8,128,128]{2,1,0:T(8,128)(2,1)S(1)}, u32[]{:S(2)}, u32[]{:S(2)}) collective-permute-start(bf16[8,128,128]{2,1,0:T(8,128)(2,1)S(1)} %get-tuple-element.71), channel_id=1, source_target_pairs={{0,16},{8,24},{16,0},{24,8},{1,17},{9,25},{17,1},{25,9},{2,18},{10... | collective-permute-start | bytes 786440 | tf_op jit(solution)/shard_map/ppermute | solution.py:504
  79.5 22.8 %copy-start = (bf16[1024,1024]{1,0:T(8,128)(2,1)S(1)}, bf16[1024,1024]{1,0:T(8,128)(2,1)}, u32[]{:S(2)}) copy-start(bf16[1024,1024]{1,0:T(8,128)(2,1)} %refs_8_.1) | copy-start | bytes 6291460
  86.7 3.6 %collective-permute-start.13 = (bf16[128,512]{1,0:T(8,128)(2,1)S(1)}, bf16[128,512]{1,0:T(8,128)(2,1)S(1)}, u32[]{:S(2)}, u32[]{:S(2)}) collective-permute-start(bf16[128,512]{1,0:T(8,128)(2,1)S(1)} %get-tuple-element.76), channel_id=1, source_target_pairs={{0,1},{1,0},{2,3},{3,2},{4,5},{5,4},{6,7},{7,6},{8,9},{9,8},{10,11... | collective-permute-start | bytes 393224 | tf_op jit(solution)/shard_map/ppermute | solution.py:508
  86.8 6.4 %collective-permute-start.14 = (bf16[128,512]{1,0:T(8,128)(2,1)S(1)}, bf16[128,512]{1,0:T(8,128)(2,1)S(1)}, u32[]{:S(2)}, u32[]{:S(2)}) collective-permute-start(bf16[128,512]{1,0:T(8,128)(2,1)S(1)} %get-tuple-element.77), channel_id=1, source_target_pairs={{0,2},{1,3},{2,0},{3,1},{4,6},{5,7},{6,4},{7,5},{8,10},{9,11},{10,... | collective-permute-start | bytes 393224 | tf_op jit(solution)/shard_map/ppermute | solution.py:508
  88.4 6.7 %collective-permute-start.15 = (bf16[128,512]{1,0:T(8,128)(2,1)S(1)}, bf16[128,512]{1,0:T(8,128)(2,1)S(1)}, u32[]{:S(2)}, u32[]{:S(2)}) collective-permute-start(bf16[128,512]{1,0:T(8,128)(2,1)S(1)} %get-tuple-element.78), channel_id=1, source_target_pairs={{0,3},{1,2},{2,1},{3,0},{4,7},{5,6},{6,5},{7,4},{8,11},{9,10},{10,... | collective-permute-start | bytes 393224 | tf_op jit(solution)/shard_map/ppermute | solution.py:508
  88.7 6.4 %collective-permute-start.16 = (bf16[128,512]{1,0:T(8,128)(2,1)S(1)}, bf16[128,512]{1,0:T(8,128)(2,1)S(1)}, u32[]{:S(2)}, u32[]{:S(2)}) collective-permute-start(bf16[128,512]{1,0:T(8,128)(2,1)S(1)} %get-tuple-element.79), channel_id=1, source_target_pairs={{0,4},{1,5},{2,6},{3,7},{4,0},{5,1},{6,2},{7,3},{8,12},{9,13},{10,... | collective-permute-start | bytes 393224 | tf_op jit(solution)/shard_map/ppermute | solution.py:508
  90.2 12.1 %collective-permute-start.17 = (bf16[128,512]{1,0:T(8,128)(2,1)S(1)}, bf16[128,512]{1,0:T(8,128)(2,1)S(1)}, u32[]{:S(2)}, u32[]{:S(2)}) collective-permute-start(bf16[128,512]{1,0:T(8,128)(2,1)S(1)} %get-tuple-element.80), channel_id=1, source_target_pairs={{0,5},{1,4},{2,7},{3,6},{4,1},{5,0},{6,3},{7,2},{8,13},{9,12},{10,... | collective-permute-start | bytes 393224 | tf_op jit(solution)/shard_map/ppermute | solution.py:508
  90.4 11.9 %collective-permute-start.18 = (bf16[128,512]{1,0:T(8,128)(2,1)S(1)}, bf16[128,512]{1,0:T(8,128)(2,1)S(1)}, u32[]{:S(2)}, u32[]{:S(2)}) collective-permute-start(bf16[128,512]{1,0:T(8,128)(2,1)S(1)} %get-tuple-element.81), channel_id=1, source_target_pairs={{0,6},{1,7},{2,4},{3,5},{4,2},{5,3},{6,0},{7,1},{8,14},{9,15},{10,... | collective-permute-start | bytes 393224 | tf_op jit(solution)/shard_map/ppermute | solution.py:508
  93.2 9.1 %collective-permute-start.19 = (bf16[128,512]{1,0:T(8,128)(2,1)S(1)}, bf16[128,512]{1,0:T(8,128)(2,1)S(1)}, u32[]{:S(2)}, u32[]{:S(2)}) collective-permute-start(bf16[128,512]{1,0:T(8,128)(2,1)S(1)} %get-tuple-element.82), channel_id=1, source_target_pairs={{0,7},{1,6},{2,5},{3,4},{4,3},{5,2},{6,1},{7,0},{8,15},{9,14},{10,... | collective-permute-start | bytes 393224 | tf_op jit(solution)/shard_map/ppermute | solution.py:508

commit v5 on v4

--- a/solution.py
+++ b/solution.py
@@ -585,13 +585,15 @@
     for h in range(heads_dev):
         tables, row = (first_kv, 0) if h == 0 else (rest, (h - 1) * 2 * HD)
         picked = list(select(npair, ncl, cap, asked, tables, row))
-        gate = rest[-1] if h == 0 else far[h - 1][0]
-        picked[-1], gate = lax.optimization_barrier((picked[-1], gate))
-        if h == 0:
-            rest[-1] = gate
+        order = sorted(range(ncl - 1), key=lambda s: (abs(2 * s + 2 - ncl), -s))
+        last = order[-1]
+        if h:
+            picked[last], far[h - 1][order[1]] = lax.optimization_barrier((picked[last], far[h - 1][order[1]]))
         else:
-            far[h - 1][0] = gate
-        far.append([shifted(x, "cluster", ncl, s + 1) for s, x in enumerate(picked)])
+            picked[last], rest[-1] = lax.optimization_barrier((picked[last], rest[-1]))
+        for s in order:
+            picked[s] = shifted(picked[s], "cluster", ncl, s + 1)
+        far.append(picked)
     near, stats = near_attention(heads_dev, npair, slots, first_kv, rest)
     outs = far_attention(
         heads_dev, npair, seq_size, ncl, cap, pos, counts, far, rest, near, stats

time: 106 us -> 105 us (level)
  the two profiles are of different devices: /device:TPU:0 before, /device:TPU:9 now
where the time goes in v5:
time: 105 us
  Pallas kernels  40.3 us (38%)
  waiting for transfers between devices  37 us (35%)
  starting transfers between devices  25.1 us (24%)
  local copies, waits for them, and re-layouts  2.03 us (2%)
    ppermute x14, waiting for transfers between devices, crossed(): return lax.ppermute(x, 'seq', [(i, i ^ k) for i in range(size)])  29.7 us
    pallas_call x1, Pallas kernels, near_attention(): pl.pallas_call(body, out_shape=[jax.ShapeDtypeStruct((nblk, feats, BLK),...  14.8 us
    ppermute x14, starting transfers between devices, crossed(): return lax.ppermute(x, 'seq', [(i, i ^ k) for i in range(size)])  13.1 us
    pallas_call x2, Pallas kernels, project(): pl.pallas_call(body, out_shape=shapes, in_specs=[ANY, ANY, ANY], out_spec...  10.6 us
    ppermute x6, waiting for transfers between devices, shifted(): return lax.ppermute(x, axis, [(i, (i + shift) % size) for i in range(size)])  7.33 us
    pallas_call x1, Pallas kernels, far_attention(): pl.pallas_call(body, out_shape=[jax.ShapeDtypeStruct((feats, dev_blocks *...  7.25 us
    ppermute x6, starting transfers between devices, shifted(): return lax.ppermute(x, axis, [(i, (i + shift) % size) for i in range(size)])  7.19 us
    all_to_all x1, starting transfers between devices, on_device(): lax.all_to_all(wanted, 'cluster', split_axis=0, concat_axis=0, tiled=True)  4.76 us
  transfers between devices with their start and end apart: 21, of which 8 were waited for; matrix products, arithmetic and copies ran while one was open for 0% of the time, Pallas kernels for 24%

profile of v5, /device:TPU:9, one launch (start us, length us, event | category | flops | bytes accessed | tf_op | source)
XLA Modules:
  0.0 104.7 jit_solution(13770027183330042514)
XLA Ops:
  0.0 0.0 copy-start.5
  0.0 0.0 copy-start.4
  0.0 0.7 collective-permute-start
  0.7 2.5 %collective-permute-done.other_ref = bf16[512,1024]{1,0:T(8,128)(2,1)S(1)} collective-permute-done((bf16[512,1024]{1,0:T(8,128)(2,1)}, bf16[512,1024]{1,0:T(8,128)(2,1)S(1)}, u32[]{:S(2)}, u32[]{:S(2)}) %collective-permute-start) | collective-permute-done | bytes 1048608 | tf_op jit(solution)/shard_map/ppermute | solution.py:508
  3.2 0.0 copy-start.6
  3.2 1.0 copy-done.6
  4.1 4.4 %project.2 = (bf16[128,1024]{1,0:T(8,128)(2,1)}, bf16[128,1024]{1,0:T(8,128)(2,1)}, bf16[128,1024]{1,0:T(8,128)(2,1)}, bf16[128,1024]{1,0:T(8,128)(2,1)}) custom-call(bf16[512,1024]{1,0:T(8,128)(2,1)} %own_ref.3, bf16[512,1024]{1,0:T(8,128)(2,1)} %copy-done.6, bf16[1024,3072]{1,0:T(8,128)(2,1)} %w_ref.3), custom_call_target="tpu_custom_call" | custom-call | flops 1073741824 | bytes 4194304 | tf_op jit(solution)/shard_map/project/pallas_call | solution.py:111
  8.6 2.2 %collective-permute-start.3 = (bf16[128,1024]{1,0:T(8,128)(2,1)}, bf16[128,1024]{1,0:T(8,128)(2,1)S(1)}, u32[]{:S(2)}, u32[]{:S(2)}) collective-permute-start(bf16[128,1024]{1,0:T(8,128)(2,1)} %get-tuple-element.57), channel_id=1, source_target_pairs={{0,6},{1,7},{2,4},{3,5},{4,2},{5,3},{6,0},{7,1},{8,14},{9,15},{10,... | collective-permute-start | bytes 786440 | tf_op jit(solution)/shard_map/ppermute | solution.py:508
  10.8 0.0 copy-done.5
  10.8 0.0 copy-done.4
  10.8 0.9 block_lists.1
  11.7 4.8 %all-to-all-start = ((s32[4,8,128]{2,1,0:T(8,128)}), s32[4,8,128]{2,1,0:T(8,128)S(1)}, u32[]{:S(2)}, u32[]{:S(2)}) async-start(s32[4,8,128]{2,1,0:T(8,128)} %get-tuple-element.47), calls=%async_computation | async-start | bytes 32768 | tf_op jit(solution)/shard_map/all_to_all | solution.py:579
  16.5 0.3 collective-permute-start.1
  16.7 0.0 copy-start.3
  16.7 0.2 collective-permute-start.2
  17.0 6.1 %project.3 = (bf16[256,1024]{1,0:T(8,128)(2,1)}, bf16[256,1024]{1,0:T(8,128)(2,1)}, bf16[256,1024]{1,0:T(8,128)(2,1)}, bf16[256,1024]{1,0:T(8,128)(2,1)}) custom-call(bf16[512,1024]{1,0:T(8,128)(2,1)} %own_ref.3, bf16[512,1024]{1,0:T(8,128)(2,1)} %copy-done.6, bf16[1024,3072]{1,0:T(8,128)(2,1)} %w_ref.3), custom_call_target="tpu_custom_call" | custom-call | flops 2147483648 | bytes 5242880 | tf_op jit(solution)/shard_map/project/pallas_call | solution.py:111
  23.1 0.0 copy-start.2
  23.1 0.0 all-to-all-done.asked_ref
  23.1 2.2 %collective-permute-start.4 = (bf16[256,1024]{1,0:T(8,128)(2,1)}, bf16[256,1024]{1,0:T(8,128)(2,1)S(1)}, u32[]{:S(2)}, u32[]{:S(2)}) collective-permute-start(bf16[256,1024]{1,0:T(8,128)(2,1)} %get-tuple-element.60), channel_id=1, source_target_pairs={{0,6},{1,7},{2,4},{3,5},{4,2},{5,3},{6,0},{7,1},{8,14},{9,15},{10,... | collective-permute-start | bytes 1572872 | tf_op jit(solution)/shard_map/ppermute | solution.py:508
  25.3 0.2 collective-permute-start.8
  25.6 0.0 collective-permute-done.3.refs_3_
  25.6 0.3 collective-permute-start.7
  25.8 0.0 collective-permute-done.1.refs_1_
  25.8 0.0 collective-permute-done.2.refs_2_
  25.8 0.0 copy-done.3
  25.8 1.6 %select.2 = (bf16[8,128,128]{2,1,0:T(8,128)(2,1)S(1)}, bf16[8,128,128]{2,1,0:T(8,128)(2,1)S(1)}, bf16[8,128,128]{2,1,0:T(8,128)(2,1)S(1)}) custom-call(s32[4,8,128]{2,1,0:T(8,128)S(1)} %all-to-all-done.asked_ref, bf16[128,1024]{1,0:T(8,128)(2,1)S(1)} %copy-done.3, bf16[128,1024]{1,0:T(8,128)(2,1)S(1)} %collective-permute-done.1.refs_1_, ...), custom_call_target="tpu_custom_call" | custom-call | bytes 2097152 | tf_op jit(solution)/shard_map/select/pallas_call | solution.py:166
  27.5 0.1 collective-permute-start.9
  27.5 2.3 %collective-permute-start.6 = (bf16[8,128,128]{2,1,0:T(8,128)(2,1)S(1)}, bf16[8,128,128]{2,1,0:T(8,128)(2,1)S(1)}, u32[]{:S(2)}, u32[]{:S(2)}) collective-permute-start(bf16[8,128,128]{2,1,0:T(8,128)(2,1)S(1)} %get-tuple-element.62), channel_id=1, source_target_pairs={{0,16},{8,24},{16,0},{24,8},{1,17},{9,25},{17,1},{25,9},{2,18},{10... | collective-permute-start | bytes 786440 | tf_op jit(solution)/shard_map/ppermute | solution.py:504
  29.9 6.1 %collective-permute-done.4.refs_3_.refs_7_.refs_9_ = bf16[256,1024]{1,0:T(8,128)(2,1)S(1)} collective-permute-done((bf16[256,1024]{1,0:T(8,128)(2,1)}, bf16[256,1024]{1,0:T(8,128)(2,1)S(1)}, u32[]{:S(2)}, u32[]{:S(2)}) %collective-permute-start.4) | collective-permute-done | bytes 524320 | tf_op jit(solution)/shard_map/ppermute | solution.py:508
  36.0 1.2 %collective-permute-start.5 = (bf16[8,128,128]{2,1,0:T(8,128)(2,1)S(1)}, bf16[8,128,128]{2,1,0:T(8,128)(2,1)S(1)}, u32[]{:S(2)}, u32[]{:S(2)}) collective-permute-start(bf16[8,128,128]{2,1,0:T(8,128)(2,1)S(1)} %get-tuple-element.61), channel_id=1, source_target_pairs={{0,8},{8,16},{16,24},{24,0},{1,9},{9,17},{17,25},{25,1},{2,10},{10... | collective-permute-start | bytes 786440 | tf_op jit(solution)/shard_map/ppermute | solution.py:504
  37.1 12.2 %collective-permute-done.8.refs_2_.refs_6_.refs_8_ = bf16[256,1024]{1,0:T(8,128)(2,1)S(1)} collective-permute-done((bf16[256,1024]{1,0:T(8,128)(2,1)}, bf16[256,1024]{1,0:T(8,128)(2,1)S(1)}, u32[]{:S(2)}, u32[]{:S(2)}) %collective-permute-start.8) | collective-permute-done | bytes 524320 | tf_op jit(solution)/shard_map/ppermute | solution.py:508
  49.4 0.0 collective-permute-done.7.refs_1_.refs_5_.refs_7_
  49.4 0.0 copy-start.1
  49.4 1.0 copy-done.1
  50.4 1.6 %select.3 = (bf16[8,128,128]{2,1,0:T(8,128)(2,1)S(1)}, bf16[8,128,128]{2,1,0:T(8,128)(2,1)S(1)}, bf16[8,128,128]{2,1,0:T(8,128)(2,1)S(1)}) custom-call(s32[4,8,128]{2,1,0:T(8,128)S(1)} %all-to-all-done.asked_ref, bf16[256,1024]{1,0:T(8,128)(2,1)S(1)} %copy-done.1, bf16[256,1024]{1,0:T(8,128)(2,1)S(1)} %collective-permute-done.7.refs_1_.refs_5_.refs_7_, ...), custom_call_target="tpu_custom_call" | custom-call | bytes 2097152 | tf_op jit(solution)/shard_map/select/pallas_call | solution.py:166
  52.0 0.0 collective-permute-done.9.refs_2_
  52.1 1.2 %collective-permute-start.10 = (bf16[8,128,128]{2,1,0:T(8,128)(2,1)S(1)}, bf16[8,128,128]{2,1,0:T(8,128)(2,1)S(1)}, u32[]{:S(2)}, u32[]{:S(2)}) collective-permute-start(bf16[8,128,128]{2,1,0:T(8,128)(2,1)S(1)} %get-tuple-element.70), channel_id=1, source_target_pairs={{0,8},{8,16},{16,24},{24,0},{1,9},{9,17},{17,25},{25,1},{2,10},{10... | collective-permute-start | bytes 786440 | tf_op jit(solution)/shard_map/ppermute | solution.py:504
  53.3 1.0 collective-permute-start.11
  54.3 1.4 %collective-permute-start.12 = (bf16[8,128,128]{2,1,0:T(8,128)(2,1)S(1)}, bf16[8,128,128]{2,1,0:T(8,128)(2,1)S(1)}, u32[]{:S(2)}, u32[]{:S(2)}) collective-permute-start(bf16[8,128,128]{2,1,0:T(8,128)(2,1)S(1)} %get-tuple-element.72), channel_id=1, source_target_pairs={{0,24},{8,0},{16,8},{24,16},{1,25},{9,1},{17,9},{25,17},{2,26},{10... | collective-permute-start | bytes 786440 | tf_op jit(solution)/shard_map/ppermute | solution.py:504
  55.7 0.0 copy-done.2
  55.7 14.8 %near_attention.1 = (f32[32,128,128]{2,1,0:T(8,128)S(1)}, f32[32,8,256]{2,1,0:T(8,128)S(1)}) custom-call(s32[16,32]{1,0:T(8,128)S(1)} %bitcast.3, bf16[128,1024]{1,0:T(8,128)(2,1)S(1)} %copy-done.3, bf16[128,1024]{1,0:T(8,128)(2,1)S(1)} %collective-permute-done.1.refs_1_, bf16[128,1024]{1,0:T(8,128)(2,1)S(1)} %collective-permute-done.2.refs_2_, ...), custom_call_target="tpu_custom_call" | custom-call | flops 12884901888 | bytes 4194304 | tf_op jit(solution)/shard_map/near_attention/pallas_call | solution.py:290
  70.5 0.0 collective-permute-done.6.refs_1_
  70.5 0.0 collective-permute-done.5.refs_0_
  70.5 0.0 collective-permute-done.10.refs_3_
  70.5 4.7 %collective-permute-done.11.refs_4_ = bf16[8,128,128]{2,1,0:T(8,128)(2,1)S(1)} collective-permute-done((bf16[8,128,128]{2,1,0:T(8,128)(2,1)S(1)}, bf16[8,128,128]{2,1,0:T(8,128)(2,1)S(1)}, u32[]{:S(2)}, u32[]{:S(2)}) %collective-permute-start.11) | collective-permute-done | bytes 262176 | tf_op jit(solution)/shard_map/ppermute | solution.py:504
  75.2 2.6 %collective-permute-done.12.refs_5_ = bf16[8,128,128]{2,1,0:T(8,128)(2,1)S(1)} collective-permute-done((bf16[8,128,128]{2,1,0:T(8,128)(2,1)S(1)}, bf16[8,128,128]{2,1,0:T(8,128)(2,1)S(1)}, u32[]{:S(2)}, u32[]{:S(2)}) %collective-permute-start.12) | collective-permute-done | bytes 262176 | tf_op jit(solution)/shard_map/ppermute | solution.py:504
  77.9 0.0 copy-start
  77.9 7.3 %far_attention.1 = (bf16[128,512]{1,0:T(8,128)(2,1)S(1)}, bf16[128,512]{1,0:T(8,128)(2,1)S(1)}, bf16[128,512]{1,0:T(8,128)(2,1)S(1)}, bf16[128,512]{1,0:T(8,128)...) custom-call(s32[4,32]{1,0:T(4,128)S(1)} %get-tuple-element.44.pos_re, ...), custom_call_target="tpu_custom_call" | custom-call | flops 2147483648 | bytes 3145728 | tf_op jit(solution)/shard_map/far_attention/pallas_call | solution.py:436
  85.1 0.6 collective-permute-start.13
  85.7 1.2 %collective-permute-start.14 = (bf16[128,512]{1,0:T(8,128)(2,1)S(1)}, bf16[128,512]{1,0:T(8,128)(2,1)S(1)}, u32[]{:S(2)}, u32[]{:S(2)}) collective-permute-start(bf16[128,512]{1,0:T(8,128)(2,1)S(1)} %get-tuple-element.77), channel_id=1, source_target_pairs={{0,2},{1,3},{2,0},{3,1},{4,6},{5,7},{6,4},{7,5},{8,10},{9,11},{10,... | collective-permute-start | bytes 393224 | tf_op jit(solution)/shard_map/ppermute | solution.py:508
  86.9 0.5 collective-permute-start.15
  87.4 1.2 %collective-permute-start.16 = (bf16[128,512]{1,0:T(8,128)(2,1)S(1)}, bf16[128,512]{1,0:T(8,128)(2,1)S(1)}, u32[]{:S(2)}, u32[]{:S(2)}) collective-permute-start(bf16[128,512]{1,0:T(8,128)(2,1)S(1)} %get-tuple-element.79), channel_id=1, source_target_pairs={{0,4},{1,5},{2,6},{3,7},{4,0},{5,1},{6,2},{7,3},{8,12},{9,13},{10,... | collective-permute-start | bytes 393224 | tf_op jit(solution)/shard_map/ppermute | solution.py:508
  88.6 0.6 collective-permute-start.17
  89.2 0.0 collective-permute-done.13.refs_1_
  89.2 1.0 collective-permute-start.18
  90.2 0.6 collective-permute-done.14.refs_2_
  90.8 2.0 %collective-permute-start.19 = (bf16[128,512]{1,0:T(8,128)(2,1)S(1)}, bf16[128,512]{1,0:T(8,128)(2,1)S(1)}, u32[]{:S(2)}, u32[]{:S(2)}) collective-permute-start(bf16[128,512]{1,0:T(8,128)(2,1)S(1)} %get-tuple-element.82), channel_id=1, source_target_pairs={{0,7},{1,6},{2,5},{3,4},{4,3},{5,2},{6,1},{7,0},{8,15},{9,14},{10,... | collective-permute-start | bytes 393224 | tf_op jit(solution)/shard_map/ppermute | solution.py:508
  92.7 1.8 %collective-permute-done.15.refs_3_ = bf16[128,512]{1,0:T(8,128)(2,1)S(1)} collective-permute-done((bf16[128,512]{1,0:T(8,128)(2,1)S(1)}, bf16[128,512]{1,0:T(8,128)(2,1)S(1)}, u32[]{:S(2)}, u32[]{:S(2)}) %collective-permute-start.15) | collective-permute-done | bytes 131104 | tf_op jit(solution)/shard_map/ppermute | solution.py:508
  94.5 0.0 collective-permute-done.16.refs_4_
  94.5 6.6 %collective-permute-done.17.refs_5_ = bf16[128,512]{1,0:T(8,128)(2,1)S(1)} collective-permute-done((bf16[128,512]{1,0:T(8,128)(2,1)S(1)}, bf16[128,512]{1,0:T(8,128)(2,1)S(1)}, u32[]{:S(2)}, u32[]{:S(2)}) %collective-permute-start.17) | collective-permute-done | bytes 131104 | tf_op jit(solution)/shard_map/ppermute | solution.py:508
  101.0 0.0 collective-permute-done.18.refs_6_
  101.0 0.0 collective-permute-done.19.refs_7_
  101.0 0.0 copy-done
  101.1 3.5 %project_out.1 = bf16[512,1024]{1,0:T(8,128)(2,1)} custom-call(bf16[128,512]{1,0:T(8,128)(2,1)S(1)} %get-tuple-element.75.refs_0_, bf16[128,512]{1,0:T(8,128)(2,1)S(1)} %collective-permute-done.13.refs_1_, bf16[128,512]{1,0:T(8,128)(2,1)S(1)} %collective-permute-done.14.refs_2_, bf16[128,512]{1,0:T(8,128)(2,1)S(1)} %collective-permute-done.15.refs_3_, ...), custom_call_target="tpu_custom_call" | custom-call | flops 1073741824 | bytes 4194304 | tf_op jit(solution)/shard_map/project_out/pallas_call | solution.py:487
Async XLA Ops:
  0.0 10.8 %copy-start.5 = (s32[32]{0:T(128)S(1)}, s32[32]{0:T(128)}, u32[]{:S(2)}) copy-start(s32[32]{0:T(128)} %counts_ref.1) | copy-start | bytes 388
  0.0 10.8 %copy-start.4 = (s32[32,16]{0,1:T(8,128)S(1)}, s32[32,16]{0,1:T(8,128)}, u32[]{:S(2)}) copy-start(s32[32,16]{0,1:T(8,128)} %param.8) | copy-start | bytes 6148
  0.0 3.2 %collective-permute-start = (bf16[512,1024]{1,0:T(8,128)(2,1)}, bf16[512,1024]{1,0:T(8,128)(2,1)S(1)}, u32[]{:S(2)}, u32[]{:S(2)}) collective-permute-start(bf16[512,1024]{1,0:T(8,128)(2,1)} %own_ref.3), channel_id=1, source_target_pairs={{0,1},{1,0},{2,3},{3,2},{4,5},{5,4},{6,7},{7,6},{8,9},{9,8},{10,11... | collective-permute-start | bytes 3145736 | tf_op jit(solution)/shard_map/ppermute | solution.py:508
  3.2 1.0 copy-start.6
  8.6 17.0 %collective-permute-start.3 = (bf16[128,1024]{1,0:T(8,128)(2,1)}, bf16[128,1024]{1,0:T(8,128)(2,1)S(1)}, u32[]{:S(2)}, u32[]{:S(2)}) collective-permute-start(bf16[128,1024]{1,0:T(8,128)(2,1)} %get-tuple-element.57), channel_id=1, source_target_pairs={{0,6},{1,7},{2,4},{3,5},{4,2},{5,3},{6,0},{7,1},{8,14},{9,15},{10,... | collective-permute-start | bytes 786440 | tf_op jit(solution)/shard_map/ppermute | solution.py:508
  11.7 11.4 %all-to-all-start = ((s32[4,8,128]{2,1,0:T(8,128)}), s32[4,8,128]{2,1,0:T(8,128)S(1)}, u32[]{:S(2)}, u32[]{:S(2)}) async-start(s32[4,8,128]{2,1,0:T(8,128)} %get-tuple-element.47), calls=%async_computation | async-start | bytes 32768 | tf_op jit(solution)/shard_map/all_to_all | solution.py:579
  16.5 9.4 %collective-permute-start.1 = (bf16[128,1024]{1,0:T(8,128)(2,1)}, bf16[128,1024]{1,0:T(8,128)(2,1)S(1)}, u32[]{:S(2)}, u32[]{:S(2)}) collective-permute-start(bf16[128,1024]{1,0:T(8,128)(2,1)} %get-tuple-element.54), channel_id=1, source_target_pairs={{0,2},{1,3},{2,0},{3,1},{4,6},{5,7},{6,4},{7,5},{8,10},{9,11},{10,... | collective-permute-start | bytes 786440 | tf_op jit(solution)/shard_map/ppermute | solution.py:508
  16.7 9.1 %copy-start.3 = (bf16[128,1024]{1,0:T(8,128)(2,1)S(1)}, bf16[128,1024]{1,0:T(8,128)(2,1)}, u32[]{:S(2)}) copy-start(bf16[128,1024]{1,0:T(8,128)(2,1)} %get-tuple-element.53.refs_0_) | copy-start | bytes 786436
  16.7 9.1 %collective-permute-start.2 = (bf16[128,1024]{1,0:T(8,128)(2,1)}, bf16[128,1024]{1,0:T(8,128)(2,1)S(1)}, u32[]{:S(2)}, u32[]{:S(2)}) collective-permute-start(bf16[128,1024]{1,0:T(8,128)(2,1)} %get-tuple-element.55), channel_id=1, source_target_pairs={{0,4},{1,5},{2,6},{3,7},{4,0},{5,1},{6,2},{7,3},{8,12},{9,13},{10,... | collective-permute-start | bytes 786440 | tf_op jit(solution)/shard_map/ppermute | solution.py:508
  23.1 32.6 %copy-start.2 = (bf16[256,1024]{1,0:T(8,128)(2,1)S(1)}, bf16[256,1024]{1,0:T(8,128)(2,1)}, u32[]{:S(2)}) copy-start(bf16[256,1024]{1,0:T(8,128)(2,1)} %get-tuple-element.63.refs_0_.refs_4_.refs_6_) | copy-start | bytes 1572868
  23.1 12.8 %collective-permute-start.4 = (bf16[256,1024]{1,0:T(8,128)(2,1)}, bf16[256,1024]{1,0:T(8,128)(2,1)S(1)}, u32[]{:S(2)}, u32[]{:S(2)}) collective-permute-start(bf16[256,1024]{1,0:T(8,128)(2,1)} %get-tuple-element.60), channel_id=1, source_target_pairs={{0,6},{1,7},{2,4},{3,5},{4,2},{5,3},{6,0},{7,1},{8,14},{9,15},{10,... | collective-permute-start | bytes 1572872 | tf_op jit(solution)/shard_map/ppermute | solution.py:508
  25.3 24.0 %collective-permute-start.8 = (bf16[256,1024]{1,0:T(8,128)(2,1)}, bf16[256,1024]{1,0:T(8,128)(2,1)S(1)}, u32[]{:S(2)}, u32[]{:S(2)}) collective-permute-start(bf16[256,1024]{1,0:T(8,128)(2,1)} %get-tuple-element.65), channel_id=1, source_target_pairs={{0,4},{1,5},{2,6},{3,7},{4,0},{5,1},{6,2},{7,3},{8,12},{9,13},{10,... | collective-permute-start | bytes 1572872 | tf_op jit(solution)/shard_map/ppermute | solution.py:508
  25.6 23.8 %collective-permute-start.7 = (bf16[256,1024]{1,0:T(8,128)(2,1)}, bf16[256,1024]{1,0:T(8,128)(2,1)S(1)}, u32[]{:S(2)}, u32[]{:S(2)}) collective-permute-start(bf16[256,1024]{1,0:T(8,128)(2,1)} %get-tuple-element.64), channel_id=1, source_target_pairs={{0,2},{1,3},{2,0},{3,1},{4,6},{5,7},{6,4},{7,5},{8,10},{9,11},{10,... | collective-permute-start | bytes 1572872 | tf_op jit(solution)/shard_map/ppermute | solution.py:508
  27.5 24.6 %collective-permute-start.9 = (bf16[8,128,128]{2,1,0:T(8,128)(2,1)S(1)}, bf16[8,128,128]{2,1,0:T(8,128)(2,1)S(1)}, u32[]{:S(2)}, u32[]{:S(2)}) collective-permute-start(bf16[8,128,128]{2,1,0:T(8,128)(2,1)S(1)} %get-tuple-element.68), channel_id=1, source_target_pairs={{0,24},{8,0},{16,8},{24,16},{1,25},{9,1},{17,9},{25,17},{2,26},{10... | collective-permute-start | bytes 786440 | tf_op jit(solution)/shard_map/ppermute | solution.py:504
  27.5 43.0 %collective-permute-start.6 = (bf16[8,128,128]{2,1,0:T(8,128)(2,1)S(1)}, bf16[8,128,128]{2,1,0:T(8,128)(2,1)S(1)}, u32[]{:S(2)}, u32[]{:S(2)}) collective-permute-start(bf16[8,128,128]{2,1,0:T(8,128)(2,1)S(1)} %get-tuple-element.62), channel_id=1, source_target_pairs={{0,16},{8,24},{16,0},{24,8},{1,17},{9,25},{17,1},{25,9},{2,18},{10... | collective-permute-start | bytes 786440 | tf_op jit(solution)/shard_map/ppermute | solution.py:504
  36.0 34.6 %collective-permute-start.5 = (bf16[8,128,128]{2,1,0:T(8,128)(2,1)S(1)}, bf16[8,128,128]{2,1,0:T(8,128)(2,1)S(1)}, u32[]{:S(2)}, u32[]{:S(2)}) collective-permute-start(bf16[8,128,128]{2,1,0:T(8,128)(2,1)S(1)} %get-tuple-element.61), channel_id=1, source_target_pairs={{0,8},{8,16},{16,24},{24,0},{1,9},{9,17},{17,25},{25,1},{2,10},{10... | collective-permute-start | bytes 786440 | tf_op jit(solution)/shard_map/ppermute | solution.py:504
  49.4 1.0 copy-start.1
  52.1 18.5 %collective-permute-start.10 = (bf16[8,128,128]{2,1,0:T(8,128)(2,1)S(1)}, bf16[8,128,128]{2,1,0:T(8,128)(2,1)S(1)}, u32[]{:S(2)}, u32[]{:S(2)}) collective-permute-start(bf16[8,128,128]{2,1,0:T(8,128)(2,1)S(1)} %get-tuple-element.70), channel_id=1, source_target_pairs={{0,8},{8,16},{16,24},{24,0},{1,9},{9,17},{17,25},{25,1},{2,10},{10... | collective-permute-start | bytes 786440 | tf_op jit(solution)/shard_map/ppermute | solution.py:504
  53.3 21.9 %collective-permute-start.11 = (bf16[8,128,128]{2,1,0:T(8,128)(2,1)S(1)}, bf16[8,128,128]{2,1,0:T(8,128)(2,1)S(1)}, u32[]{:S(2)}, u32[]{:S(2)}) collective-permute-start(bf16[8,128,128]{2,1,0:T(8,128)(2,1)S(1)} %get-tuple-element.71), channel_id=1, source_target_pairs={{0,16},{8,24},{16,0},{24,8},{1,17},{9,25},{17,1},{25,9},{2,18},{10... | collective-permute-start | bytes 786440 | tf_op jit(solution)/shard_map/ppermute | solution.py:504
  54.3 23.6 %collective-permute-start.12 = (bf16[8,128,128]{2,1,0:T(8,128)(2,1)S(1)}, bf16[8,128,128]{2,1,0:T(8,128)(2,1)S(1)}, u32[]{:S(2)}, u32[]{:S(2)}) collective-permute-start(bf16[8,128,128]{2,1,0:T(8,128)(2,1)S(1)} %get-tuple-element.72), channel_id=1, source_target_pairs={{0,24},{8,0},{16,8},{24,16},{1,25},{9,1},{17,9},{25,17},{2,26},{10... | collective-permute-start | bytes 786440 | tf_op jit(solution)/shard_map/ppermute | solution.py:504
  77.9 23.2 %copy-start = (bf16[1024,1024]{1,0:T(8,128)(2,1)S(1)}, bf16[1024,1024]{1,0:T(8,128)(2,1)}, u32[]{:S(2)}) copy-start(bf16[1024,1024]{1,0:T(8,128)(2,1)} %refs_8_.1) | copy-start | bytes 6291460
  85.1 4.1 %collective-permute-start.13 = (bf16[128,512]{1,0:T(8,128)(2,1)S(1)}, bf16[128,512]{1,0:T(8,128)(2,1)S(1)}, u32[]{:S(2)}, u32[]{:S(2)}) collective-permute-start(bf16[128,512]{1,0:T(8,128)(2,1)S(1)} %get-tuple-element.76), channel_id=1, source_target_pairs={{0,1},{1,0},{2,3},{3,2},{4,5},{5,4},{6,7},{7,6},{8,9},{9,8},{10,11... | collective-permute-start | bytes 393224 | tf_op jit(solution)/shard_map/ppermute | solution.py:508
  85.7 5.1 %collective-permute-start.14 = (bf16[128,512]{1,0:T(8,128)(2,1)S(1)}, bf16[128,512]{1,0:T(8,128)(2,1)S(1)}, u32[]{:S(2)}, u32[]{:S(2)}) collective-permute-start(bf16[128,512]{1,0:T(8,128)(2,1)S(1)} %get-tuple-element.77), channel_id=1, source_target_pairs={{0,2},{1,3},{2,0},{3,1},{4,6},{5,7},{6,4},{7,5},{8,10},{9,11},{10,... | collective-permute-start | bytes 393224 | tf_op jit(solution)/shard_map/ppermute | solution.py:508
  86.9 7.6 %collective-permute-start.15 = (bf16[128,512]{1,0:T(8,128)(2,1)S(1)}, bf16[128,512]{1,0:T(8,128)(2,1)S(1)}, u32[]{:S(2)}, u32[]{:S(2)}) collective-permute-start(bf16[128,512]{1,0:T(8,128)(2,1)S(1)} %get-tuple-element.78), channel_id=1, source_target_pairs={{0,3},{1,2},{2,1},{3,0},{4,7},{5,6},{6,5},{7,4},{8,11},{9,10},{10,... | collective-permute-start | bytes 393224 | tf_op jit(solution)/shard_map/ppermute | solution.py:508
  87.4 7.1 %collective-permute-start.16 = (bf16[128,512]{1,0:T(8,128)(2,1)S(1)}, bf16[128,512]{1,0:T(8,128)(2,1)S(1)}, u32[]{:S(2)}, u32[]{:S(2)}) collective-permute-start(bf16[128,512]{1,0:T(8,128)(2,1)S(1)} %get-tuple-element.79), channel_id=1, source_target_pairs={{0,4},{1,5},{2,6},{3,7},{4,0},{5,1},{6,2},{7,3},{8,12},{9,13},{10,... | collective-permute-start | bytes 393224 | tf_op jit(solution)/shard_map/ppermute | solution.py:508
  88.6 12.4 %collective-permute-start.17 = (bf16[128,512]{1,0:T(8,128)(2,1)S(1)}, bf16[128,512]{1,0:T(8,128)(2,1)S(1)}, u32[]{:S(2)}, u32[]{:S(2)}) collective-permute-start(bf16[128,512]{1,0:T(8,128)(2,1)S(1)} %get-tuple-element.80), channel_id=1, source_target_pairs={{0,5},{1,4},{2,7},{3,6},{4,1},{5,0},{6,3},{7,2},{8,13},{9,12},{10,... | collective-permute-start | bytes 393224 | tf_op jit(solution)/shard_map/ppermute | solution.py:508
  89.2 11.9 %collective-permute-start.18 = (bf16[128,512]{1,0:T(8,128)(2,1)S(1)}, bf16[128,512]{1,0:T(8,128)(2,1)S(1)}, u32[]{:S(2)}, u32[]{:S(2)}) collective-permute-start(bf16[128,512]{1,0:T(8,128)(2,1)S(1)} %get-tuple-element.81), channel_id=1, source_target_pairs={{0,6},{1,7},{2,4},{3,5},{4,2},{5,3},{6,0},{7,1},{8,14},{9,15},{10,... | collective-permute-start | bytes 393224 | tf_op jit(solution)/shard_map/ppermute | solution.py:508
  90.8 10.3 %collective-permute-start.19 = (bf16[128,512]{1,0:T(8,128)(2,1)S(1)}, bf16[128,512]{1,0:T(8,128)(2,1)S(1)}, u32[]{:S(2)}, u32[]{:S(2)}) collective-permute-start(bf16[128,512]{1,0:T(8,128)(2,1)S(1)} %get-tuple-element.82), channel_id=1, source_target_pairs={{0,7},{1,6},{2,5},{3,4},{4,3},{5,2},{6,1},{7,0},{8,15},{9,14},{10,... | collective-permute-start | bytes 393224 | tf_op jit(solution)/shard_map/ppermute | solution.py:508

commit v6 on v5

--- a/solution.py
+++ b/solution.py
@@ -312,7 +312,7 @@
     )(ids, *first_kv, *rest)
 
 
-def far_attention(heads_dev, npair, seq_size, ncl, cap, pos, counts, tables, rest, near, stats):
+def far_attention(heads_dev, npair, seq_size, ncl, cap, pos, tables, rest, near, stats):
     wide = rest[0].shape[1]
     per = wide // BLK
     nblk = npair * per
@@ -323,7 +323,7 @@
     keys = REMOTE * BLK
     shifts = ncl - 1
 
-    def body(pos_ref, counts_ref, *refs):
+    def body(pos_ref, *refs):
         tabs = refs[: heads_dev * shifts]
         refs = refs[heads_dev * shifts :]
         rests = refs[:npair]
@@ -374,7 +374,7 @@
             return (seq ^ (n // dev_blocks)) * dev_blocks + lax.rem(n, dev_blocks)
 
         def scores(b, qm, held, c, best):
-            valid = counts_ref[b] - NEAR
+            valid = pos_ref[REMOTE, b] - NEAR
             for j in range(c, c + 4):
                 s = jnp.dot(ktab[pos_ref[j, b]], qm, preferred_element_type=F32)
                 if j:
@@ -436,7 +436,7 @@
     return pl.pallas_call(
         body,
         out_shape=[jax.ShapeDtypeStruct((feats, dev_blocks * BLK), BF16)] * seq_size,
-        in_specs=[SMEM, SMEM] + [ANY] * (heads_dev * shifts + npair) + [ANY, VMEM],
+        in_specs=[SMEM] + [ANY] * (heads_dev * shifts + npair) + [ANY, VMEM],
         out_specs=[VMEM] * seq_size,
         scratch_shapes=[
             pltpu.VMEM((heads_dev, ncl * cap, 2 * HD, BLK), BF16),
@@ -454,7 +454,7 @@
         compiler_params=params(40),
         cost_estimate=cost(flops, 6 * nblk * BLK * feats, nblk * keys * cols),
         name="far_attention",
-    )(pos, counts, *[x for t in tables for x in t], *rest, near, stats)
+    )(pos, *[x for t in tables for x in t], *rest, near, stats)
 
 
 def project_out(seq_size, pieces, w_out):
@@ -534,11 +534,12 @@
                 spot[j] = spot[j] + jnp.sum(jnp.where(hits[j], place, 0.0), axis=0, keepdims=True)
         for j in range(REMOTE):
             pos_ref[j : j + 1, :] = jnp.where(valid[j], spot[j], spot[0]).astype(jnp.int32)
+        pos_ref[REMOTE:, :] = counts_ref[...]
 
     return pl.pallas_call(
         body,
         out_shape=[
-            jax.ShapeDtypeStruct((REMOTE, nblk), jnp.int32),
+            jax.ShapeDtypeStruct((REMOTE + 1, nblk), jnp.int32),
             jax.ShapeDtypeStruct((ncl, 8, 128), jnp.int32),
         ],
         in_specs=[VMEM, VMEM],
@@ -596,7 +597,7 @@
         far.append(picked)
     near, stats = near_attention(heads_dev, npair, slots, first_kv, rest)
     outs = far_attention(
-        heads_dev, npair, seq_size, ncl, cap, pos, counts, far, rest, near, stats
+        heads_dev, npair, seq_size, ncl, cap, pos, far, rest, near, stats
     )
     pieces = list(outs)
     for k in sorted(range(1, seq_size), key=lambda k: (-bin(k // 2).count("1"), k)):

time: 105 us -> 105 us (level)
  no operation moved by 1% of the time
where the time goes in v6:
time: 105 us
  Pallas kernels  40.4 us (38%)
  waiting for transfers between devices  37 us (35%)
  starting transfers between devices  25.1 us (24%)
  local copies, waits for them, and re-layouts  2.03 us (2%)
    ppermute x14, waiting for transfers between devices, crossed(): return lax.ppermute(x, 'seq', [(i, i ^ k) for i in range(size)])  29.7 us
    pallas_call x1, Pallas kernels, near_attention(): pl.pallas_call(body, out_shape=[jax.ShapeDtypeStruct((nblk, feats, BLK),...  14.8 us
    ppermute x14, starting transfers between devices, crossed(): return lax.ppermute(x, 'seq', [(i, i ^ k) for i in range(size)])  13.1 us
    pallas_call x2, Pallas kernels, project(): pl.pallas_call(body, out_shape=shapes, in_specs=[ANY, ANY, ANY], out_spec...  10.6 us
    ppermute x6, waiting for transfers between devices, shifted(): return lax.ppermute(x, axis, [(i, (i + shift) % size) for i in range(size)])  7.33 us
    pallas_call x1, Pallas kernels, far_attention(): pl.pallas_call(body, out_shape=[jax.ShapeDtypeStruct((feats, dev_blocks *...  7.27 us
    ppermute x6, starting transfers between devices, shifted(): return lax.ppermute(x, axis, [(i, (i + shift) % size) for i in range(size)])  7.19 us
    all_to_all x1, starting transfers between devices, on_device(): lax.all_to_all(wanted, 'cluster', split_axis=0, concat_axis=0, tiled=True)  4.76 us
  transfers between devices with their start and end apart: 21, of which 8 were waited for; matrix products, arithmetic and copies ran while one was open for 0% of the time, Pallas kernels for 24%

profile of v6, /device:TPU:9, one launch (start us, length us, event | category | flops | bytes accessed | tf_op | source)
XLA Modules:
  0.0 104.8 jit_solution(3215271788298505031)
XLA Ops:
  0.0 0.0 copy-start.5
  0.0 0.0 copy-start.4
  0.0 0.7 collective-permute-start
  0.7 2.5 %collective-permute-done.other_ref = bf16[512,1024]{1,0:T(8,128)(2,1)S(1)} collective-permute-done((bf16[512,1024]{1,0:T(8,128)(2,1)}, bf16[512,1024]{1,0:T(8,128)(2,1)S(1)}, u32[]{:S(2)}, u32[]{:S(2)}) %collective-permute-start) | collective-permute-done | bytes 1048608 | tf_op jit(solution)/shard_map/ppermute | solution.py:508
  3.2 0.0 copy-start.6
  3.2 1.0 copy-done.6
  4.1 4.4 %project.2 = (bf16[128,1024]{1,0:T(8,128)(2,1)}, bf16[128,1024]{1,0:T(8,128)(2,1)}, bf16[128,1024]{1,0:T(8,128)(2,1)}, bf16[128,1024]{1,0:T(8,128)(2,1)}) custom-call(bf16[512,1024]{1,0:T(8,128)(2,1)} %own_ref.3, bf16[512,1024]{1,0:T(8,128)(2,1)} %copy-done.6, bf16[1024,3072]{1,0:T(8,128)(2,1)} %w_ref.3), custom_call_target="tpu_custom_call" | custom-call | flops 1073741824 | bytes 4194304 | tf_op jit(solution)/shard_map/project/pallas_call | solution.py:111
  8.6 2.2 %collective-permute-start.3 = (bf16[128,1024]{1,0:T(8,128)(2,1)}, bf16[128,1024]{1,0:T(8,128)(2,1)S(1)}, u32[]{:S(2)}, u32[]{:S(2)}) collective-permute-start(bf16[128,1024]{1,0:T(8,128)(2,1)} %get-tuple-element.57), channel_id=1, source_target_pairs={{0,6},{1,7},{2,4},{3,5},{4,2},{5,3},{6,0},{7,1},{8,14},{9,15},{10,... | collective-permute-start | bytes 786440 | tf_op jit(solution)/shard_map/ppermute | solution.py:508
  10.8 0.0 copy-done.5
  10.8 0.0 copy-done.4
  10.8 0.9 block_lists.1
  11.7 4.8 %all-to-all-start = ((s32[4,8,128]{2,1,0:T(8,128)}), s32[4,8,128]{2,1,0:T(8,128)S(1)}, u32[]{:S(2)}, u32[]{:S(2)}) async-start(s32[4,8,128]{2,1,0:T(8,128)} %get-tuple-element.47), calls=%async_computation | async-start | bytes 32768 | tf_op jit(solution)/shard_map/all_to_all | solution.py:580
  16.5 0.3 collective-permute-start.1
  16.7 0.0 copy-start.3
  16.7 0.2 collective-permute-start.2
  17.0 6.1 %project.3 = (bf16[256,1024]{1,0:T(8,128)(2,1)}, bf16[256,1024]{1,0:T(8,128)(2,1)}, bf16[256,1024]{1,0:T(8,128)(2,1)}, bf16[256,1024]{1,0:T(8,128)(2,1)}) custom-call(bf16[512,1024]{1,0:T(8,128)(2,1)} %own_ref.3, bf16[512,1024]{1,0:T(8,128)(2,1)} %copy-done.6, bf16[1024,3072]{1,0:T(8,128)(2,1)} %w_ref.3), custom_call_target="tpu_custom_call" | custom-call | flops 2147483648 | bytes 5242880 | tf_op jit(solution)/shard_map/project/pallas_call | solution.py:111
  23.1 0.0 copy-start.2
  23.1 0.0 all-to-all-done.asked_ref
  23.1 2.2 %collective-permute-start.4 = (bf16[256,1024]{1,0:T(8,128)(2,1)}, bf16[256,1024]{1,0:T(8,128)(2,1)S(1)}, u32[]{:S(2)}, u32[]{:S(2)}) collective-permute-start(bf16[256,1024]{1,0:T(8,128)(2,1)} %get-tuple-element.60), channel_id=1, source_target_pairs={{0,6},{1,7},{2,4},{3,5},{4,2},{5,3},{6,0},{7,1},{8,14},{9,15},{10,... | collective-permute-start | bytes 1572872 | tf_op jit(solution)/shard_map/ppermute | solution.py:508
  25.3 0.2 collective-permute-start.8
  25.6 0.0 collective-permute-done.3.refs_3_
  25.6 0.3 collective-permute-start.7
  25.8 0.0 collective-permute-done.1.refs_1_
  25.8 0.0 collective-permute-done.2.refs_2_
  25.8 0.0 copy-done.3
  25.8 1.6 %select.2 = (bf16[8,128,128]{2,1,0:T(8,128)(2,1)S(1)}, bf16[8,128,128]{2,1,0:T(8,128)(2,1)S(1)}, bf16[8,128,128]{2,1,0:T(8,128)(2,1)S(1)}) custom-call(s32[4,8,128]{2,1,0:T(8,128)S(1)} %all-to-all-done.asked_ref, bf16[128,1024]{1,0:T(8,128)(2,1)S(1)} %copy-done.3, bf16[128,1024]{1,0:T(8,128)(2,1)S(1)} %collective-permute-done.1.refs_1_, ...), custom_call_target="tpu_custom_call" | custom-call | bytes 2097152 | tf_op jit(solution)/shard_map/select/pallas_call | solution.py:166
  27.5 0.1 collective-permute-start.9
  27.5 2.3 %collective-permute-start.6 = (bf16[8,128,128]{2,1,0:T(8,128)(2,1)S(1)}, bf16[8,128,128]{2,1,0:T(8,128)(2,1)S(1)}, u32[]{:S(2)}, u32[]{:S(2)}) collective-permute-start(bf16[8,128,128]{2,1,0:T(8,128)(2,1)S(1)} %get-tuple-element.62), channel_id=1, source_target_pairs={{0,16},{8,24},{16,0},{24,8},{1,17},{9,25},{17,1},{25,9},{2,18},{10... | collective-permute-start | bytes 786440 | tf_op jit(solution)/shard_map/ppermute | solution.py:504
  29.9 6.1 %collective-permute-done.4.refs_3_.refs_7_.refs_9_ = bf16[256,1024]{1,0:T(8,128)(2,1)S(1)} collective-permute-done((bf16[256,1024]{1,0:T(8,128)(2,1)}, bf16[256,1024]{1,0:T(8,128)(2,1)S(1)}, u32[]{:S(2)}, u32[]{:S(2)}) %collective-permute-start.4) | collective-permute-done | bytes 524320 | tf_op jit(solution)/shard_map/ppermute | solution.py:508
  36.0 1.2 %collective-permute-start.5 = (bf16[8,128,128]{2,1,0:T(8,128)(2,1)S(1)}, bf16[8,128,128]{2,1,0:T(8,128)(2,1)S(1)}, u32[]{:S(2)}, u32[]{:S(2)}) collective-permute-start(bf16[8,128,128]{2,1,0:T(8,128)(2,1)S(1)} %get-tuple-element.61), channel_id=1, source_target_pairs={{0,8},{8,16},{16,24},{24,0},{1,9},{9,17},{17,25},{25,1},{2,10},{10... | collective-permute-start | bytes 786440 | tf_op jit(solution)/shard_map/ppermute | solution.py:504
  37.1 12.2 %collective-permute-done.8.refs_2_.refs_6_.refs_8_ = bf16[256,1024]{1,0:T(8,128)(2,1)S(1)} collective-permute-done((bf16[256,1024]{1,0:T(8,128)(2,1)}, bf16[256,1024]{1,0:T(8,128)(2,1)S(1)}, u32[]{:S(2)}, u32[]{:S(2)}) %collective-permute-start.8) | collective-permute-done | bytes 524320 | tf_op jit(solution)/shard_map/ppermute | solution.py:508
  49.4 0.0 collective-permute-done.7.refs_1_.refs_5_.refs_7_
  49.4 0.0 copy-start.1
  49.4 1.0 copy-done.1
  50.4 1.6 %select.3 = (bf16[8,128,128]{2,1,0:T(8,128)(2,1)S(1)}, bf16[8,128,128]{2,1,0:T(8,128)(2,1)S(1)}, bf16[8,128,128]{2,1,0:T(8,128)(2,1)S(1)}) custom-call(s32[4,8,128]{2,1,0:T(8,128)S(1)} %all-to-all-done.asked_ref, bf16[256,1024]{1,0:T(8,128)(2,1)S(1)} %copy-done.1, bf16[256,1024]{1,0:T(8,128)(2,1)S(1)} %collective-permute-done.7.refs_1_.refs_5_.refs_7_, ...), custom_call_target="tpu_custom_call" | custom-call | bytes 2097152 | tf_op jit(solution)/shard_map/select/pallas_call | solution.py:166
  52.0 0.0 collective-permute-done.9.refs_2_
  52.1 1.2 %collective-permute-start.10 = (bf16[8,128,128]{2,1,0:T(8,128)(2,1)S(1)}, bf16[8,128,128]{2,1,0:T(8,128)(2,1)S(1)}, u32[]{:S(2)}, u32[]{:S(2)}) collective-permute-start(bf16[8,128,128]{2,1,0:T(8,128)(2,1)S(1)} %get-tuple-element.70), channel_id=1, source_target_pairs={{0,8},{8,16},{16,24},{24,0},{1,9},{9,17},{17,25},{25,1},{2,10},{10... | collective-permute-start | bytes 786440 | tf_op jit(solution)/shard_map/ppermute | solution.py:504
  53.3 1.0 collective-permute-start.11
  54.3 1.4 %collective-permute-start.12 = (bf16[8,128,128]{2,1,0:T(8,128)(2,1)S(1)}, bf16[8,128,128]{2,1,0:T(8,128)(2,1)S(1)}, u32[]{:S(2)}, u32[]{:S(2)}) collective-permute-start(bf16[8,128,128]{2,1,0:T(8,128)(2,1)S(1)} %get-tuple-element.72), channel_id=1, source_target_pairs={{0,24},{8,0},{16,8},{24,16},{1,25},{9,1},{17,9},{25,17},{2,26},{10... | collective-permute-start | bytes 786440 | tf_op jit(solution)/shard_map/ppermute | solution.py:504
  55.7 0.0 copy-done.2
  55.7 14.8 %near_attention.1 = (f32[32,128,128]{2,1,0:T(8,128)S(1)}, f32[32,8,256]{2,1,0:T(8,128)S(1)}) custom-call(s32[16,32]{1,0:T(8,128)S(1)} %bitcast.3, bf16[128,1024]{1,0:T(8,128)(2,1)S(1)} %copy-done.3, bf16[128,1024]{1,0:T(8,128)(2,1)S(1)} %collective-permute-done.1.refs_1_, bf16[128,1024]{1,0:T(8,128)(2,1)S(1)} %collective-permute-done.2.refs_2_, ...), custom_call_target="tpu_custom_call" | custom-call | flops 12884901888 | bytes 4194304 | tf_op jit(solution)/shard_map/near_attention/pallas_call | solution.py:290
  70.5 0.0 collective-permute-done.6.refs_1_
  70.5 0.0 collective-permute-done.5.refs_0_
  70.5 0.0 collective-permute-done.10.refs_3_
  70.5 4.7 %collective-permute-done.11.refs_4_ = bf16[8,128,128]{2,1,0:T(8,128)(2,1)S(1)} collective-permute-done((bf16[8,128,128]{2,1,0:T(8,128)(2,1)S(1)}, bf16[8,128,128]{2,1,0:T(8,128)(2,1)S(1)}, u32[]{:S(2)}, u32[]{:S(2)}) %collective-permute-start.11) | collective-permute-done | bytes 262176 | tf_op jit(solution)/shard_map/ppermute | solution.py:504
  75.2 2.6 %collective-permute-done.12.refs_5_ = bf16[8,128,128]{2,1,0:T(8,128)(2,1)S(1)} collective-permute-done((bf16[8,128,128]{2,1,0:T(8,128)(2,1)S(1)}, bf16[8,128,128]{2,1,0:T(8,128)(2,1)S(1)}, u32[]{:S(2)}, u32[]{:S(2)}) %collective-permute-start.12) | collective-permute-done | bytes 262176 | tf_op jit(solution)/shard_map/ppermute | solution.py:504
  77.9 0.0 copy-start
  77.9 7.3 %far_attention.1 = (bf16[128,512]{1,0:T(8,128)(2,1)S(1)}, bf16[128,512]{1,0:T(8,128)(2,1)S(1)}, bf16[128,512]{1,0:T(8,128)(2,1)S(1)}, bf16[128,512]{1,0:T(8,128)...) custom-call(s32[5,32]{1,0:T(8,128)S(1)} %get-tuple-element.44.pos_re, ...), custom_call_target="tpu_custom_call" | custom-call | flops 2147483648 | bytes 3145728 | tf_op jit(solution)/shard_map/far_attention/pallas_call | solution.py:436
  85.1 0.6 collective-permute-start.13
  85.7 1.2 %collective-permute-start.14 = (bf16[128,512]{1,0:T(8,128)(2,1)S(1)}, bf16[128,512]{1,0:T(8,128)(2,1)S(1)}, u32[]{:S(2)}, u32[]{:S(2)}) collective-permute-start(bf16[128,512]{1,0:T(8,128)(2,1)S(1)} %get-tuple-element.77), channel_id=1, source_target_pairs={{0,2},{1,3},{2,0},{3,1},{4,6},{5,7},{6,4},{7,5},{8,10},{9,11},{10,... | collective-permute-start | bytes 393224 | tf_op jit(solution)/shard_map/ppermute | solution.py:508
  86.9 0.5 collective-permute-start.15
  87.4 1.2 %collective-permute-start.16 = (bf16[128,512]{1,0:T(8,128)(2,1)S(1)}, bf16[128,512]{1,0:T(8,128)(2,1)S(1)}, u32[]{:S(2)}, u32[]{:S(2)}) collective-permute-start(bf16[128,512]{1,0:T(8,128)(2,1)S(1)} %get-tuple-element.79), channel_id=1, source_target_pairs={{0,4},{1,5},{2,6},{3,7},{4,0},{5,1},{6,2},{7,3},{8,12},{9,13},{10,... | collective-permute-start | bytes 393224 | tf_op jit(solution)/shard_map/ppermute | solution.py:508
  88.6 0.6 collective-permute-start.17
  89.2 0.0 collective-permute-done.13.refs_1_
  89.2 1.0 collective-permute-start.18
  90.2 0.6 collective-permute-done.14.refs_2_
  90.8 2.0 %collective-permute-start.19 = (bf16[128,512]{1,0:T(8,128)(2,1)S(1)}, bf16[128,512]{1,0:T(8,128)(2,1)S(1)}, u32[]{:S(2)}, u32[]{:S(2)}) collective-permute-start(bf16[128,512]{1,0:T(8,128)(2,1)S(1)} %get-tuple-element.82), channel_id=1, source_target_pairs={{0,7},{1,6},{2,5},{3,4},{4,3},{5,2},{6,1},{7,0},{8,15},{9,14},{10,... | collective-permute-start | bytes 393224 | tf_op jit(solution)/shard_map/ppermute | solution.py:508
  92.7 1.8 %collective-permute-done.15.refs_3_ = bf16[128,512]{1,0:T(8,128)(2,1)S(1)} collective-permute-done((bf16[128,512]{1,0:T(8,128)(2,1)S(1)}, bf16[128,512]{1,0:T(8,128)(2,1)S(1)}, u32[]{:S(2)}, u32[]{:S(2)}) %collective-permute-start.15) | collective-permute-done | bytes 131104 | tf_op jit(solution)/shard_map/ppermute | solution.py:508
  94.5 0.0 collective-permute-done.16.refs_4_
  94.5 6.6 %collective-permute-done.17.refs_5_ = bf16[128,512]{1,0:T(8,128)(2,1)S(1)} collective-permute-done((bf16[128,512]{1,0:T(8,128)(2,1)S(1)}, bf16[128,512]{1,0:T(8,128)(2,1)S(1)}, u32[]{:S(2)}, u32[]{:S(2)}) %collective-permute-start.17) | collective-permute-done | bytes 131104 | tf_op jit(solution)/shard_map/ppermute | solution.py:508
  101.1 0.0 collective-permute-done.18.refs_6_
  101.1 0.0 collective-permute-done.19.refs_7_
  101.1 0.0 copy-done
  101.1 3.6 %project_out.1 = bf16[512,1024]{1,0:T(8,128)(2,1)} custom-call(bf16[128,512]{1,0:T(8,128)(2,1)S(1)} %get-tuple-element.75.refs_0_, bf16[128,512]{1,0:T(8,128)(2,1)S(1)} %collective-permute-done.13.refs_1_, bf16[128,512]{1,0:T(8,128)(2,1)S(1)} %collective-permute-done.14.refs_2_, bf16[128,512]{1,0:T(8,128)(2,1)S(1)} %collective-permute-done.15.refs_3_, ...), custom_call_target="tpu_custom_call" | custom-call | flops 1073741824 | bytes 4194304 | tf_op jit(solution)/shard_map/project_out/pallas_call | solution.py:487
Async XLA Ops:
  0.0 10.8 %copy-start.5 = (s32[32]{0:T(128)S(1)}, s32[32]{0:T(128)}, u32[]{:S(2)}) copy-start(s32[32]{0:T(128)} %param.9) | copy-start | bytes 388
  0.0 10.8 %copy-start.4 = (s32[32,16]{0,1:T(8,128)S(1)}, s32[32,16]{0,1:T(8,128)}, u32[]{:S(2)}) copy-start(s32[32,16]{0,1:T(8,128)} %param.8) | copy-start | bytes 6148
  0.0 3.2 %collective-permute-start = (bf16[512,1024]{1,0:T(8,128)(2,1)}, bf16[512,1024]{1,0:T(8,128)(2,1)S(1)}, u32[]{:S(2)}, u32[]{:S(2)}) collective-permute-start(bf16[512,1024]{1,0:T(8,128)(2,1)} %own_ref.3), channel_id=1, source_target_pairs={{0,1},{1,0},{2,3},{3,2},{4,5},{5,4},{6,7},{7,6},{8,9},{9,8},{10,11... | collective-permute-start | bytes 3145736 | tf_op jit(solution)/shard_map/ppermute | solution.py:508
  3.2 1.0 copy-start.6
  8.6 17.0 %collective-permute-start.3 = (bf16[128,1024]{1,0:T(8,128)(2,1)}, bf16[128,1024]{1,0:T(8,128)(2,1)S(1)}, u32[]{:S(2)}, u32[]{:S(2)}) collective-permute-start(bf16[128,1024]{1,0:T(8,128)(2,1)} %get-tuple-element.57), channel_id=1, source_target_pairs={{0,6},{1,7},{2,4},{3,5},{4,2},{5,3},{6,0},{7,1},{8,14},{9,15},{10,... | collective-permute-start | bytes 786440 | tf_op jit(solution)/shard_map/ppermute | solution.py:508
  11.7 11.4 %all-to-all-start = ((s32[4,8,128]{2,1,0:T(8,128)}), s32[4,8,128]{2,1,0:T(8,128)S(1)}, u32[]{:S(2)}, u32[]{:S(2)}) async-start(s32[4,8,128]{2,1,0:T(8,128)} %get-tuple-element.47), calls=%async_computation | async-start | bytes 32768 | tf_op jit(solution)/shard_map/all_to_all | solution.py:580
  16.5 9.4 %collective-permute-start.1 = (bf16[128,1024]{1,0:T(8,128)(2,1)}, bf16[128,1024]{1,0:T(8,128)(2,1)S(1)}, u32[]{:S(2)}, u32[]{:S(2)}) collective-permute-start(bf16[128,1024]{1,0:T(8,128)(2,1)} %get-tuple-element.54), channel_id=1, source_target_pairs={{0,2},{1,3},{2,0},{3,1},{4,6},{5,7},{6,4},{7,5},{8,10},{9,11},{10,... | collective-permute-start | bytes 786440 | tf_op jit(solution)/shard_map/ppermute | solution.py:508
  16.7 9.1 %copy-start.3 = (bf16[128,1024]{1,0:T(8,128)(2,1)S(1)}, bf16[128,1024]{1,0:T(8,128)(2,1)}, u32[]{:S(2)}) copy-start(bf16[128,1024]{1,0:T(8,128)(2,1)} %get-tuple-element.53.refs_0_) | copy-start | bytes 786436
  16.7 9.1 %collective-permute-start.2 = (bf16[128,1024]{1,0:T(8,128)(2,1)}, bf16[128,1024]{1,0:T(8,128)(2,1)S(1)}, u32[]{:S(2)}, u32[]{:S(2)}) collective-permute-start(bf16[128,1024]{1,0:T(8,128)(2,1)} %get-tuple-element.55), channel_id=1, source_target_pairs={{0,4},{1,5},{2,6},{3,7},{4,0},{5,1},{6,2},{7,3},{8,12},{9,13},{10,... | collective-permute-start | bytes 786440 | tf_op jit(solution)/shard_map/ppermute | solution.py:508
  23.1 32.6 %copy-start.2 = (bf16[256,1024]{1,0:T(8,128)(2,1)S(1)}, bf16[256,1024]{1,0:T(8,128)(2,1)}, u32[]{:S(2)}) copy-start(bf16[256,1024]{1,0:T(8,128)(2,1)} %get-tuple-element.63.refs_0_.refs_4_.refs_6_) | copy-start | bytes 1572868
  23.1 12.8 %collective-permute-start.4 = (bf16[256,1024]{1,0:T(8,128)(2,1)}, bf16[256,1024]{1,0:T(8,128)(2,1)S(1)}, u32[]{:S(2)}, u32[]{:S(2)}) collective-permute-start(bf16[256,1024]{1,0:T(8,128)(2,1)} %get-tuple-element.60), channel_id=1, source_target_pairs={{0,6},{1,7},{2,4},{3,5},{4,2},{5,3},{6,0},{7,1},{8,14},{9,15},{10,... | collective-permute-start | bytes 1572872 | tf_op jit(solution)/shard_map/ppermute | solution.py:508
  25.3 24.0 %collective-permute-start.8 = (bf16[256,1024]{1,0:T(8,128)(2,1)}, bf16[256,1024]{1,0:T(8,128)(2,1)S(1)}, u32[]{:S(2)}, u32[]{:S(2)}) collective-permute-start(bf16[256,1024]{1,0:T(8,128)(2,1)} %get-tuple-element.65), channel_id=1, source_target_pairs={{0,4},{1,5},{2,6},{3,7},{4,0},{5,1},{6,2},{7,3},{8,12},{9,13},{10,... | collective-permute-start | bytes 1572872 | tf_op jit(solution)/shard_map/ppermute | solution.py:508
  25.6 23.8 %collective-permute-start.7 = (bf16[256,1024]{1,0:T(8,128)(2,1)}, bf16[256,1024]{1,0:T(8,128)(2,1)S(1)}, u32[]{:S(2)}, u32[]{:S(2)}) collective-permute-start(bf16[256,1024]{1,0:T(8,128)(2,1)} %get-tuple-element.64), channel_id=1, source_target_pairs={{0,2},{1,3},{2,0},{3,1},{4,6},{5,7},{6,4},{7,5},{8,10},{9,11},{10,... | collective-permute-start | bytes 1572872 | tf_op jit(solution)/shard_map/ppermute | solution.py:508
  27.5 24.6 %collective-permute-start.9 = (bf16[8,128,128]{2,1,0:T(8,128)(2,1)S(1)}, bf16[8,128,128]{2,1,0:T(8,128)(2,1)S(1)}, u32[]{:S(2)}, u32[]{:S(2)}) collective-permute-start(bf16[8,128,128]{2,1,0:T(8,128)(2,1)S(1)} %get-tuple-element.68), channel_id=1, source_target_pairs={{0,24},{8,0},{16,8},{24,16},{1,25},{9,1},{17,9},{25,17},{2,26},{10... | collective-permute-start | bytes 786440 | tf_op jit(solution)/shard_map/ppermute | solution.py:504
  27.5 43.0 %collective-permute-start.6 = (bf16[8,128,128]{2,1,0:T(8,128)(2,1)S(1)}, bf16[8,128,128]{2,1,0:T(8,128)(2,1)S(1)}, u32[]{:S(2)}, u32[]{:S(2)}) collective-permute-start(bf16[8,128,128]{2,1,0:T(8,128)(2,1)S(1)} %get-tuple-element.62), channel_id=1, source_target_pairs={{0,16},{8,24},{16,0},{24,8},{1,17},{9,25},{17,1},{25,9},{2,18},{10... | collective-permute-start | bytes 786440 | tf_op jit(solution)/shard_map/ppermute | solution.py:504
  36.0 34.6 %collective-permute-start.5 = (bf16[8,128,128]{2,1,0:T(8,128)(2,1)S(1)}, bf16[8,128,128]{2,1,0:T(8,128)(2,1)S(1)}, u32[]{:S(2)}, u32[]{:S(2)}) collective-permute-start(bf16[8,128,128]{2,1,0:T(8,128)(2,1)S(1)} %get-tuple-element.61), channel_id=1, source_target_pairs={{0,8},{8,16},{16,24},{24,0},{1,9},{9,17},{17,25},{25,1},{2,10},{10... | collective-permute-start | bytes 786440 | tf_op jit(solution)/shard_map/ppermute | solution.py:504
  49.4 1.0 copy-start.1
  52.1 18.5 %collective-permute-start.10 = (bf16[8,128,128]{2,1,0:T(8,128)(2,1)S(1)}, bf16[8,128,128]{2,1,0:T(8,128)(2,1)S(1)}, u32[]{:S(2)}, u32[]{:S(2)}) collective-permute-start(bf16[8,128,128]{2,1,0:T(8,128)(2,1)S(1)} %get-tuple-element.70), channel_id=1, source_target_pairs={{0,8},{8,16},{16,24},{24,0},{1,9},{9,17},{17,25},{25,1},{2,10},{10... | collective-permute-start | bytes 786440 | tf_op jit(solution)/shard_map/ppermute | solution.py:504
  53.3 21.9 %collective-permute-start.11 = (bf16[8,128,128]{2,1,0:T(8,128)(2,1)S(1)}, bf16[8,128,128]{2,1,0:T(8,128)(2,1)S(1)}, u32[]{:S(2)}, u32[]{:S(2)}) collective-permute-start(bf16[8,128,128]{2,1,0:T(8,128)(2,1)S(1)} %get-tuple-element.71), channel_id=1, source_target_pairs={{0,16},{8,24},{16,0},{24,8},{1,17},{9,25},{17,1},{25,9},{2,18},{10... | collective-permute-start | bytes 786440 | tf_op jit(solution)/shard_map/ppermute | solution.py:504
  54.3 23.6 %collective-permute-start.12 = (bf16[8,128,128]{2,1,0:T(8,128)(2,1)S(1)}, bf16[8,128,128]{2,1,0:T(8,128)(2,1)S(1)}, u32[]{:S(2)}, u32[]{:S(2)}) collective-permute-start(bf16[8,128,128]{2,1,0:T(8,128)(2,1)S(1)} %get-tuple-element.72), channel_id=1, source_target_pairs={{0,24},{8,0},{16,8},{24,16},{1,25},{9,1},{17,9},{25,17},{2,26},{10... | collective-permute-start | bytes 786440 | tf_op jit(solution)/shard_map/ppermute | solution.py:504
  77.9 23.2 %copy-start = (bf16[1024,1024]{1,0:T(8,128)(2,1)S(1)}, bf16[1024,1024]{1,0:T(8,128)(2,1)}, u32[]{:S(2)}) copy-start(bf16[1024,1024]{1,0:T(8,128)(2,1)} %refs_8_.1) | copy-start | bytes 6291460
  85.1 4.1 %collective-permute-start.13 = (bf16[128,512]{1,0:T(8,128)(2,1)S(1)}, bf16[128,512]{1,0:T(8,128)(2,1)S(1)}, u32[]{:S(2)}, u32[]{:S(2)}) collective-permute-start(bf16[128,512]{1,0:T(8,128)(2,1)S(1)} %get-tuple-element.76), channel_id=1, source_target_pairs={{0,1},{1,0},{2,3},{3,2},{4,5},{5,4},{6,7},{7,6},{8,9},{9,8},{10,11... | collective-permute-start | bytes 393224 | tf_op jit(solution)/shard_map/ppermute | solution.py:508
  85.7 5.1 %collective-permute-start.14 = (bf16[128,512]{1,0:T(8,128)(2,1)S(1)}, bf16[128,512]{1,0:T(8,128)(2,1)S(1)}, u32[]{:S(2)}, u32[]{:S(2)}) collective-permute-start(bf16[128,512]{1,0:T(8,128)(2,1)S(1)} %get-tuple-element.77), channel_id=1, source_target_pairs={{0,2},{1,3},{2,0},{3,1},{4,6},{5,7},{6,4},{7,5},{8,10},{9,11},{10,... | collective-permute-start | bytes 393224 | tf_op jit(solution)/shard_map/ppermute | solution.py:508
  86.9 7.6 %collective-permute-start.15 = (bf16[128,512]{1,0:T(8,128)(2,1)S(1)}, bf16[128,512]{1,0:T(8,128)(2,1)S(1)}, u32[]{:S(2)}, u32[]{:S(2)}) collective-permute-start(bf16[128,512]{1,0:T(8,128)(2,1)S(1)} %get-tuple-element.78), channel_id=1, source_target_pairs={{0,3},{1,2},{2,1},{3,0},{4,7},{5,6},{6,5},{7,4},{8,11},{9,10},{10,... | collective-permute-start | bytes 393224 | tf_op jit(solution)/shard_map/ppermute | solution.py:508
  87.4 7.1 %collective-permute-start.16 = (bf16[128,512]{1,0:T(8,128)(2,1)S(1)}, bf16[128,512]{1,0:T(8,128)(2,1)S(1)}, u32[]{:S(2)}, u32[]{:S(2)}) collective-permute-start(bf16[128,512]{1,0:T(8,128)(2,1)S(1)} %get-tuple-element.79), channel_id=1, source_target_pairs={{0,4},{1,5},{2,6},{3,7},{4,0},{5,1},{6,2},{7,3},{8,12},{9,13},{10,... | collective-permute-start | bytes 393224 | tf_op jit(solution)/shard_map/ppermute | solution.py:508
  88.6 12.4 %collective-permute-start.17 = (bf16[128,512]{1,0:T(8,128)(2,1)S(1)}, bf16[128,512]{1,0:T(8,128)(2,1)S(1)}, u32[]{:S(2)}, u32[]{:S(2)}) collective-permute-start(bf16[128,512]{1,0:T(8,128)(2,1)S(1)} %get-tuple-element.80), channel_id=1, source_target_pairs={{0,5},{1,4},{2,7},{3,6},{4,1},{5,0},{6,3},{7,2},{8,13},{9,12},{10,... | collective-permute-start | bytes 393224 | tf_op jit(solution)/shard_map/ppermute | solution.py:508
  89.2 11.9 %collective-permute-start.18 = (bf16[128,512]{1,0:T(8,128)(2,1)S(1)}, bf16[128,512]{1,0:T(8,128)(2,1)S(1)}, u32[]{:S(2)}, u32[]{:S(2)}) collective-permute-start(bf16[128,512]{1,0:T(8,128)(2,1)S(1)} %get-tuple-element.81), channel_id=1, source_target_pairs={{0,6},{1,7},{2,4},{3,5},{4,2},{5,3},{6,0},{7,1},{8,14},{9,15},{10,... | collective-permute-start | bytes 393224 | tf_op jit(solution)/shard_map/ppermute | solution.py:508
  90.8 10.3 %collective-permute-start.19 = (bf16[128,512]{1,0:T(8,128)(2,1)S(1)}, bf16[128,512]{1,0:T(8,128)(2,1)S(1)}, u32[]{:S(2)}, u32[]{:S(2)}) collective-permute-start(bf16[128,512]{1,0:T(8,128)(2,1)S(1)} %get-tuple-element.82), channel_id=1, source_target_pairs={{0,7},{1,6},{2,5},{3,4},{4,3},{5,2},{6,1},{7,0},{8,15},{9,14},{10,... | collective-permute-start | bytes 393224 | tf_op jit(solution)/shard_map/ppermute | solution.py:508
